TPU v7x, 32 devices: a whole 2x2x4 slice. The times are simulated.
32 devices in a mesh: dp: 16 (over z, y, core), mp: 2 (over x).
Axes of the slice: x: 2, y: 2, z: 4, core: 2. Of those that a mesh axis runs over, the one named last changes fastest.
Arguments:
- image: bfloat16 [1152, 8192], P(None, ('dp', 'mp')), may hold values from -0.29882812 to 0.29882812
- text: bfloat16 [1152, 8192], P(None, ('dp', 'mp')), may hold values from -0.29882812 to 0.29882812
- scale: float32 [1], replicated, may hold values from 5 to 15
- bias: float32 [1], replicated, may hold values from -5 to -3
Outputs:
- grad_image: float32 [1152, 8192], P(None, ('dp', 'mp'))
- row_loss: float32 [8192], P(('dp', 'mp'))
- grad_text: float32 [1152, 8192], P(None, ('dp', 'mp'))
All inputs are finite; a program needn't handle non-finite values.
Results may differ from a plain program's by a relative error of at most 0.0022.
Values may be sent and summed in bfloat16 or wider, within the bound.
No kernel may reach another device: no remote copies, remote signals or barrier semaphores. Data moves between devices by JAX's collectives and lax.ppermute only.
A program may use at most 64 MiB of HBM per device.

v0:
```python
import jax
import jax.numpy as jnp
from jax import lax
from jax.sharding import PartitionSpec as P

WINDOW = 8


def shifted(block, axis, distance):
    devices = range(lax.axis_size(axis))
    route = [((i - distance) % len(devices), i) for i in devices]
    return lax.ppermute(block, axis, route)


def shards(image, text, scale, bias):
    width, rows = image.shape
    temper = scale[0]
    offset = bias[0]
    ident = (jnp.arange(rows)[:, None] == jnp.arange(rows)[None, :]).astype(jnp.float32)
    blank = jnp.zeros_like(ident)
    grad_img = jnp.zeros((width, rows), jnp.float32)
    losses = jnp.zeros((rows,), jnp.float32)
    current = text
    carried = jnp.zeros((width, rows), jnp.float32)
    for step in range(WINDOW):
        positive = ident if step == 0 else blank
        inner = lax.dot_general(
            image, current, (((0,), (0,)), ((), ())), preferred_element_type=jnp.float32
        )
        logits = temper * inner + offset
        grad_logit = (jax.nn.sigmoid(logits) - positive).astype(jnp.bfloat16)
        row_terms = jnp.sum(jax.nn.softplus(logits) - positive * logits, axis=1)
        grad_left = temper * lax.dot_general(
            current, grad_logit, (((1,), (1,)), ((), ())), preferred_element_type=jnp.float32
        )
        grad_right = temper * jnp.dot(image, grad_logit, preferred_element_type=jnp.float32)
        grad_left, row_terms, grad_right = (grad_left, row_terms, grad_right)
        grad_img = grad_img + grad_left
        losses = losses + row_terms
        carried = carried + grad_right
        if step + 1 < WINDOW:
            current, carried = (
                shifted(current.astype(jnp.float32), ("dp", "mp"), 1).astype(current.dtype),
                shifted(carried, ("dp", "mp"), 1),
            )
    grad_txt = shifted(carried, ("dp", "mp"), -(WINDOW - 1))
    return (grad_img, losses / float(rows), grad_txt)


def solution(mesh):
    return jax.shard_map(
        shards,
        mesh=mesh,
        in_specs=(P(None, ("dp", "mp")), P(None, ("dp", "mp")), P(), P()),
        out_specs=(P(None, ("dp", "mp")), P(("dp", "mp")), P(None, ("dp", "mp"))),
        check_vma=False,
    )
```

profile of v0, /device:TPU:0, one launch (start us, length us, event | category | flops | bytes accessed | tf_op | source)
XLA Modules:
  0.0 322.6 jit_solution(8554385018001040352)
XLA Ops:
  2.0 1.6 fusion.28
  4.0 3.0 collective-permute-start.7
  7.0 0.6 collective-permute-start
  7.6 37.3 %collective-permute-done = bf16[1152,256]{1,0:T(8,128)(2,1)S(1)} collective-permute-done((bf16[1152,256]{1,0:T(8,128)(2,1)S(1)}, bf16[1152,256]{1,0:T(8,128)(2,1)S(1)}, u32[]{:S(2)}, u32[]{:S(2)}) %collective-permute-start) | collective-permute-done | bytes 589856 | tf_op jit(solution)/shard_map/ppermute | solution.py:12
  45.8 2.5 collective-permute-start.8
  48.4 36.9 %collective-permute-done.1 = bf16[1152,256]{1,0:T(8,128)(2,1)S(1)} collective-permute-done((bf16[1152,256]{1,0:T(8,128)(2,1)S(1)}, bf16[1152,256]{1,0:T(8,128)(2,1)S(1)}, u32[]{:S(2)}, u32[]{:S(2)}) %collective-permute-start.1) | collective-permute-done | bytes 589856 | tf_op jit(solution)/shard_map/ppermute | solution.py:12
  86.4 2.5 collective-permute-start.9
  89.0 37.6 %collective-permute-done.2 = bf16[1152,256]{1,0:T(8,128)(2,1)S(1)} collective-permute-done((bf16[1152,256]{1,0:T(8,128)(2,1)S(1)}, bf16[1152,256]{1,0:T(8,128)(2,1)S(1)}, u32[]{:S(2)}, u32[]{:S(2)}) %collective-permute-start.2) | collective-permute-done | bytes 589856 | tf_op jit(solution)/shard_map/ppermute | solution.py:12
  126.6 0.5 fusion.34
  127.7 2.5 collective-permute-start.10
  130.3 36.9 %collective-permute-done.3 = bf16[1152,256]{1,0:T(8,128)(2,1)S(1)} collective-permute-done((bf16[1152,256]{1,0:T(8,128)(2,1)S(1)}, bf16[1152,256]{1,0:T(8,128)(2,1)S(1)}, u32[]{:S(2)}, u32[]{:S(2)}) %collective-permute-start.3) | collective-permute-done | bytes 589856 | tf_op jit(solution)/shard_map/ppermute | solution.py:12
  168.2 2.5 collective-permute-start.11
  170.9 37.6 %collective-permute-done.4 = bf16[1152,256]{1,0:T(8,128)(2,1)S(1)} collective-permute-done((bf16[1152,256]{1,0:T(8,128)(2,1)S(1)}, bf16[1152,256]{1,0:T(8,128)(2,1)S(1)}, u32[]{:S(2)}, u32[]{:S(2)}) %collective-permute-start.4) | collective-permute-done | bytes 589856 | tf_op jit(solution)/shard_map/ppermute | solution.py:12
  209.5 2.5 collective-permute-start.12
  212.9 36.1 %collective-permute-done.5 = bf16[1152,256]{1,0:T(8,128)(2,1)S(1)} collective-permute-done((bf16[1152,256]{1,0:T(8,128)(2,1)S(1)}, bf16[1152,256]{1,0:T(8,128)(2,1)S(1)}, u32[]{:S(2)}, u32[]{:S(2)}) %collective-permute-start.5) | collective-permute-done | bytes 589856 | tf_op jit(solution)/shard_map/ppermute | solution.py:12
  249.1 2.5 collective-permute-start.6
  253.9 11.4 %collective-permute-done.6 = bf16[1152,256]{1,0:T(8,128)(2,1)S(1)} collective-permute-done((bf16[1152,256]{1,0:T(8,128)(2,1)S(1)}, bf16[1152,256]{1,0:T(8,128)(2,1)S(1)}, u32[]{:S(2)}, u32[]{:S(2)}) %collective-permute-start.6) | collective-permute-done | bytes 589856 | tf_op jit(solution)/shard_map/ppermute | solution.py:12
  266.2 23.0 %collective-permute-done.13 = f32[1152,256]{0,1:T(8,128)S(1)} collective-permute-done((f32[1152,256]{0,1:T(8,128)S(1)}, f32[1152,256]{0,1:T(8,128)S(1)}, u32[]{:S(2)}, u32[]{:S(2)}) %collective-permute-start.13) | collective-permute-done | bytes 1179680 | tf_op jit(solution)/shard_map/ppermute | solution.py:12
  289.3 5.6 %collective-permute-start.14 = (f32[1152,256]{0,1:T(8,128)S(1)}, f32[1152,256]{0,1:T(8,128)}, u32[]{:S(2)}, u32[]{:S(2)}) collective-permute-start(f32[1152,256]{0,1:T(8,128)S(1)} %add.197), channel_id=1, source_target_pairs={{7,0},{8,1},{9,2},{10,3},{11,4},{12,5},{13,6},{14,7},{15,8},{16,9}... | collective-permute-start | bytes 3538952 | tf_op jit(solution)/shard_map/ppermute | solution.py:12
  295.7 0.6 fusion.15
  296.4 1.4 copy.7
  297.7 0.6 add_multiply_fusion
  298.3 21.6 %collective-permute-done.14 = f32[1152,256]{0,1:T(8,128)} collective-permute-done((f32[1152,256]{0,1:T(8,128)S(1)}, f32[1152,256]{0,1:T(8,128)}, u32[]{:S(2)}, u32[]{:S(2)}) %collective-permute-start.14) | collective-permute-done | bytes 1179680 | tf_op jit(solution)/shard_map/ppermute | solution.py:12
  319.9 2.7 copy.8
  (43 shorter events, 10.2 us)
Async XLA Ops:
  0.6 1.4 copy-start
  3.6 3.4 %copy-start.1 = (bf16[1152,256]{1,0:T(8,128)(2,1)S(1)}, bf16[1152,256]{1,0:T(8,128)(2,1)}, u32[]{:S(2)}) copy-start(bf16[1152,256]{1,0:T(8,128)(2,1)} %param.5) | copy-start | bytes 1769476
  4.0 41.4 %collective-permute-start.7 = (f32[1152,256]{0,1:T(8,128)S(1)}, f32[1152,256]{0,1:T(8,128)S(1)}, u32[]{:S(2)}, u32[]{:S(2)}) collective-permute-start(f32[1152,256]{0,1:T(8,128)S(1)} %fusion.6), channel_id=1, source_target_pairs={{31,0},{0,1},{1,2},{2,3},{3,4},{4,5},{5,6},{6,7},{7,8},{8,9},{9,10... | collective-permute-start | bytes 3538952 | tf_op jit(solution)/shard_map/ppermute | solution.py:12
  7.0 37.9 %collective-permute-start = (bf16[1152,256]{1,0:T(8,128)(2,1)S(1)}, bf16[1152,256]{1,0:T(8,128)(2,1)S(1)}, u32[]{:S(2)}, u32[]{:S(2)}) collective-permute-start(bf16[1152,256]{1,0:T(8,128)(2,1)S(1)} %copy-done.1), channel_id=1, source_target_pairs={{31,0},{0,1},{1,2},{2,3},{3,4},{4,5},{5,6},{6,7},{7,8},{8,9},{9,10... | collective-permute-start | bytes 1769480 | tf_op jit(solution)/shard_map/ppermute | solution.py:12
  45.8 40.5 %collective-permute-start.8 = (f32[1152,256]{0,1:T(8,128)S(1)}, f32[1152,256]{0,1:T(8,128)S(1)}, u32[]{:S(2)}, u32[]{:S(2)}) collective-permute-start(f32[1152,256]{0,1:T(8,128)S(1)} %fusion.8), channel_id=1, source_target_pairs={{31,0},{0,1},{1,2},{2,3},{3,4},{4,5},{5,6},{6,7},{7,8},{8,9},{9,10... | collective-permute-start | bytes 3538952 | tf_op jit(solution)/shard_map/ppermute | solution.py:12
  48.3 37.0 %collective-permute-start.1 = (bf16[1152,256]{1,0:T(8,128)(2,1)S(1)}, bf16[1152,256]{1,0:T(8,128)(2,1)S(1)}, u32[]{:S(2)}, u32[]{:S(2)}) collective-permute-start(bf16[1152,256]{1,0:T(8,128)(2,1)S(1)} %collective-permute-done), channel_id=1, source_target_pairs={{31,0},{0,1},{1,2},{2,3},{3,4},{4,5},{5,6},{6,7},{7,8},{8,9},{9,10... | collective-permute-start | bytes 1769480 | tf_op jit(solution)/shard_map/ppermute | solution.py:12
  86.4 41.1 %collective-permute-start.9 = (f32[1152,256]{0,1:T(8,128)S(1)}, f32[1152,256]{0,1:T(8,128)S(1)}, u32[]{:S(2)}, u32[]{:S(2)}) collective-permute-start(f32[1152,256]{0,1:T(8,128)S(1)} %add.192), channel_id=1, source_target_pairs={{31,0},{0,1},{1,2},{2,3},{3,4},{4,5},{5,6},{6,7},{7,8},{8,9},{9,10... | collective-permute-start | bytes 3538952 | tf_op jit(solution)/shard_map/ppermute | solution.py:12
  88.9 37.7 %collective-permute-start.2 = (bf16[1152,256]{1,0:T(8,128)(2,1)S(1)}, bf16[1152,256]{1,0:T(8,128)(2,1)S(1)}, u32[]{:S(2)}, u32[]{:S(2)}) collective-permute-start(bf16[1152,256]{1,0:T(8,128)(2,1)S(1)} %collective-permute-done.1), channel_id=1, source_target_pairs={{31,0},{0,1},{1,2},{2,3},{3,4},{4,5},{5,6},{6,7},{7,8},{8,9},{9,10... | collective-permute-start | bytes 1769480 | tf_op jit(solution)/shard_map/ppermute | solution.py:12
  127.7 40.5 %collective-permute-start.10 = (f32[1152,256]{0,1:T(8,128)S(1)}, f32[1152,256]{0,1:T(8,128)S(1)}, u32[]{:S(2)}, u32[]{:S(2)}) collective-permute-start(f32[1152,256]{0,1:T(8,128)S(1)} %add.193), channel_id=1, source_target_pairs={{31,0},{0,1},{1,2},{2,3},{3,4},{4,5},{5,6},{6,7},{7,8},{8,9},{9,10... | collective-permute-start | bytes 3538952 | tf_op jit(solution)/shard_map/ppermute | solution.py:12
  130.2 37.0 %collective-permute-start.3 = (bf16[1152,256]{1,0:T(8,128)(2,1)S(1)}, bf16[1152,256]{1,0:T(8,128)(2,1)S(1)}, u32[]{:S(2)}, u32[]{:S(2)}) collective-permute-start(bf16[1152,256]{1,0:T(8,128)(2,1)S(1)} %collective-permute-done.2), channel_id=1, source_target_pairs={{31,0},{0,1},{1,2},{2,3},{3,4},{4,5},{5,6},{6,7},{7,8},{8,9},{9,10... | collective-permute-start | bytes 1769480 | tf_op jit(solution)/shard_map/ppermute | solution.py:12
  168.2 41.1 %collective-permute-start.11 = (f32[1152,256]{0,1:T(8,128)S(1)}, f32[1152,256]{0,1:T(8,128)S(1)}, u32[]{:S(2)}, u32[]{:S(2)}) collective-permute-start(f32[1152,256]{0,1:T(8,128)S(1)} %add.194), channel_id=1, source_target_pairs={{31,0},{0,1},{1,2},{2,3},{3,4},{4,5},{5,6},{6,7},{7,8},{8,9},{9,10... | collective-permute-start | bytes 3538952 | tf_op jit(solution)/shard_map/ppermute | solution.py:12
  170.8 37.7 %collective-permute-start.4 = (bf16[1152,256]{1,0:T(8,128)(2,1)S(1)}, bf16[1152,256]{1,0:T(8,128)(2,1)S(1)}, u32[]{:S(2)}, u32[]{:S(2)}) collective-permute-start(bf16[1152,256]{1,0:T(8,128)(2,1)S(1)} %collective-permute-done.3), channel_id=1, source_target_pairs={{31,0},{0,1},{1,2},{2,3},{3,4},{4,5},{5,6},{6,7},{7,8},{8,9},{9,10... | collective-permute-start | bytes 1769480 | tf_op jit(solution)/shard_map/ppermute | solution.py:12
  209.5 42.9 %collective-permute-start.12 = (f32[1152,256]{0,1:T(8,128)S(1)}, f32[1152,256]{0,1:T(8,128)S(1)}, u32[]{:S(2)}, u32[]{:S(2)}) collective-permute-start(f32[1152,256]{0,1:T(8,128)S(1)} %add.195), channel_id=1, source_target_pairs={{31,0},{0,1},{1,2},{2,3},{3,4},{4,5},{5,6},{6,7},{7,8},{8,9},{9,10... | collective-permute-start | bytes 3538952 | tf_op jit(solution)/shard_map/ppermute | solution.py:12
  212.1 37.0 %collective-permute-start.5 = (bf16[1152,256]{1,0:T(8,128)(2,1)S(1)}, bf16[1152,256]{1,0:T(8,128)(2,1)S(1)}, u32[]{:S(2)}, u32[]{:S(2)}) collective-permute-start(bf16[1152,256]{1,0:T(8,128)(2,1)S(1)} %collective-permute-done.4), channel_id=1, source_target_pairs={{31,0},{0,1},{1,2},{2,3},{3,4},{4,5},{5,6},{6,7},{7,8},{8,9},{9,10... | collective-permute-start | bytes 1769480 | tf_op jit(solution)/shard_map/ppermute | solution.py:12
  249.1 16.2 %collective-permute-start.6 = (bf16[1152,256]{1,0:T(8,128)(2,1)S(1)}, bf16[1152,256]{1,0:T(8,128)(2,1)S(1)}, u32[]{:S(2)}, u32[]{:S(2)}) collective-permute-start(bf16[1152,256]{1,0:T(8,128)(2,1)S(1)} %collective-permute-done.5), channel_id=1, source_target_pairs={{31,0},{0,1},{1,2},{2,3},{3,4},{4,5},{5,6},{6,7},{7,8},{8,9},{9,10... | collective-permute-start | bytes 1769480 | tf_op jit(solution)/shard_map/ppermute | solution.py:12
  252.6 36.6 %collective-permute-start.13 = (f32[1152,256]{0,1:T(8,128)S(1)}, f32[1152,256]{0,1:T(8,128)S(1)}, u32[]{:S(2)}, u32[]{:S(2)}) collective-permute-start(f32[1152,256]{0,1:T(8,128)S(1)} %add.196), channel_id=1, source_target_pairs={{31,0},{0,1},{1,2},{2,3},{3,4},{4,5},{5,6},{6,7},{7,8},{8,9},{9,10... | collective-permute-start | bytes 3538952 | tf_op jit(solution)/shard_map/ppermute | solution.py:12
  289.3 30.6 %collective-permute-start.14 = (f32[1152,256]{0,1:T(8,128)S(1)}, f32[1152,256]{0,1:T(8,128)}, u32[]{:S(2)}, u32[]{:S(2)}) collective-permute-start(f32[1152,256]{0,1:T(8,128)S(1)} %add.197), channel_id=1, source_target_pairs={{7,0},{8,1},{9,2},{10,3},{11,4},{12,5},{13,6},{14,7},{15,8},{16,9}... | collective-permute-start | bytes 3538952 | tf_op jit(solution)/shard_map/ppermute | solution.py:12
where the time goes:
time: 323 us
  waiting for transfers between devices  278 us (86%)
  starting transfers between devices  24.8 us (8%)
  matrix products  11.7 us (4%)
  local copies, waits for them, and re-layouts  4.05 us (1%)
    ppermute x15, waiting for transfers between devices, shifted(): return lax.ppermute(block, axis, route)  278 us
    ppermute x15, starting transfers between devices, shifted(): return lax.ppermute(block, axis, route)  24.8 us
  transfers between devices with their start and end apart: 15, of which 9 were waited for; matrix products, arithmetic and copies ran while one was open for 4% of the time, Pallas kernels for 0%

commit v1 on v0

v1 whole, which is shorter than its diff:
```python
import functools

import jax
import jax.numpy as jnp
from jax import lax
from jax.experimental import pallas as pl
from jax.experimental.pallas import tpu as pltpu
from jax.sharding import PartitionSpec as P

AXES = ("dp", "mp")
WINDOW = 8
PAIR, CORE, SIDE = 1, 2, 4
MASKS = (0, CORE, PAIR, CORE | PAIR)
EXTRA = 16
VMEM_BYTES = 40 * 1024 * 1024

NN = (((1,), (0,)), ((), ()))
NT = (((1,), (1,)), ((), ()))


def dot(a, b, dims):
    return lax.dot_general(a, b, dims, preferred_element_type=jnp.float32)


def moved(block, target):
    n = lax.axis_size(AXES)
    route = [(i, target(i, n)) for i in range(n) if target(i, n) is not None]
    return lax.ppermute(block, AXES, route)


def forward(i, n):
    return (i + WINDOW) % n


def back(i, n):
    return (i - WINDOW) % n


def swap(mask):
    return lambda i, n: i ^ mask


def to_high(i, n):
    return None if i & SIDE else i | SIDE


def to_low(i, n):
    return i ^ SIDE if i & SIDE else None


def terms(inner, temper, offset):
    z = temper * inner + offset
    e = jnp.exp(-jnp.abs(z))
    r = 1.0 / (1.0 + e)
    return z, jnp.where(z >= 0, r, e * r), jnp.maximum(z, 0.0) + jnp.log1p(e)


def partner_kernel(start, tb, i0, i1, i2, i3, whole, part, grad_x, grad, loss, kept):
    temper, offset = tb[0], tb[1]
    cols = part.shape[1]
    text = whole[:, start : start + cols] + part[...]
    kept[...] = text
    turned = text.T
    images = (i0, i1, i2, i3)
    for r, image in enumerate(images):
        _, s, soft = terms(dot(turned, image[...], NN), temper, offset)
        grad[r] = s.astype(jnp.bfloat16)
        loss[r : r + 1] = jnp.sum(soft, axis=0, keepdims=True)
    tile = 384
    for d in range(0, text.shape[0], tile):
        total = dot(i0[d : d + tile], grad[0], NT)
        for r in (1, 2, 3):
            total = total + dot(images[r][d : d + tile], grad[r], NT)
        grad_x[d : d + tile] = (temper * total).astype(jnp.bfloat16)


def own_kernel(tb, later, i0, i1, i2, i3, text, m1, m2, grad_t, grad_m1, grad_m2, grad, loss, kept, turned, masked):
    temper, offset = tb[0], tb[1]
    rows = text.shape[1]
    half = rows // 2
    kept[0] = text[...]
    kept[1, :, :half] = m1[...]
    kept[1, :, half:] = m2[...]
    turned[0] = text[...].T
    turned[1, :half] = m1[...].T
    turned[1, half:] = m2[...].T
    images = (i0, i1, i2, i3)
    for r, image in enumerate(images):
        same = later[r]
        z, s, soft = terms(dot(turned[1 - same], image[...], NN), temper, offset)
        if r == 0:
            diag = lax.broadcasted_iota(jnp.int32, z.shape, 0) == lax.broadcasted_iota(jnp.int32, z.shape, 1)
            s = jnp.where(diag, s - 1.0, s)
            soft = jnp.where(diag, soft - z, soft)
        g = s.astype(jnp.bfloat16)
        grad[r] = g
        loss[r : r + 1] = jnp.sum(soft, axis=0, keepdims=True)
        masked[0, r] = jnp.where(same == 1, g, jnp.zeros_like(g))
        masked[1, r] = jnp.where(same == 1, jnp.zeros_like(g), g)
    tile = 384
    for d in range(0, text.shape[0], tile):
        total = dot(i0[d : d + tile], masked[0, 0], NT)
        for r in (1, 2, 3):
            total = total + dot(images[r][d : d + tile], masked[0, r], NT)
        grad_t[d : d + tile] = temper * total
        total = dot(i1[d : d + tile], masked[1, 1], NT)
        for r in (2, 3):
            total = total + dot(images[r][d : d + tile], masked[1, r], NT)
        total = temper * total
        grad_m1[d : d + tile] = total[:, :half]
        grad_m2[d : d + tile] = total[:, half:]


def row_total(r, tb, later, kept, k1, k2, g, g1, g2, d, tile):
    same = later[r]
    total = dot(kept[1 - same, d : d + tile], g[r], NN)
    total = total + dot(k1[d : d + tile], g1[r], NN)
    total = total + dot(k2[d : d + tile], g2[r], NN)
    return tb[0] * total


def split_loss(r, l0, l1, l2, shape):
    value = l0[r : r + 1] + l1[r : r + 1] + l2[r : r + 1]
    high = value.astype(jnp.bfloat16).astype(jnp.float32)
    place = lax.broadcasted_iota(jnp.int32, shape, 0)
    value, high = jnp.broadcast_to(value, shape), jnp.broadcast_to(high, shape)
    return jnp.where(place == 0, high, jnp.where(place == 1, value - high, 0.0))


def away_kernel(tb, later, kept, k1, k2, g, g1, g2, l0, l1, l2, out):
    width = k1.shape[0]
    tile = 384
    for slot, r in enumerate((1, 3)):
        for d in range(0, width, tile):
            out[slot, d : d + tile] = row_total(r, tb, later, kept, k1, k2, g, g1, g2, d, tile).astype(jnp.bfloat16)
        out[slot, width:] = split_loss(r, l0, l1, l2, out[slot, width:].shape).astype(jnp.bfloat16)


def home_kernel(tb, later, kept, k1, k2, g, g1, g2, l0, l1, l2, out, loss):
    width = k1.shape[0]
    tile = 384
    for slot, r in enumerate((0, 2)):
        for d in range(0, width, tile):
            out[slot, d : d + tile] = row_total(r, tb, later, kept, k1, k2, g, g1, g2, d, tile)
        loss[slot : slot + 1] = l0[r : r + 1] + l1[r : r + 1] + l2[r : r + 1]


def joined_kernel(home, loss, came, out):
    width = home.shape[1]
    out[:width] = (home[1] + came[1, :width].astype(jnp.float32)).astype(jnp.bfloat16)
    shape = (EXTRA, home.shape[2])
    tail = came[1, width:].astype(jnp.float32)
    value = loss[1:2] + tail[0:1] + tail[1:2]
    high = value.astype(jnp.bfloat16).astype(jnp.float32)
    place = lax.broadcasted_iota(jnp.int32, shape, 0)
    value, high = jnp.broadcast_to(value, shape), jnp.broadcast_to(high, shape)
    out[width:] = jnp.where(place == 0, high, jnp.where(place == 1, value - high, 0.0)).astype(jnp.bfloat16)


def call(kernel, out_shape, args, scratch=(), flops=0):
    spaces = [pltpu.SMEM if a.ndim == 1 else pltpu.VMEM for a in args]
    return pl.pallas_call(
        kernel,
        out_shape=out_shape,
        in_specs=[pl.BlockSpec(memory_space=s) for s in spaces],
        out_specs=jax.tree.map(lambda _: pl.BlockSpec(memory_space=pltpu.VMEM), out_shape),
        scratch_shapes=list(scratch),
        compiler_params=pltpu.CompilerParams(vmem_limit_bytes=VMEM_BYTES),
        cost_estimate=pl.CostEstimate(flops=flops, bytes_accessed=sum(a.size * a.dtype.itemsize for a in args), transcendentals=0),
    )(*args)


def shards(image, text, scale, bias):
    width, rows = image.shape
    half = rows // 2
    f32, bf16 = jnp.float32, jnp.bfloat16
    sds = jax.ShapeDtypeStruct
    place = lax.axis_index(AXES) % WINDOW
    tb = jnp.concatenate([scale, bias])
    later = jnp.stack([((place ^ m) >= place).astype(jnp.int32) for m in MASKS])
    unit = 2 * rows * rows * width

    m1 = moved(text[:, :half], forward)
    m2 = moved(text[:, half:], forward)
    low = moved(text, to_high)
    image_c = moved(image, swap(CORE))
    image_p = moved(image, swap(PAIR))
    x1 = moved(m1, to_low)
    x2 = moved(m2, to_low)
    image_pc = moved(image_p, swap(CORE))
    images = (image, image_c, image_p, image_pc)

    def partner(start, part):
        return call(
            functools.partial(partner_kernel, start),
            (sds((width, half), bf16), sds((4, half, rows), bf16), sds((8, rows), f32), sds((width, half), bf16)),
            (tb, *images, low, part),
            flops=4 * unit,
        )

    grad_x1, g1, l1, k1 = partner(0, x1)
    grad_t, grad_m1, grad_m2, g0, l0, kept = call(
        own_kernel,
        (
            sds((width, rows), f32),
            sds((width, half), f32),
            sds((width, half), f32),
            sds((4, rows, rows), bf16),
            sds((8, rows), f32),
            sds((2, width, rows), bf16),
        ),
        (tb, later, *images, text, m1, m2),
        scratch=(pltpu.VMEM((2, rows, width), bf16), pltpu.VMEM((2, 4, rows, rows), bf16)),
        flops=11 * unit,
    )
    grad_x2, g2, l2, k2 = partner(half, x2)

    up1 = moved(grad_x1, to_high)
    up2 = moved(grad_x2, to_high)
    down1 = moved(grad_x1, to_low)
    down2 = moved(grad_x2, to_low)
    past1 = moved((grad_m1 + up1).astype(bf16), back)
    past2 = moved((grad_m2 + up2).astype(bf16), back)

    rest = (tb, later, kept, k1, k2, g0, g1, g2, l0, l1, l2)
    away = call(away_kernel, sds((2, width + EXTRA, rows), bf16), rest, flops=4 * unit)
    came = moved(away, swap(CORE))
    home, home_loss = call(home_kernel, (sds((2, width, rows), f32), sds((8, rows), f32)), rest, flops=4 * unit)
    joined = call(joined_kernel, sds((width + EXTRA, rows), bf16), (home, home_loss, came))
    other = moved(joined, swap(PAIR))

    grad_image = home[0] + came[0, :width].astype(f32) + other[:width].astype(f32)
    losses = home_loss[0] + jnp.sum(came[0, width : width + 2].astype(f32), axis=0) + jnp.sum(other[width : width + 2].astype(f32), axis=0)
    downs = jnp.concatenate([down1.astype(f32) + past1.astype(f32), down2.astype(f32) + past2.astype(f32)], axis=1)
    return grad_image, losses / float(rows), grad_t + downs


def solution(mesh):
    spread = P(None, AXES)
    return jax.shard_map(
        shards,
        mesh=mesh,
        in_specs=(spread, spread, P(), P()),
        out_specs=(spread, P(AXES), spread),
        check_vma=False,
    )
```

time: 323 us -> 89.7 us (0.28)
  waiting for transfers between devices: 278 us -> 41.6 us
  Pallas kernels: 0 us -> 12.1 us
  matrix products: 11.7 us -> 0 us
  starting transfers between devices: 24.8 us -> 28.8 us
    ppermute x15 -> x16, waiting for transfers between devices: 278 us -> 41.6 us  [moved(): return lax.ppermute(block, AXES, route)]
    pallas_call x0 -> x6, Pallas kernels: none -> 12.1 us  [call(): pl.pallas_call(kernel, out_shape=out_shape, in_specs=[pl.BlockSpec(memory...]
    dot_general x24 -> x0, matrix products: 11.7 us -> none  [the longest x8 5.27 us: shards(): lax.dot_general(image, current, (((0,), (0,)), ((), ())), preferred_eleme...]
    unnamed x6 -> x4, local copies, waits for them, and re-layouts: 4.05 us -> 0.01 us
    ppermute x15 -> x16, starting transfers between devices: 24.8 us -> 28.8 us  [moved(): return lax.ppermute(block, AXES, route)]
  transfers between devices with their start and end apart: 15 -> 16, of which waited for: 9 -> 5; matrix products, arithmetic and copies ran while one was open for 4% -> 3% of each run, Pallas kernels for 0% -> 13%
where the time goes in v1:
time: 89.7 us; the launch traced here: 89.3 us
  waiting for transfers between devices  41.6 us (46%)
  starting transfers between devices  28.8 us (32%)
  Pallas kernels  12.1 us (13%)
  other arithmetic  3.43 us (4%)
  between operations  2.15 us (2%)
  local copies, waits for them, and re-layouts  1.1 us (1%)
    ppermute x16, waiting for transfers between devices, moved(): return lax.ppermute(block, AXES, route)  41.6 us
    ppermute x16, starting transfers between devices, moved(): return lax.ppermute(block, AXES, route)  28.8 us
    pallas_call x6, Pallas kernels, call(): pl.pallas_call(kernel, out_shape=out_shape, in_specs=[pl.BlockSpec(memory...  12.1 us
  transfers between devices with their start and end apart: 16, of which 5 were waited for; matrix products, arithmetic and copies ran while one was open for 3% of the time, Pallas kernels for 13%

profile of v1, /device:TPU:0, one launch (start us, length us, event | category | flops | bytes accessed | tf_op | source)
XLA Modules:
  0.0 89.3 jit_solution(56462483944335572)
XLA Ops:
  0.6 3.0 %collective-permute-start.1 = (bf16[1152,256]{1,0:T(8,128)(2,1)}, bf16[1152,256]{1,0:T(8,128)(2,1)S(1)}, u32[]{:S(2)}, u32[]{:S(2)}) collective-permute-start(bf16[1152,256]{1,0:T(8,128)(2,1)} %i0.5), channel_id=1, source_target_pairs={{0,1},{1,0},{2,3},{3,2},{4,5},{5,4},{6,7},{7,6},{8,9},{9,8},{10,11... | collective-permute-start | bytes 1769480 | tf_op jit(solution)/shard_map/ppermute | solution.py:28
  4.7 1.6 %collective-permute-start.3 = (bf16[1152,128]{1,0:T(8,128)(2,1)S(1)}, bf16[1152,128]{1,0:T(8,128)(2,1)}, u32[]{:S(2)}, u32[]{:S(2)}) collective-permute-start(bf16[1152,128]{1,0:T(8,128)(2,1)S(1)} %get-tuple-element.36), channel_id=1, source_target_pairs={{0,8},{1,9},{2,10},{3,11},{4,12},{5,13},{6,14},{7,15},{8,16},{9,17... | collective-permute-start | bytes 884744 | tf_op jit(solution)/shard_map/ppermute | solution.py:28
  6.4 3.5 %collective-permute-start.5 = (bf16[1152,256]{1,0:T(8,128)(2,1)S(1)}, bf16[1152,256]{1,0:T(8,128)(2,1)S(1)}, u32[]{:S(2)}, u32[]{:S(2)}) collective-permute-start(bf16[1152,256]{1,0:T(8,128)(2,1)S(1)} %copy-done.1), channel_id=1, source_target_pairs={{0,4},{1,5},{2,6},{3,7},{8,12},{9,13},{10,14},{11,15},{16,20},{17,... | collective-permute-start | bytes 1769480 | tf_op jit(solution)/shard_map/ppermute | solution.py:28
  9.9 7.3 %collective-permute-done.1.i2 = bf16[1152,256]{1,0:T(8,128)(2,1)S(1)} collective-permute-done((bf16[1152,256]{1,0:T(8,128)(2,1)}, bf16[1152,256]{1,0:T(8,128)(2,1)S(1)}, u32[]{:S(2)}, u32[]{:S(2)}) %collective-permute-start.1) | collective-permute-done | bytes 589856 | tf_op jit(solution)/shard_map/ppermute | solution.py:28
  17.2 1.8 %collective-permute-start.4 = (bf16[1152,128]{1,0:T(8,128)(2,1)S(1)}, bf16[1152,128]{1,0:T(8,128)(2,1)}, u32[]{:S(2)}, u32[]{:S(2)}) collective-permute-start(bf16[1152,128]{1,0:T(8,128)(2,1)S(1)} %get-tuple-element.35), channel_id=1, source_target_pairs={{0,8},{1,9},{2,10},{3,11},{4,12},{5,13},{6,14},{7,15},{8,16},{9,17... | collective-permute-start | bytes 884744 | tf_op jit(solution)/shard_map/ppermute | solution.py:28
  19.0 1.3 %collective-permute-start.6 = (bf16[1152,128]{1,0:T(8,128)(2,1)}, bf16[1152,128]{1,0:T(8,128)(2,1)}, u32[]{:S(2)}, u32[]{:S(2)}) collective-permute-start(bf16[1152,128]{1,0:T(8,128)(2,1)} %collective-permute-done.3.m1), channel_id=1, source_target_pairs={{4,0},{5,1},{6,2},{7,3},{12,8},{13,9},{14,10},{15,11},{20,16},{21,... | collective-permute-start | bytes 884744 | tf_op jit(solution)/shard_map/ppermute | solution.py:28
  20.3 8.5 %collective-permute-done.4.m2 = bf16[1152,128]{1,0:T(8,128)(2,1)} collective-permute-done((bf16[1152,128]{1,0:T(8,128)(2,1)S(1)}, bf16[1152,128]{1,0:T(8,128)(2,1)}, u32[]{:S(2)}, u32[]{:S(2)}) %collective-permute-start.4) | collective-permute-done | bytes 294944 | tf_op jit(solution)/shard_map/ppermute | solution.py:28
  28.8 1.3 %collective-permute-start.7 = (bf16[1152,128]{1,0:T(8,128)(2,1)}, bf16[1152,128]{1,0:T(8,128)(2,1)}, u32[]{:S(2)}, u32[]{:S(2)}) collective-permute-start(bf16[1152,128]{1,0:T(8,128)(2,1)} %collective-permute-done.4.m2), channel_id=1, source_target_pairs={{4,0},{5,1},{6,2},{7,3},{12,8},{13,9},{14,10},{15,11},{20,16},{21,... | collective-permute-start | bytes 884744 | tf_op jit(solution)/shard_map/ppermute | solution.py:28
  31.6 2.5 %shard_map.68 = (bf16[1152,128]{1,0:T(8,128)(2,1)S(1)}, bf16[4,128,256]{2,1,0:T(8,128)(2,1)S(1)}, f32[8,256]{1,0:T(8,128)S(1)}, bf16[1152,128]{1,0:T(8,128)(2,1)S(1)}) custom-call(f32[2]{0:T(128)S(1)} %pad_maximum_fusion.tb, bf16[1152,256]{1,0:T(8,128)(2,1)S(1)} %copy-done, bf16[1152,256]{1,0:T(8,128)(2,1)S(1)} %collective-permute-done.i1, ...), custom_call_target="tpu_custom_call" | custom-call | flops 603979776 | bytes 3244040 | tf_op jit(solution)/shard_map/pallas_call | solution.py:162
  34.1 5.3 %collective-permute-start.11 = (bf16[1152,128]{1,0:T(8,128)(2,1)S(1)}, bf16[1152,128]{1,0:T(8,128)(2,1)S(1)}, u32[]{:S(2)}, u32[]{:S(2)}) collective-permute-start(bf16[1152,128]{1,0:T(8,128)(2,1)S(1)} %get-tuple-element.31), channel_id=1, source_target_pairs={{0,4},{1,5},{2,6},{3,7},{8,12},{9,13},{10,14},{11,15},{16,20},{17,... | collective-permute-start | bytes 884744 | tf_op jit(solution)/shard_map/ppermute | solution.py:28
  39.4 1.3 %collective-permute-start.10 = (bf16[1152,128]{1,0:T(8,128)(2,1)S(1)}, bf16[1152,128]{1,0:T(8,128)(2,1)S(1)}, u32[]{:S(2)}, u32[]{:S(2)}) collective-permute-start(bf16[1152,128]{1,0:T(8,128)(2,1)S(1)} %get-tuple-element.31), channel_id=1, source_target_pairs={{4,0},{5,1},{6,2},{7,3},{12,8},{13,9},{14,10},{15,11},{20,16},{21,... | collective-permute-start | bytes 884744 | tf_op jit(solution)/shard_map/ppermute | solution.py:28
  40.7 2.5 %shard_map.69 = (bf16[1152,128]{1,0:T(8,128)(2,1)S(1)}, bf16[4,128,256]{2,1,0:T(8,128)(2,1)S(1)}, f32[8,256]{1,0:T(8,128)S(1)}, bf16[1152,128]{1,0:T(8,128)(2,1)S(1)}) custom-call(f32[2]{0:T(128)S(1)} %pad_maximum_fusion.tb, bf16[1152,256]{1,0:T(8,128)(2,1)S(1)} %copy-done, bf16[1152,256]{1,0:T(8,128)(2,1)S(1)} %collective-permute-done.i1, ...), custom_call_target="tpu_custom_call" | custom-call | flops 603979776 | bytes 3244040 | tf_op jit(solution)/shard_map/pallas_call | solution.py:162
  43.2 4.6 %collective-permute-start.14 = (bf16[1152,128]{1,0:T(8,128)(2,1)S(1)}, bf16[1152,128]{1,0:T(8,128)(2,1)S(1)}, u32[]{:S(2)}, u32[]{:S(2)}) collective-permute-start(bf16[1152,128]{1,0:T(8,128)(2,1)S(1)} %get-tuple-element.33), channel_id=1, source_target_pairs={{0,4},{1,5},{2,6},{3,7},{8,12},{9,13},{10,14},{11,15},{16,20},{17,... | collective-permute-start | bytes 884744 | tf_op jit(solution)/shard_map/ppermute | solution.py:28
  47.8 1.3 %collective-permute-start.13 = (bf16[1152,128]{1,0:T(8,128)(2,1)S(1)}, bf16[1152,128]{1,0:T(8,128)(2,1)S(1)}, u32[]{:S(2)}, u32[]{:S(2)}) collective-permute-start(bf16[1152,128]{1,0:T(8,128)(2,1)S(1)} %get-tuple-element.33), channel_id=1, source_target_pairs={{4,0},{5,1},{6,2},{7,3},{12,8},{13,9},{14,10},{15,11},{20,16},{21,... | collective-permute-start | bytes 884744 | tf_op jit(solution)/shard_map/ppermute | solution.py:28
  49.1 3.8 %shard_map.67 = (f32[1152,256]{1,0:T(8,128)S(1)}, f32[1152,128]{1,0:T(8,128)S(1)}, f32[1152,128]{1,0:T(8,128)S(1)}, bf16[4,256,256]{2,1,0:T(8,128)(2,1)S(1)}, f3...) custom-call(f32[2]{0:T(128)S(1)} %pad_maximum_fusion.tb, s32[4]{0:T(128)S(1)} %add_convert_fusion.2.later, ...), custom_call_target="tpu_custom_call" | custom-call | flops 1660944384 | bytes 3538968 | tf_op jit(solution)/shard_map/pallas_call | solution.py:162
  52.9 1.6 %shard_map.71 = bf16[2,1168,256]{2,1,0:T(8,128)(2,1)S(1)} custom-call(f32[2]{0:T(128)S(1)} %pad_maximum_fusion.tb, s32[4]{0:T(128)S(1)} %add_convert_fusion.2.later, bf16[2,1152,256]{2,1,0:T(8,128)(2,1)S(1)} %get-tuple-element.19.kept, bf16[1152,128]{1,0:T(8,128)(2,1)S(1)} %get-tuple-element.20.k1, bf16[1152,128]{1,0:T(8,128)(2,1)S(1)} %get-tuple-element.21.k2, ...), custom_call_target="tpu_custom_call" | custom-call | flops 603979776 | bytes 2842648 | tf_op jit(solution)/shard_map/pallas_call | solution.py:162
  54.6 1.6 %shard_map.70 = (f32[2,1152,256]{2,1,0:T(8,128)S(1)}, f32[8,256]{1,0:T(8,128)S(1)}) custom-call(f32[2]{0:T(128)S(1)} %pad_maximum_fusion.tb, s32[4]{0:T(128)S(1)} %add_convert_fusion.2.later, bf16[2,1152,256]{2,1,0:T(8,128)(2,1)S(1)} %get-tuple-element.19.kept, bf16[1152,128]{1,0:T(8,128)(2,1)S(1)} %get-tuple-element.20.k1, ...), custom_call_target="tpu_custom_call" | custom-call | flops 603979776 | bytes 2842648 | tf_op jit(solution)/shard_map/pallas_call | solution.py:162
  56.3 1.8 %collective-permute-start.12 = (bf16[1152,128]{1,0:T(8,128)(2,1)S(1)}, bf16[1152,128]{1,0:T(8,128)(2,1)S(1)}, u32[]{:S(2)}, u32[]{:S(2)}) collective-permute-start(bf16[1152,128]{1,0:T(8,128)(2,1)S(1)} %add_convert_fusion.1), channel_id=1, source_target_pairs={{0,24},{1,25},{2,26},{3,27},{4,28},{5,29},{6,30},{7,31},{8,0},{9,1... | collective-permute-start | bytes 884744 | tf_op jit(solution)/shard_map/ppermute | solution.py:28
  58.7 7.5 %collective-permute-done.12 = bf16[1152,128]{1,0:T(8,128)(2,1)S(1)} collective-permute-done((bf16[1152,128]{1,0:T(8,128)(2,1)S(1)}, bf16[1152,128]{1,0:T(8,128)(2,1)S(1)}, u32[]{:S(2)}, u32[]{:S(2)}) %collective-permute-start.12) | collective-permute-done | bytes 294944 | tf_op jit(solution)/shard_map/ppermute | solution.py:28
  66.3 5.8 %collective-permute-done.15 = bf16[1152,128]{1,0:T(8,128)(2,1)S(1)} collective-permute-done((bf16[1152,128]{1,0:T(8,128)(2,1)S(1)}, bf16[1152,128]{1,0:T(8,128)(2,1)S(1)}, u32[]{:S(2)}, u32[]{:S(2)}) %collective-permute-start.15) | collective-permute-done | bytes 294944 | tf_op jit(solution)/shard_map/ppermute | solution.py:28
  72.3 1.6 %collective-permute-start.9 = (bf16[1168,256]{1,0:T(8,128)(2,1)S(1)}, bf16[1168,256]{1,0:T(8,128)(2,1)S(1)}, u32[]{:S(2)}, u32[]{:S(2)}) collective-permute-start(bf16[1168,256]{1,0:T(8,128)(2,1)S(1)} %shard_map.72), channel_id=1, source_target_pairs={{0,1},{1,0},{2,3},{3,2},{4,5},{5,4},{6,7},{7,6},{8,9},{9,8},{10,11... | collective-permute-start | bytes 1794056 | tf_op jit(solution)/shard_map/ppermute | solution.py:28
  73.9 1.2 %maximum_add_fusion = f32[1152,256]{1,0:T(8,128)} fusion(f32[1152,256]{1,0:T(8,128)S(1)} %get-tuple-element.30, f32[1152,128]{1,0:T(8,128)S(1)} %convert_add_fusion, f32[1152,128]{1,0:T(8,128)S(1)} %convert_add_fusion.1), kind=kLoop, calls=%fused_computation | loop fusion | flops 589824 | bytes 3538944 | tf_op jit(solution)/shard_map/add | solution.py:235
  75.1 12.4 %collective-permute-done.9 = bf16[1168,256]{1,0:T(8,128)(2,1)S(1)} collective-permute-done((bf16[1168,256]{1,0:T(8,128)(2,1)S(1)}, bf16[1168,256]{1,0:T(8,128)(2,1)S(1)}, u32[]{:S(2)}, u32[]{:S(2)}) %collective-permute-start.9) | collective-permute-done | bytes 598048 | tf_op jit(solution)/shard_map/ppermute | solution.py:28
  88.1 1.2 %bitcast_add_fusion = f32[1152,256]{1,0:T(8,128)} fusion(f32[2,1152,256]{2,1,0:T(8,128)S(1)} %get-tuple-element.28.home, bf16[1168,256]{1,0:T(8,128)(2,1)S(1)} %collective-permute-done.9, bf16[2,1168,256]{2,1,0:T(8,128)(2,1)S(1)} %collective-permute-done.8.came), kind=kLoop, calls=%fused_computation.1 | loop fusion | flops 1179648 | bytes 3538944 | tf_op jit(solution)/shard_map/add | solution.py:232
  (31 shorter events, 2.8 us)
Async XLA Ops:
  0.6 5.7 %copy-start = (bf16[1152,256]{1,0:T(8,128)(2,1)S(1)}, bf16[1152,256]{1,0:T(8,128)(2,1)}, u32[]{:S(2)}) copy-start(bf16[1152,256]{1,0:T(8,128)(2,1)} %i0.5) | copy-start | bytes 1769476
  0.6 5.7 %copy-start.1 = (bf16[1152,256]{1,0:T(8,128)(2,1)S(1)}, bf16[1152,256]{1,0:T(8,128)(2,1)}, u32[]{:S(2)}) copy-start(bf16[1152,256]{1,0:T(8,128)(2,1)} %text.1) | copy-start | bytes 1769476
  0.6 16.5 %collective-permute-start.1 = (bf16[1152,256]{1,0:T(8,128)(2,1)}, bf16[1152,256]{1,0:T(8,128)(2,1)S(1)}, u32[]{:S(2)}, u32[]{:S(2)}) collective-permute-start(bf16[1152,256]{1,0:T(8,128)(2,1)} %i0.5), channel_id=1, source_target_pairs={{0,1},{1,0},{2,3},{3,2},{4,5},{5,4},{6,7},{7,6},{8,9},{9,8},{10,11... | collective-permute-start | bytes 1769480 | tf_op jit(solution)/shard_map/ppermute | solution.py:28
  4.7 14.3 %collective-permute-start.3 = (bf16[1152,128]{1,0:T(8,128)(2,1)S(1)}, bf16[1152,128]{1,0:T(8,128)(2,1)}, u32[]{:S(2)}, u32[]{:S(2)}) collective-permute-start(bf16[1152,128]{1,0:T(8,128)(2,1)S(1)} %get-tuple-element.36), channel_id=1, source_target_pairs={{0,8},{1,9},{2,10},{3,11},{4,12},{5,13},{6,14},{7,15},{8,16},{9,17... | collective-permute-start | bytes 884744 | tf_op jit(solution)/shard_map/ppermute | solution.py:28
  6.4 25.2 %collective-permute-start = (bf16[1152,256]{1,0:T(8,128)(2,1)S(1)}, bf16[1152,256]{1,0:T(8,128)(2,1)S(1)}, u32[]{:S(2)}, u32[]{:S(2)}) collective-permute-start(bf16[1152,256]{1,0:T(8,128)(2,1)S(1)} %copy-done), channel_id=1, source_target_pairs={{0,2},{1,3},{2,0},{3,1},{4,6},{5,7},{6,4},{7,5},{8,10},{9,11},{10,... | collective-permute-start | bytes 1769480 | tf_op jit(solution)/shard_map/ppermute | solution.py:28
  6.4 25.2 %collective-permute-start.5 = (bf16[1152,256]{1,0:T(8,128)(2,1)S(1)}, bf16[1152,256]{1,0:T(8,128)(2,1)S(1)}, u32[]{:S(2)}, u32[]{:S(2)}) collective-permute-start(bf16[1152,256]{1,0:T(8,128)(2,1)S(1)} %copy-done.1), channel_id=1, source_target_pairs={{0,4},{1,5},{2,6},{3,7},{8,12},{9,13},{10,14},{11,15},{16,20},{17,... | collective-permute-start | bytes 1769480 | tf_op jit(solution)/shard_map/ppermute | solution.py:28
  17.2 14.4 %collective-permute-start.2 = (bf16[1152,256]{1,0:T(8,128)(2,1)S(1)}, bf16[1152,256]{1,0:T(8,128)(2,1)S(1)}, u32[]{:S(2)}, u32[]{:S(2)}) collective-permute-start(bf16[1152,256]{1,0:T(8,128)(2,1)S(1)} %collective-permute-done.1.i2), channel_id=1, source_target_pairs={{0,2},{1,3},{2,0},{3,1},{4,6},{5,7},{6,4},{7,5},{8,10},{9,11},{10,... | collective-permute-start | bytes 1769480 | tf_op jit(solution)/shard_map/ppermute | solution.py:28
  17.2 11.6 %collective-permute-start.4 = (bf16[1152,128]{1,0:T(8,128)(2,1)S(1)}, bf16[1152,128]{1,0:T(8,128)(2,1)}, u32[]{:S(2)}, u32[]{:S(2)}) collective-permute-start(bf16[1152,128]{1,0:T(8,128)(2,1)S(1)} %get-tuple-element.35), channel_id=1, source_target_pairs={{0,8},{1,9},{2,10},{3,11},{4,12},{5,13},{6,14},{7,15},{8,16},{9,17... | collective-permute-start | bytes 884744 | tf_op jit(solution)/shard_map/ppermute | solution.py:28
  19.0 12.6 %collective-permute-start.6 = (bf16[1152,128]{1,0:T(8,128)(2,1)}, bf16[1152,128]{1,0:T(8,128)(2,1)}, u32[]{:S(2)}, u32[]{:S(2)}) collective-permute-start(bf16[1152,128]{1,0:T(8,128)(2,1)} %collective-permute-done.3.m1), channel_id=1, source_target_pairs={{4,0},{5,1},{6,2},{7,3},{12,8},{13,9},{14,10},{15,11},{20,16},{21,... | collective-permute-start | bytes 884744 | tf_op jit(solution)/shard_map/ppermute | solution.py:28
  28.8 11.9 %collective-permute-start.7 = (bf16[1152,128]{1,0:T(8,128)(2,1)}, bf16[1152,128]{1,0:T(8,128)(2,1)}, u32[]{:S(2)}, u32[]{:S(2)}) collective-permute-start(bf16[1152,128]{1,0:T(8,128)(2,1)} %collective-permute-done.4.m2), channel_id=1, source_target_pairs={{4,0},{5,1},{6,2},{7,3},{12,8},{13,9},{14,10},{15,11},{20,16},{21,... | collective-permute-start | bytes 884744 | tf_op jit(solution)/shard_map/ppermute | solution.py:28
  34.1 22.1 %collective-permute-start.11 = (bf16[1152,128]{1,0:T(8,128)(2,1)S(1)}, bf16[1152,128]{1,0:T(8,128)(2,1)S(1)}, u32[]{:S(2)}, u32[]{:S(2)}) collective-permute-start(bf16[1152,128]{1,0:T(8,128)(2,1)S(1)} %get-tuple-element.31), channel_id=1, source_target_pairs={{0,4},{1,5},{2,6},{3,7},{8,12},{9,13},{10,14},{11,15},{16,20},{17,... | collective-permute-start | bytes 884744 | tf_op jit(solution)/shard_map/ppermute | solution.py:28
  39.4 19.3 %collective-permute-start.10 = (bf16[1152,128]{1,0:T(8,128)(2,1)S(1)}, bf16[1152,128]{1,0:T(8,128)(2,1)S(1)}, u32[]{:S(2)}, u32[]{:S(2)}) collective-permute-start(bf16[1152,128]{1,0:T(8,128)(2,1)S(1)} %get-tuple-element.31), channel_id=1, source_target_pairs={{4,0},{5,1},{6,2},{7,3},{12,8},{13,9},{14,10},{15,11},{20,16},{21,... | collective-permute-start | bytes 884744 | tf_op jit(solution)/shard_map/ppermute | solution.py:28
  43.2 14.9 %collective-permute-start.14 = (bf16[1152,128]{1,0:T(8,128)(2,1)S(1)}, bf16[1152,128]{1,0:T(8,128)(2,1)S(1)}, u32[]{:S(2)}, u32[]{:S(2)}) collective-permute-start(bf16[1152,128]{1,0:T(8,128)(2,1)S(1)} %get-tuple-element.33), channel_id=1, source_target_pairs={{0,4},{1,5},{2,6},{3,7},{8,12},{9,13},{10,14},{11,15},{16,20},{17,... | collective-permute-start | bytes 884744 | tf_op jit(solution)/shard_map/ppermute | solution.py:28
  47.8 18.4 %collective-permute-start.13 = (bf16[1152,128]{1,0:T(8,128)(2,1)S(1)}, bf16[1152,128]{1,0:T(8,128)(2,1)S(1)}, u32[]{:S(2)}, u32[]{:S(2)}) collective-permute-start(bf16[1152,128]{1,0:T(8,128)(2,1)S(1)} %get-tuple-element.33), channel_id=1, source_target_pairs={{4,0},{5,1},{6,2},{7,3},{12,8},{13,9},{14,10},{15,11},{20,16},{21,... | collective-permute-start | bytes 884744 | tf_op jit(solution)/shard_map/ppermute | solution.py:28
  54.5 17.6 %collective-permute-start.8 = (bf16[2,1168,256]{2,1,0:T(8,128)(2,1)S(1)}, bf16[2,1168,256]{2,1,0:T(8,128)(2,1)S(1)}, u32[]{:S(2)}, u32[]{:S(2)}) collective-permute-start(bf16[2,1168,256]{2,1,0:T(8,128)(2,1)S(1)} %shard_map.71), channel_id=1, source_target_pairs={{0,2},{1,3},{2,0},{3,1},{4,6},{5,7},{6,4},{7,5},{8,10},{9,11},{10,... | collective-permute-start | bytes 3588104 | tf_op jit(solution)/shard_map/ppermute | solution.py:28
  56.3 9.9 %collective-permute-start.12 = (bf16[1152,128]{1,0:T(8,128)(2,1)S(1)}, bf16[1152,128]{1,0:T(8,128)(2,1)S(1)}, u32[]{:S(2)}, u32[]{:S(2)}) collective-permute-start(bf16[1152,128]{1,0:T(8,128)(2,1)S(1)} %add_convert_fusion.1), channel_id=1, source_target_pairs={{0,24},{1,25},{2,26},{3,27},{4,28},{5,29},{6,30},{7,31},{8,0},{9,1... | collective-permute-start | bytes 884744 | tf_op jit(solution)/shard_map/ppermute | solution.py:28
  58.2 13.9 %collective-permute-start.15 = (bf16[1152,128]{1,0:T(8,128)(2,1)S(1)}, bf16[1152,128]{1,0:T(8,128)(2,1)S(1)}, u32[]{:S(2)}, u32[]{:S(2)}) collective-permute-start(bf16[1152,128]{1,0:T(8,128)(2,1)S(1)} %add_convert_fusion), channel_id=1, source_target_pairs={{0,24},{1,25},{2,26},{3,27},{4,28},{5,29},{6,30},{7,31},{8,0},{9,1... | collective-permute-start | bytes 884744 | tf_op jit(solution)/shard_map/ppermute | solution.py:28
  72.3 15.2 %collective-permute-start.9 = (bf16[1168,256]{1,0:T(8,128)(2,1)S(1)}, bf16[1168,256]{1,0:T(8,128)(2,1)S(1)}, u32[]{:S(2)}, u32[]{:S(2)}) collective-permute-start(bf16[1168,256]{1,0:T(8,128)(2,1)S(1)} %shard_map.72), channel_id=1, source_target_pairs={{0,1},{1,0},{2,3},{3,2},{4,5},{5,4},{6,7},{7,6},{8,9},{9,8},{10,11... | collective-permute-start | bytes 1794056 | tf_op jit(solution)/shard_map/ppermute | solution.py:28

commit v2 on v1

v2 whole, which is shorter than its diff:
```python
import functools

import jax
import jax.numpy as jnp
from jax import lax
from jax.experimental import pallas as pl
from jax.experimental.pallas import tpu as pltpu
from jax.sharding import PartitionSpec as P

AXES = ("dp", "mp")
WINDOW = 8
PAIR, CORE, SIDE = 1, 2, 4
MASKS = (0, CORE, PAIR, CORE | PAIR)
EXTRA = 16
VMEM_BYTES = 20 * 1024 * 1024

NN = (((1,), (0,)), ((), ()))
NT = (((1,), (1,)), ((), ()))


def dot(a, b, dims):
    return lax.dot_general(a, b, dims, preferred_element_type=jnp.float32)


def moved(block, target):
    n = lax.axis_size(AXES)
    return lax.ppermute(block, AXES, [(i, target(i, n)) for i in range(n)])


def forward(i, n):
    return (i + WINDOW) % n


def back(i, n):
    return (i - WINDOW) % n


def swap(mask):
    return lambda i, n: i ^ mask


def terms(inner, temper, offset):
    z = temper * inner + offset
    e = jnp.exp(-jnp.abs(z))
    r = 1.0 / (1.0 + e)
    return z, jnp.where(z >= 0, r, e * r), jnp.maximum(z, 0.0) + jnp.log1p(e)


def partner_kernel(tb, i0, i1, i2, i3, text, grad_x, grad, loss):
    temper, offset = tb[0], tb[1]
    turned = text[...].T
    images = (i0, i1, i2, i3)
    for r, image in enumerate(images):
        _, s, soft = terms(dot(turned, image[...], NN), temper, offset)
        grad[r] = s.astype(jnp.bfloat16)
        loss[r : r + 1] = jnp.sum(soft, axis=0, keepdims=True)
    tile = 384
    for d in range(0, text.shape[0], tile):
        total = dot(i0[d : d + tile], grad[0], NT)
        for r in (1, 2, 3):
            total = total + dot(images[r][d : d + tile], grad[r], NT)
        grad_x[d : d + tile] = (temper * total).astype(jnp.bfloat16)


def own_kernel(tb, later, i0, i1, i2, i3, text, m1, m2, grad_t, grad_m1, grad_m2, grad, loss, kept, turned, masked):
    temper, offset = tb[0], tb[1]
    rows = text.shape[1]
    half = rows // 2
    kept[0] = text[...]
    kept[1, :, :half] = m1[...]
    kept[1, :, half:] = m2[...]
    turned[0] = text[...].T
    turned[1, :half] = m1[...].T
    turned[1, half:] = m2[...].T
    images = (i0, i1, i2, i3)
    for r, image in enumerate(images):
        same = later[r]
        z, s, soft = terms(dot(turned[1 - same], image[...], NN), temper, offset)
        if r == 0:
            diag = lax.broadcasted_iota(jnp.int32, z.shape, 0) == lax.broadcasted_iota(jnp.int32, z.shape, 1)
            s = jnp.where(diag, s - 1.0, s)
            soft = jnp.where(diag, soft - z, soft)
        g = s.astype(jnp.bfloat16)
        grad[r] = g
        loss[r : r + 1] = jnp.sum(soft, axis=0, keepdims=True)
        masked[0, r] = jnp.where(same == 1, g, jnp.zeros_like(g))
        masked[1, r] = jnp.where(same == 1, jnp.zeros_like(g), g)
    tile = 384
    for d in range(0, text.shape[0], tile):
        total = dot(i0[d : d + tile], masked[0, 0], NT)
        for r in (1, 2, 3):
            total = total + dot(images[r][d : d + tile], masked[0, r], NT)
        grad_t[d : d + tile] = temper * total
        total = dot(i1[d : d + tile], masked[1, 1], NT)
        for r in (2, 3):
            total = total + dot(images[r][d : d + tile], masked[1, r], NT)
        total = temper * total
        grad_m1[d : d + tile] = total[:, :half]
        grad_m2[d : d + tile] = total[:, half:]


def halves_kernel(text, first, second):
    half = first.shape[1]
    first[...] = text[:, :half]
    second[...] = text[:, half:]


def row_total(r, tb, later, kept, k1, k2, g, g1, g2, d, tile):
    same = later[r]
    total = dot(kept[1 - same, d : d + tile], g[r], NN)
    total = total + dot(k1[d : d + tile], g1[r], NN)
    total = total + dot(k2[d : d + tile], g2[r], NN)
    return tb[0] * total


def away_kernel(tb, later, kept, k1, k2, g, g1, g2, l0, l1, l2, out):
    width = k1.shape[0]
    tile = 384
    for slot, r in enumerate((1, 3)):
        for d in range(0, width, tile):
            out[slot, d : d + tile] = row_total(r, tb, later, kept, k1, k2, g, g1, g2, d, tile).astype(jnp.bfloat16)
        out[slot, width:] = packed_loss(l0[r : r + 1] + l1[r : r + 1] + l2[r : r + 1], (EXTRA, out.shape[2]))


def home_kernel(tb, later, kept, k1, k2, g, g1, g2, l0, l1, l2, out, loss):
    width = k1.shape[0]
    tile = 384
    for slot, r in enumerate((0, 2)):
        for d in range(0, width, tile):
            out[slot, d : d + tile] = row_total(r, tb, later, kept, k1, k2, g, g1, g2, d, tile)
        loss[slot : slot + 1] = l0[r : r + 1] + l1[r : r + 1] + l2[r : r + 1]


def packed_loss(value, shape):
    high = value.astype(jnp.bfloat16).astype(jnp.float32)
    place = lax.broadcasted_iota(jnp.int32, shape, 0)
    value, high = jnp.broadcast_to(value, shape), jnp.broadcast_to(high, shape)
    return jnp.where(place == 0, high, jnp.where(place == 1, value - high, 0.0)).astype(jnp.bfloat16)


def unpacked_loss(rows):
    rows = rows.astype(jnp.float32)
    return rows[0:1] + rows[1:2]


def joined_kernel(home, loss, came, out):
    width = home.shape[1]
    out[:width] = (home[1] + came[1, :width].astype(jnp.float32)).astype(jnp.bfloat16)
    out[width:] = packed_loss(loss[1:2] + unpacked_loss(came[1, width:]), (EXTRA, home.shape[2]))


def last_kernel(parts, later, home, loss, came, other, grad_t, r1, r2, p1, p2, grad_image, losses, grad_text, image_buf, loss_buf, text_buf, sems):
    width, rows = grad_text.shape
    half = rows // 2
    low = later[len(MASKS)] == 0
    step = width // parts
    copies = []

    def send(source, target, sem):
        copy = pltpu.make_async_copy(source, target, sems.at[sem])
        copy.start()
        copies.append(copy)

    f32 = jnp.float32
    for k in range(parts):
        d = pl.ds(k * step, step)
        image_buf[d] = home[0, d] + came[0, d].astype(f32) + other[d].astype(f32)
        send(image_buf.at[d], grad_image.at[d], k)
        text_buf[d, :half] = grad_t[d, :half] + jnp.where(low, r1[d].astype(f32), 0.0) + p1[d].astype(f32)
        text_buf[d, half:] = grad_t[d, half:] + jnp.where(low, r2[d].astype(f32), 0.0) + p2[d].astype(f32)
        send(text_buf.at[d], grad_text.at[d], parts + k)
    loss_buf[...] = (loss[0:1] + unpacked_loss(came[0, width:]) + unpacked_loss(other[width:])) / float(rows)
    send(loss_buf, losses, 2 * parts)
    for copy in copies:
        copy.wait()


def call(kernel, out_shape, args, scratch=(), flops=0, out_space=pltpu.VMEM):
    spaces = [pltpu.SMEM if a.ndim == 1 else pltpu.VMEM for a in args]
    return pl.pallas_call(
        kernel,
        out_shape=out_shape,
        in_specs=[pl.BlockSpec(memory_space=s) for s in spaces],
        out_specs=jax.tree.map(lambda _: pl.BlockSpec(memory_space=out_space), out_shape),
        scratch_shapes=list(scratch),
        cost_estimate=pl.CostEstimate(flops=flops, bytes_accessed=0, transcendentals=0),
        compiler_params=pltpu.CompilerParams(vmem_limit_bytes=VMEM_BYTES),
    )(*args)


def shards(image, text, scale, bias):
    width, rows = image.shape
    half = rows // 2
    f32, bf16 = jnp.float32, jnp.bfloat16
    sds = jax.ShapeDtypeStruct
    place = lax.axis_index(AXES) % WINDOW
    tb = jnp.concatenate([scale, bias])
    later = jnp.stack([((place ^ m) >= place).astype(jnp.int32) for m in MASKS] + [(place >= SIDE).astype(jnp.int32)])
    unit = 2 * rows * rows * width

    high = place >= SIDE
    t1, t2 = call(halves_kernel, (sds((width, half), bf16),) * 2, (text,))
    sent, t1, t2 = lax.optimization_barrier((image, t1, t2))
    m1 = moved(t1, forward)
    m2 = moved(t2, forward)
    image_p = moved(sent, swap(PAIR))
    image_c = moved(sent, swap(CORE))
    x1 = moved(jnp.where(high, m1, t1), swap(SIDE))
    x2 = moved(jnp.where(high, m2, t2), swap(SIDE))
    image_pc = moved(image_p, swap(CORE))
    images = (image, image_c, image_p, image_pc)

    def partner(part):
        return call(
            partner_kernel,
            (sds((width, half), bf16), sds((4, half, rows), bf16), sds((8, rows), f32)),
            (tb, *images, part),
            flops=4 * unit,
        )

    grad_x1, g1, l1 = partner(x1)
    late2, _ = lax.optimization_barrier((m2, l1))
    grad_t, grad_m1, grad_m2, g0, l0, kept = call(
        own_kernel,
        (
            sds((width, rows), f32),
            sds((width, half), f32),
            sds((width, half), f32),
            sds((4, rows, rows), bf16),
            sds((8, rows), f32),
            sds((2, width, rows), bf16),
        ),
        (tb, later, *images, text, m1, late2),
        scratch=(pltpu.VMEM((2, rows, width), bf16), pltpu.VMEM((2, 4, rows, rows), bf16)),
        flops=11 * unit,
    )
    x2, _ = lax.optimization_barrier((x2, l0))
    grad_x2, g2, l2 = partner(x2)

    r1 = moved(grad_x1, swap(SIDE))
    r2 = moved(grad_x2, swap(SIDE))
    rest = (tb, later, kept, x1, x2, g0, g1, g2, l0, l1, l2)
    away = call(away_kernel, sds((2, width + EXTRA, rows), bf16), rest, flops=4 * unit)
    came = moved(away, swap(CORE))
    _, l2 = lax.optimization_barrier((r1, l2))
    rest = (tb, later, kept, x1, x2, g0, g1, g2, l0, l1, l2)
    home, home_loss = call(home_kernel, (sds((2, width, rows), f32), sds((8, rows), f32)), rest, flops=120 * unit)
    joined = call(joined_kernel, sds((width + EXTRA, rows), bf16), (home, home_loss, came))
    other = moved(joined, swap(PAIR))
    past1 = moved((grad_m1 + jnp.where(high, r1.astype(f32), 0.0)).astype(bf16), back)
    past2 = moved((grad_m2 + jnp.where(high, r2.astype(f32), 0.0)).astype(bf16), back)
    parts = 4
    grad_image, losses, grad_text = call(
        functools.partial(last_kernel, parts),
        (sds((width, rows), f32), sds((1, rows), f32), sds((width, rows), f32)),
        (later, home, home_loss, came, other, grad_t, r1, r2, past1, past2),
        scratch=(
            pltpu.VMEM((width, rows), f32),
            pltpu.VMEM((1, rows), f32),
            pltpu.VMEM((width, rows), f32),
            pltpu.SemaphoreType.DMA((2 * parts + 1,)),
        ),
        out_space=pl.ANY,
    )
    return grad_image, losses.reshape(rows), grad_text


def solution(mesh):
    spread = P(None, AXES)
    return jax.shard_map(
        shards,
        mesh=mesh,
        in_specs=(spread, spread, P(), P()),
        out_specs=(spread, P(AXES), spread),
        check_vma=False,
    )
```

time: 89.7 us -> 59.4 us (0.66)
  waiting for transfers between devices: 41.6 us -> 20.7 us
  starting transfers between devices: 28.8 us -> 17.7 us
  local copies, waits for them, and re-layouts: 1.1 us -> 3.96 us
  other arithmetic: 3.43 us -> 1.08 us
  Pallas kernels: 12.1 us -> 13.6 us
    ppermute x16 -> x13, waiting for transfers between devices: 41.6 us -> 20.7 us  [moved(): return lax.ppermute(block, AXES, [(i, target(i, n)) for i in range(n)])]
    ppermute x16 -> x13, starting transfers between devices: 28.8 us -> 17.7 us  [moved(): return lax.ppermute(block, AXES, [(i, target(i, n)) for i in range(n)])]
    unnamed x4 -> x14, local copies, waits for them, and re-layouts: 0.01 us -> 3.86 us
    add x4 -> x0, other arithmetic: 2.54 us -> none  [the longest x1 1.23 us: shards(): home[0] + came[0, :width].astype(f32) + other[:width].astype(f32)]
    pallas_call x6 -> x8, Pallas kernels: 12.1 us -> 13.6 us  [call(): pl.pallas_call(kernel, out_shape=out_shape, in_specs=[pl.BlockSpec(memory...]
    slice x2 -> x0, local copies, waits for them, and re-layouts: 1.09 us -> none  [the longest x1 1.09 us: shards(): m2 = moved(text[:, half:], forward)]
  transfers between devices with their start and end apart: 16 -> 13, of which waited for: 5 -> 7; matrix products, arithmetic and copies ran while one was open for 3% -> 2% of each run, Pallas kernels for 13% -> 19%
where the time goes in v2:
time: 59.4 us; the launch traced here: 59.2 us
  waiting for transfers between devices  20.7 us (35%)
  starting transfers between devices  17.7 us (30%)
  Pallas kernels  13.6 us (23%)
  local copies, waits for them, and re-layouts  3.96 us (7%)
  between operations  2.06 us (3%)
  other arithmetic  1.08 us (2%)
    ppermute x13, waiting for transfers between devices, moved(): return lax.ppermute(block, AXES, [(i, target(i, n)) for i in range(n)])  20.7 us
    ppermute x13, starting transfers between devices, moved(): return lax.ppermute(block, AXES, [(i, target(i, n)) for i in range(n)])  17.7 us
    pallas_call x8, Pallas kernels, call(): pl.pallas_call(kernel, out_shape=out_shape, in_specs=[pl.BlockSpec(memory...  13.6 us
    unnamed x14, local copies, waits for them, and re-layouts  3.86 us
  transfers between devices with their start and end apart: 13, of which 7 were waited for; matrix products, arithmetic and copies ran while one was open for 2% of the time, Pallas kernels for 19%

profile of v2, /device:TPU:0, one launch (start us, length us, event | category | flops | bytes accessed | tf_op | source)
XLA Modules:
  0.0 59.2 jit_solution(6788613164848984553)
XLA Ops:
  0.7 1.1 %copy-done.1 = bf16[1152,256]{1,0:T(8,128)(2,1)S(1)} copy-done((bf16[1152,256]{1,0:T(8,128)(2,1)S(1)}, bf16[1152,256]{1,0:T(8,128)(2,1)}, u32[]{:S(2)}) %copy-start.1) | copy-done | bytes 589848
  1.9 3.1 %collective-permute-start.3 = (bf16[1152,128]{1,0:T(8,128)(2,1)S(1)}, bf16[1152,128]{1,0:T(8,128)(2,1)S(1)}, u32[]{:S(2)}, u32[]{:S(2)}) collective-permute-start(bf16[1152,128]{1,0:T(8,128)(2,1)S(1)} %get-tuple-element.31), channel_id=1, source_target_pairs={{0,8},{1,9},{2,10},{3,11},{4,12},{5,13},{6,14},{7,15},{8,16},{9,17... | collective-permute-start | bytes 884744 | tf_op jit(solution)/shard_map/ppermute | solution.py:27
  5.0 1.5 %collective-permute-start.1 = (bf16[1152,256]{1,0:T(8,128)(2,1)}, bf16[1152,256]{1,0:T(8,128)(2,1)S(1)}, u32[]{:S(2)}, u32[]{:S(2)}) collective-permute-start(bf16[1152,256]{1,0:T(8,128)(2,1)} %i0.5), channel_id=1, source_target_pairs={{0,1},{1,0},{2,3},{3,2},{4,5},{5,4},{6,7},{7,6},{8,9},{9,8},{10,11... | collective-permute-start | bytes 1769480 | tf_op jit(solution)/shard_map/ppermute | solution.py:27
  6.4 1.6 %collective-permute-start.4 = (bf16[1152,128]{1,0:T(8,128)(2,1)S(1)}, bf16[1152,128]{1,0:T(8,128)(2,1)S(1)}, u32[]{:S(2)}, u32[]{:S(2)}) collective-permute-start(bf16[1152,128]{1,0:T(8,128)(2,1)S(1)} %get-tuple-element.32), channel_id=1, source_target_pairs={{0,8},{1,9},{2,10},{3,11},{4,12},{5,13},{6,14},{7,15},{8,16},{9,17... | collective-permute-start | bytes 884744 | tf_op jit(solution)/shard_map/ppermute | solution.py:27
  9.3 5.5 %collective-permute-done.3.m1 = bf16[1152,128]{1,0:T(8,128)(2,1)S(1)} collective-permute-done((bf16[1152,128]{1,0:T(8,128)(2,1)S(1)}, bf16[1152,128]{1,0:T(8,128)(2,1)S(1)}, u32[]{:S(2)}, u32[]{:S(2)}) %collective-permute-start.3) | collective-permute-done | bytes 294944 | tf_op jit(solution)/shard_map/ppermute | solution.py:27
  14.8 1.8 %collective-permute-start.5 = (bf16[1152,128]{1,0:T(8,128)(2,1)S(1)}, bf16[1152,128]{1,0:T(8,128)(2,1)S(1)}, u32[]{:S(2)}, u32[]{:S(2)}) collective-permute-start(bf16[1152,128]{1,0:T(8,128)(2,1)S(1)} %broadcast_select_fusion.1), channel_id=1, source_target_pairs={{0,4},{1,5},{2,6},{3,7},{4,0},{5,1},{6,2},{7,3},{8,12},{9,13},{10,... | collective-permute-start | bytes 884744 | tf_op jit(solution)/shard_map/ppermute | solution.py:27
  16.7 3.3 %collective-permute-done.1.i2 = bf16[1152,256]{1,0:T(8,128)(2,1)S(1)} collective-permute-done((bf16[1152,256]{1,0:T(8,128)(2,1)}, bf16[1152,256]{1,0:T(8,128)(2,1)S(1)}, u32[]{:S(2)}, u32[]{:S(2)}) %collective-permute-start.1) | collective-permute-done | bytes 589856 | tf_op jit(solution)/shard_map/ppermute | solution.py:27
  21.1 1.5 %collective-permute-start.6 = (bf16[1152,128]{1,0:T(8,128)(2,1)}, bf16[1152,128]{1,0:T(8,128)(2,1)S(1)}, u32[]{:S(2)}, u32[]{:S(2)}) collective-permute-start(bf16[1152,128]{1,0:T(8,128)(2,1)} %broadcast_select_fusion), channel_id=1, source_target_pairs={{0,4},{1,5},{2,6},{3,7},{4,0},{5,1},{6,2},{7,3},{8,12},{9,13},{10,... | collective-permute-start | bytes 884744 | tf_op jit(solution)/shard_map/ppermute | solution.py:27
  22.7 2.8 %shard_map.68 = (bf16[1152,128]{1,0:T(8,128)(2,1)}, bf16[4,128,256]{2,1,0:T(8,128)(2,1)S(1)}, f32[8,256]{1,0:T(8,128)S(1)}) custom-call(f32[2]{0:T(128)S(1)} %pad_maximum_fusion.tb, bf16[1152,256]{1,0:T(8,128)(2,1)S(1)} %copy-done, bf16[1152,256]{1,0:T(8,128)(2,1)S(1)} %collective-permute-done.i1, bf16[1152,256]{1,0:T(8,128)(2,1)S(1)} %collective-permute-done.1.i2, ...), custom_call_target="tpu_custom_call" | custom-call | flops 603979776 | tf_op jit(solution)/shard_map/pallas_call | solution.py:180
  26.2 0.9 %collective-permute-start.7 = (bf16[1152,128]{1,0:T(8,128)(2,1)}, bf16[1152,128]{1,0:T(8,128)(2,1)S(1)}, u32[]{:S(2)}, u32[]{:S(2)}) collective-permute-start(bf16[1152,128]{1,0:T(8,128)(2,1)} %get-tuple-element.41), channel_id=1, source_target_pairs={{0,4},{1,5},{2,6},{3,7},{4,0},{5,1},{6,2},{7,3},{8,12},{9,13},{10,... | collective-permute-start | bytes 884744 | tf_op jit(solution)/shard_map/ppermute | solution.py:27
  27.2 1.1 %copy-done.2 = bf16[1152,256]{1,0:T(8,128)(2,1)S(1)} copy-done((bf16[1152,256]{1,0:T(8,128)(2,1)S(1)}, bf16[1152,256]{1,0:T(8,128)(2,1)}, u32[]{:S(2)}) %copy-start.2) | copy-done | bytes 589848
  28.2 1.0 %copy-done.4 = bf16[1152,128]{1,0:T(8,128)(2,1)S(1)} copy-done((bf16[1152,128]{1,0:T(8,128)(2,1)S(1)}, bf16[1152,128]{1,0:T(8,128)(2,1)}, u32[]{:S(2)}) %copy-start.4) | copy-done | bytes 294936
  29.2 3.3 %shard_map.69 = (f32[1152,256]{1,0:T(8,128)S(1)}, f32[1152,128]{1,0:T(8,128)S(1)}, f32[1152,128]{1,0:T(8,128)S(1)}, bf16[4,256,256]{2,1,0:T(8,128)(2,1)S(1)}, f3...) custom-call(f32[2]{0:T(128)S(1)} %pad_maximum_fusion.tb, s32[5]{0:T(128)S(1)} %stack.26.later, ...), custom_call_target="tpu_custom_call" | custom-call | flops 1660944384 | tf_op jit(solution)/shard_map/pallas_call | solution.py:180
  32.5 2.1 %shard_map.70 = (bf16[1152,128]{1,0:T(8,128)(2,1)S(1)}, bf16[4,128,256]{2,1,0:T(8,128)(2,1)S(1)}, f32[8,256]{1,0:T(8,128)S(1)}) custom-call(f32[2]{0:T(128)S(1)} %pad_maximum_fusion.tb, bf16[1152,256]{1,0:T(8,128)(2,1)S(1)} %copy-done, bf16[1152,256]{1,0:T(8,128)(2,1)S(1)} %collective-permute-done.i1, bf16[1152,256]{1,0:T(8,128)(2,1)S(1)} %collective-permute-done.1.i2, ...), custom_call_target="tpu_custom_call" | custom-call | flops 603979776 | tf_op jit(solution)/shard_map/pallas_call | solution.py:180
  34.6 1.2 %collective-permute-start.10 = (bf16[1152,128]{1,0:T(8,128)(2,1)S(1)}, bf16[1152,128]{1,0:T(8,128)(2,1)S(1)}, u32[]{:S(2)}, u32[]{:S(2)}) collective-permute-start(bf16[1152,128]{1,0:T(8,128)(2,1)S(1)} %get-tuple-element.47), channel_id=1, source_target_pairs={{0,4},{1,5},{2,6},{3,7},{4,0},{5,1},{6,2},{7,3},{8,12},{9,13},{10,... | collective-permute-start | bytes 884744 | tf_op jit(solution)/shard_map/ppermute | solution.py:27
  35.8 1.6 %shard_map.72 = bf16[2,1168,256]{2,1,0:T(8,128)(2,1)S(1)} custom-call(f32[2]{0:T(128)S(1)} %pad_maximum_fusion.tb, s32[5]{0:T(128)S(1)} %stack.26.later, bf16[2,1152,256]{2,1,0:T(8,128)(2,1)S(1)} %get-tuple-element.35.kept, bf16[1152,128]{1,0:T(8,128)(2,1)S(1)} %collective-permute-done.5.text.k1, bf16[1152,128]{1,0:T(8,128)(2,1)S(1)} %collective-permute-done.6.text.k2, ...), custom_call_target="tpu_custom_call" | custom-call | flops 603979776 | tf_op jit(solution)/shard_map/pallas_call | solution.py:180
  37.6 2.1 %collective-permute-start.11 = (bf16[1152,128]{1,0:T(8,128)(2,1)S(1)}, bf16[1152,128]{1,0:T(8,128)(2,1)S(1)}, u32[]{:S(2)}, u32[]{:S(2)}) collective-permute-start(bf16[1152,128]{1,0:T(8,128)(2,1)S(1)} %add_convert_fusion.1), channel_id=1, source_target_pairs={{0,24},{1,25},{2,26},{3,27},{4,28},{5,29},{6,30},{7,31},{8,0},{9,1... | collective-permute-start | bytes 884744 | tf_op jit(solution)/shard_map/ppermute | solution.py:27
  39.7 1.6 %shard_map.71 = (f32[2,1152,256]{2,1,0:T(8,128)S(1)}, f32[8,256]{1,0:T(8,128)S(1)}) custom-call(f32[2]{0:T(128)S(1)} %pad_maximum_fusion.tb, s32[5]{0:T(128)S(1)} %stack.26.later, bf16[2,1152,256]{2,1,0:T(8,128)(2,1)S(1)} %get-tuple-element.35.kept, bf16[1152,128]{1,0:T(8,128)(2,1)S(1)} %collective-permute-done.5.text.k1, ...), custom_call_target="tpu_custom_call" | custom-call | flops 18119393280 | tf_op jit(solution)/shard_map/pallas_call | solution.py:180
  41.5 1.5 %collective-permute-start.9 = (bf16[1168,256]{1,0:T(8,128)(2,1)S(1)}, bf16[1168,256]{1,0:T(8,128)(2,1)S(1)}, u32[]{:S(2)}, u32[]{:S(2)}) collective-permute-start(bf16[1168,256]{1,0:T(8,128)(2,1)S(1)} %shard_map.73), channel_id=1, source_target_pairs={{0,1},{1,0},{2,3},{3,2},{4,5},{5,4},{6,7},{7,6},{8,9},{9,8},{10,11... | collective-permute-start | bytes 1794056 | tf_op jit(solution)/shard_map/ppermute | solution.py:27
  43.4 2.4 %collective-permute-start.12 = (bf16[1152,128]{1,0:T(8,128)(2,1)S(1)}, bf16[1152,128]{1,0:T(8,128)(2,1)S(1)}, u32[]{:S(2)}, u32[]{:S(2)}) collective-permute-start(bf16[1152,128]{1,0:T(8,128)(2,1)S(1)} %add_convert_fusion), channel_id=1, source_target_pairs={{0,24},{1,25},{2,26},{3,27},{4,28},{5,29},{6,30},{7,31},{8,0},{9,1... | collective-permute-start | bytes 884744 | tf_op jit(solution)/shard_map/ppermute | solution.py:27
  45.8 1.6 %collective-permute-done.11.p1 = bf16[1152,128]{1,0:T(8,128)(2,1)S(1)} collective-permute-done((bf16[1152,128]{1,0:T(8,128)(2,1)S(1)}, bf16[1152,128]{1,0:T(8,128)(2,1)S(1)}, u32[]{:S(2)}, u32[]{:S(2)}) %collective-permute-start.11) | collective-permute-done | bytes 294944 | tf_op jit(solution)/shard_map/ppermute | solution.py:27
  47.5 5.9 %collective-permute-done.12.p2 = bf16[1152,128]{1,0:T(8,128)(2,1)S(1)} collective-permute-done((bf16[1152,128]{1,0:T(8,128)(2,1)S(1)}, bf16[1152,128]{1,0:T(8,128)(2,1)S(1)}, u32[]{:S(2)}, u32[]{:S(2)}) %collective-permute-start.12) | collective-permute-done | bytes 294944 | tf_op jit(solution)/shard_map/ppermute | solution.py:27
  53.4 3.7 %collective-permute-done.9.other = bf16[1168,256]{1,0:T(8,128)(2,1)S(1)} collective-permute-done((bf16[1168,256]{1,0:T(8,128)(2,1)S(1)}, bf16[1168,256]{1,0:T(8,128)(2,1)S(1)}, u32[]{:S(2)}, u32[]{:S(2)}) %collective-permute-start.9) | collective-permute-done | bytes 598048 | tf_op jit(solution)/shard_map/ppermute | solution.py:27
  57.1 2.1 %shard_map.74 = (f32[1152,256]{1,0:T(8,128)}, f32[1,256]{1,0:T(1,128)}, f32[1152,256]{1,0:T(8,128)}) custom-call(s32[5]{0:T(128)S(1)} %stack.26.later, f32[2,1152,256]{2,1,0:T(8,128)S(1)} %get-tuple-element.44.home, f32[8,256]{1,0:T(8,128)S(1)} %get-tuple-element.45.loss, bf16[2,1168,256]{2,1,0:T(8,128)(2,1)S(1)} %collective-permute-done.8.came, ...), custom_call_target="tpu_custom_call" | custom-call | tf_op jit(solution)/shard_map/pallas_call | solution.py:180
  (31 shorter events, 2.9 us)
Async XLA Ops:
  0.6 22.1 %copy-start = (bf16[1152,256]{1,0:T(8,128)(2,1)S(1)}, bf16[1152,256]{1,0:T(8,128)(2,1)}, u32[]{:S(2)}) copy-start(bf16[1152,256]{1,0:T(8,128)(2,1)} %i0.5) | copy-start | bytes 1769476
  0.6 1.1 %copy-start.1 = (bf16[1152,256]{1,0:T(8,128)(2,1)S(1)}, bf16[1152,256]{1,0:T(8,128)(2,1)}, u32[]{:S(2)}) copy-start(bf16[1152,256]{1,0:T(8,128)(2,1)} %text.3) | copy-start | bytes 1769476
  1.9 12.9 %collective-permute-start.3 = (bf16[1152,128]{1,0:T(8,128)(2,1)S(1)}, bf16[1152,128]{1,0:T(8,128)(2,1)S(1)}, u32[]{:S(2)}, u32[]{:S(2)}) collective-permute-start(bf16[1152,128]{1,0:T(8,128)(2,1)S(1)} %get-tuple-element.31), channel_id=1, source_target_pairs={{0,8},{1,9},{2,10},{3,11},{4,12},{5,13},{6,14},{7,15},{8,16},{9,17... | collective-permute-start | bytes 884744 | tf_op jit(solution)/shard_map/ppermute | solution.py:27
  5.0 15.0 %collective-permute-start.1 = (bf16[1152,256]{1,0:T(8,128)(2,1)}, bf16[1152,256]{1,0:T(8,128)(2,1)S(1)}, u32[]{:S(2)}, u32[]{:S(2)}) collective-permute-start(bf16[1152,256]{1,0:T(8,128)(2,1)} %i0.5), channel_id=1, source_target_pairs={{0,1},{1,0},{2,3},{3,2},{4,5},{5,4},{6,7},{7,6},{8,9},{9,8},{10,11... | collective-permute-start | bytes 1769480 | tf_op jit(solution)/shard_map/ppermute | solution.py:27
  6.4 16.3 %collective-permute-start = (bf16[1152,256]{1,0:T(8,128)(2,1)}, bf16[1152,256]{1,0:T(8,128)(2,1)S(1)}, u32[]{:S(2)}, u32[]{:S(2)}) collective-permute-start(bf16[1152,256]{1,0:T(8,128)(2,1)} %i0.5), channel_id=1, source_target_pairs={{0,2},{1,3},{2,0},{3,1},{4,6},{5,7},{6,4},{7,5},{8,10},{9,11},{10,... | collective-permute-start | bytes 1769480 | tf_op jit(solution)/shard_map/ppermute | solution.py:27
  6.4 13.9 %collective-permute-start.4 = (bf16[1152,128]{1,0:T(8,128)(2,1)S(1)}, bf16[1152,128]{1,0:T(8,128)(2,1)S(1)}, u32[]{:S(2)}, u32[]{:S(2)}) collective-permute-start(bf16[1152,128]{1,0:T(8,128)(2,1)S(1)} %get-tuple-element.32), channel_id=1, source_target_pairs={{0,8},{1,9},{2,10},{3,11},{4,12},{5,13},{6,14},{7,15},{8,16},{9,17... | collective-permute-start | bytes 884744 | tf_op jit(solution)/shard_map/ppermute | solution.py:27
  14.8 7.8 %collective-permute-start.5 = (bf16[1152,128]{1,0:T(8,128)(2,1)S(1)}, bf16[1152,128]{1,0:T(8,128)(2,1)S(1)}, u32[]{:S(2)}, u32[]{:S(2)}) collective-permute-start(bf16[1152,128]{1,0:T(8,128)(2,1)S(1)} %broadcast_select_fusion.1), channel_id=1, source_target_pairs={{0,4},{1,5},{2,6},{3,7},{4,0},{5,1},{6,2},{7,3},{8,12},{9,13},{10,... | collective-permute-start | bytes 884744 | tf_op jit(solution)/shard_map/ppermute | solution.py:27
  20.0 2.7 %collective-permute-start.2 = (bf16[1152,256]{1,0:T(8,128)(2,1)S(1)}, bf16[1152,256]{1,0:T(8,128)(2,1)S(1)}, u32[]{:S(2)}, u32[]{:S(2)}) collective-permute-start(bf16[1152,256]{1,0:T(8,128)(2,1)S(1)} %collective-permute-done.1.i2), channel_id=1, source_target_pairs={{0,2},{1,3},{2,0},{3,1},{4,6},{5,7},{6,4},{7,5},{8,10},{9,11},{10,... | collective-permute-start | bytes 1769480 | tf_op jit(solution)/shard_map/ppermute | solution.py:27
  20.3 5.2 %copy-start.3 = (bf16[1152,128]{1,0:T(8,128)(2,1)}, bf16[1152,128]{1,0:T(8,128)(2,1)S(1)}, u32[]{:S(2)}) copy-start(bf16[1152,128]{1,0:T(8,128)(2,1)S(1)} %collective-permute-done.4.m2) | copy-start | bytes 884740
  21.1 11.4 %collective-permute-start.6 = (bf16[1152,128]{1,0:T(8,128)(2,1)}, bf16[1152,128]{1,0:T(8,128)(2,1)S(1)}, u32[]{:S(2)}, u32[]{:S(2)}) collective-permute-start(bf16[1152,128]{1,0:T(8,128)(2,1)} %broadcast_select_fusion), channel_id=1, source_target_pairs={{0,4},{1,5},{2,6},{3,7},{4,0},{5,1},{6,2},{7,3},{8,12},{9,13},{10,... | collective-permute-start | bytes 884744 | tf_op jit(solution)/shard_map/ppermute | solution.py:27
  25.5 0.7 %copy-start.5 = (bf16[4,128,256]{2,1,0:T(8,128)(2,1)}, bf16[4,128,256]{2,1,0:T(8,128)(2,1)S(1)}, u32[]{:S(2)}) copy-start(bf16[4,128,256]{2,1,0:T(8,128)(2,1)S(1)} %get-tuple-element.39.g1) | copy-start | bytes 786436
  26.2 11.3 %collective-permute-start.7 = (bf16[1152,128]{1,0:T(8,128)(2,1)}, bf16[1152,128]{1,0:T(8,128)(2,1)S(1)}, u32[]{:S(2)}, u32[]{:S(2)}) collective-permute-start(bf16[1152,128]{1,0:T(8,128)(2,1)} %get-tuple-element.41), channel_id=1, source_target_pairs={{0,4},{1,5},{2,6},{3,7},{4,0},{5,1},{6,2},{7,3},{8,12},{9,13},{10,... | collective-permute-start | bytes 884744 | tf_op jit(solution)/shard_map/ppermute | solution.py:27
  27.2 1.1 %copy-start.2 = (bf16[1152,256]{1,0:T(8,128)(2,1)S(1)}, bf16[1152,256]{1,0:T(8,128)(2,1)}, u32[]{:S(2)}) copy-start(bf16[1152,256]{1,0:T(8,128)(2,1)} %text.3) | copy-start | bytes 1769476
  28.2 1.0 %copy-start.4 = (bf16[1152,128]{1,0:T(8,128)(2,1)S(1)}, bf16[1152,128]{1,0:T(8,128)(2,1)}, u32[]{:S(2)}) copy-start(bf16[1152,128]{1,0:T(8,128)(2,1)} %copy-done.3) | copy-start | bytes 884740
  32.5 3.3 %copy-start.6 = (bf16[4,128,256]{2,1,0:T(8,128)(2,1)S(1)}, bf16[4,128,256]{2,1,0:T(8,128)(2,1)}, u32[]{:S(2)}) copy-start(bf16[4,128,256]{2,1,0:T(8,128)(2,1)} %copy-done.5) | copy-start | bytes 786436
  34.6 8.7 %collective-permute-start.10 = (bf16[1152,128]{1,0:T(8,128)(2,1)S(1)}, bf16[1152,128]{1,0:T(8,128)(2,1)S(1)}, u32[]{:S(2)}, u32[]{:S(2)}) collective-permute-start(bf16[1152,128]{1,0:T(8,128)(2,1)S(1)} %get-tuple-element.47), channel_id=1, source_target_pairs={{0,4},{1,5},{2,6},{3,7},{4,0},{5,1},{6,2},{7,3},{8,12},{9,13},{10,... | collective-permute-start | bytes 884744 | tf_op jit(solution)/shard_map/ppermute | solution.py:27
  37.4 3.9 %collective-permute-start.8 = (bf16[2,1168,256]{2,1,0:T(8,128)(2,1)S(1)}, bf16[2,1168,256]{2,1,0:T(8,128)(2,1)S(1)}, u32[]{:S(2)}, u32[]{:S(2)}) collective-permute-start(bf16[2,1168,256]{2,1,0:T(8,128)(2,1)S(1)} %shard_map.72), channel_id=1, source_target_pairs={{0,2},{1,3},{2,0},{3,1},{4,6},{5,7},{6,4},{7,5},{8,10},{9,11},{10,... | collective-permute-start | bytes 3588104 | tf_op jit(solution)/shard_map/ppermute | solution.py:27
  37.6 9.9 %collective-permute-start.11 = (bf16[1152,128]{1,0:T(8,128)(2,1)S(1)}, bf16[1152,128]{1,0:T(8,128)(2,1)S(1)}, u32[]{:S(2)}, u32[]{:S(2)}) collective-permute-start(bf16[1152,128]{1,0:T(8,128)(2,1)S(1)} %add_convert_fusion.1), channel_id=1, source_target_pairs={{0,24},{1,25},{2,26},{3,27},{4,28},{5,29},{6,30},{7,31},{8,0},{9,1... | collective-permute-start | bytes 884744 | tf_op jit(solution)/shard_map/ppermute | solution.py:27
  41.5 15.7 %collective-permute-start.9 = (bf16[1168,256]{1,0:T(8,128)(2,1)S(1)}, bf16[1168,256]{1,0:T(8,128)(2,1)S(1)}, u32[]{:S(2)}, u32[]{:S(2)}) collective-permute-start(bf16[1168,256]{1,0:T(8,128)(2,1)S(1)} %shard_map.73), channel_id=1, source_target_pairs={{0,1},{1,0},{2,3},{3,2},{4,5},{5,4},{6,7},{7,6},{8,9},{9,8},{10,11... | collective-permute-start | bytes 1794056 | tf_op jit(solution)/shard_map/ppermute | solution.py:27
  43.4 10.0 %collective-permute-start.12 = (bf16[1152,128]{1,0:T(8,128)(2,1)S(1)}, bf16[1152,128]{1,0:T(8,128)(2,1)S(1)}, u32[]{:S(2)}, u32[]{:S(2)}) collective-permute-start(bf16[1152,128]{1,0:T(8,128)(2,1)S(1)} %add_convert_fusion), channel_id=1, source_target_pairs={{0,24},{1,25},{2,26},{3,27},{4,28},{5,29},{6,30},{7,31},{8,0},{9,1... | collective-permute-start | bytes 884744 | tf_op jit(solution)/shard_map/ppermute | solution.py:27

commit v3 on v2

v3 whole, which is shorter than its diff:
```python
import functools

import jax
import jax.numpy as jnp
from jax import lax
from jax.experimental import pallas as pl
from jax.experimental.pallas import tpu as pltpu
from jax.sharding import PartitionSpec as P

AXES = ("dp", "mp")
WINDOW = 8
PAIR, CORE, SIDE = 1, 2, 4
MASKS = (0, CORE, PAIR, CORE | PAIR)
EXTRA = 16
TILE = 384
VMEM_BYTES = 20 * 1024 * 1024

NN = (((1,), (0,)), ((), ()))
NT = (((1,), (1,)), ((), ()))


def dot(a, b, dims):
    return lax.dot_general(a, b, dims, preferred_element_type=jnp.float32)


def moved(block, target):
    n = lax.axis_size(AXES)
    return lax.ppermute(block, AXES, [(i, target(i, n)) for i in range(n)])


def forward(i, n):
    return (i + WINDOW) % n


def back(i, n):
    return (i - WINDOW) % n


def swap(mask):
    return lambda i, n: i ^ mask


GROUP = 8


def terms(inner, tb):
    z = tb[0] * inner + tb[1]
    e = jnp.exp(-jnp.abs(z))
    u = 1.0 + e
    r = pl.reciprocal(u, approx=True)
    r = r * (2.0 - u * r)
    product = e[:GROUP]
    positive = jnp.maximum(z[:GROUP], 0.0)
    for d in range(GROUP, z.shape[0], GROUP):
        product = product * u[d : d + GROUP] + e[d : d + GROUP]
        positive = positive + jnp.maximum(z[d : d + GROUP], 0.0)
    soft = jnp.sum(jnp.log1p(product) + positive, axis=0, keepdims=True)
    return z, jnp.where(z >= 0, r, e * r), soft


def scores(tb, images, turned, grad, loss):
    for r, image in enumerate(images):
        _, s, soft = terms(dot(turned, image[...], NN), tb)
        grad[r] = s.astype(jnp.bfloat16)
        loss[r : r + 1] = soft


def text_side(tb, images, grad, out):
    for d in range(0, out.shape[0], TILE):
        total = dot(images[0][d : d + TILE], grad[0], NT)
        for r in (1, 2, 3):
            total = total + dot(images[r][d : d + TILE], grad[r], NT)
        out[d : d + TILE] = (tb[0] * total).astype(jnp.bfloat16)


def partner_kernel(tb, i0, i1, i2, i3, text, grad_x, grad, loss):
    scores(tb, (i0, i1, i2, i3), text[...].T, grad, loss)
    text_side(tb, (i0, i1, i2, i3), grad, grad_x)


def text_kernel(tb, i0, i1, i2, i3, grad, grad_x):
    text_side(tb, (i0, i1, i2, i3), grad, grad_x)


def own_kernel(tb, later, i0, i1, i2, i3, text, m1, m2, grad_t, grad_m1, grad_m2, grad, loss, kept, turned, masked):
    temper = tb[0]
    rows = text.shape[1]
    half = rows // 2
    kept[0] = text[...]
    kept[1, :, :half] = m1[...]
    kept[1, :, half:] = m2[...]
    turned[0] = text[...].T
    turned[1, :half] = m1[...].T
    turned[1, half:] = m2[...].T
    images = (i0, i1, i2, i3)
    for r, image in enumerate(images):
        same = later[r]
        z, s, soft = terms(dot(turned[1 - same], image[...], NN), tb)
        if r == 0:
            diag = lax.broadcasted_iota(jnp.int32, z.shape, 0) == lax.broadcasted_iota(jnp.int32, z.shape, 1)
            s = jnp.where(diag, s - 1.0, s)
            soft = soft - jnp.sum(jnp.where(diag, z, 0.0), axis=0, keepdims=True)
        g = s.astype(jnp.bfloat16)
        grad[r] = g
        loss[r : r + 1] = soft
        masked[0, r] = jnp.where(same == 1, g, jnp.zeros_like(g))
        masked[1, r] = jnp.where(same == 1, jnp.zeros_like(g), g)
    for d in range(0, text.shape[0], TILE):
        total = dot(i0[d : d + TILE], masked[0, 0], NT)
        for r in (1, 2, 3):
            total = total + dot(images[r][d : d + TILE], masked[0, r], NT)
        grad_t[d : d + TILE] = temper * total
        total = dot(i1[d : d + TILE], masked[1, 1], NT)
        for r in (2, 3):
            total = total + dot(images[r][d : d + TILE], masked[1, r], NT)
        total = temper * total
        grad_m1[d : d + TILE] = total[:, :half]
        grad_m2[d : d + TILE] = total[:, half:]


def halves_kernel(text, first, second):
    half = first.shape[1]
    first[...] = text[:, :half]
    second[...] = text[:, half:]


def packed_loss(value, shape):
    high = value.astype(jnp.bfloat16).astype(jnp.float32)
    place = lax.broadcasted_iota(jnp.int32, shape, 0)
    value, high = jnp.broadcast_to(value, shape), jnp.broadcast_to(high, shape)
    return jnp.where(place == 0, high, jnp.where(place == 1, value - high, 0.0)).astype(jnp.bfloat16)


def unpacked_loss(rows):
    rows = rows.astype(jnp.float32)
    return rows[0:1] + rows[1:2]


def early_kernel(which, later, kept, k1, g, g1, part):
    for slot, r in enumerate(which):
        column = 1 - later[r]
        for d in range(0, k1.shape[0], TILE):
            part[slot, d : d + TILE] = dot(kept[column, d : d + TILE], g[r], NN) + dot(k1[d : d + TILE], g1[r], NN)


def away_kernel(tb, i0, i1, i2, i3, text, part, l0, l1, grad, loss, out):
    scores(tb, (i0, i1, i2, i3), text[...].T, grad, loss)
    width = text.shape[0]
    for slot, r in enumerate((1, 3)):
        for d in range(0, width, TILE):
            out[slot, d : d + TILE] = (tb[0] * (part[slot, d : d + TILE] + dot(text[d : d + TILE], grad[r], NN))).astype(jnp.bfloat16)
        out[slot, width:] = packed_loss(l0[r : r + 1] + l1[r : r + 1] + loss[r : r + 1], (EXTRA, out.shape[2]))


def joined_kernel(tb, text, part, grad, l0, l1, l2, came, out):
    width = text.shape[0]
    for d in range(0, width, TILE):
        total = tb[0] * (part[1, d : d + TILE] + dot(text[d : d + TILE], grad[2], NN))
        out[d : d + TILE] = (total + came[1, d : d + TILE].astype(jnp.float32)).astype(jnp.bfloat16)
    loss = l0[2:3] + l1[2:3] + l2[2:3] + unpacked_loss(came[1, width:])
    out[width:] = packed_loss(loss, (EXTRA, out.shape[1]))


def home_kernel(tb, text, part, grad, l0, l1, l2, came, out, loss):
    width = text.shape[0]
    for d in range(0, width, TILE):
        total = tb[0] * (part[0, d : d + TILE] + dot(text[d : d + TILE], grad[0], NN))
        out[d : d + TILE] = total + came[0, d : d + TILE].astype(jnp.float32)
    loss[0:1] = l0[0:1] + l1[0:1] + l2[0:1] + unpacked_loss(came[0, width:])


def older_kernel(later, grad_m, returned, out):
    high = later[len(MASKS)] == 1
    out[...] = (grad_m[...] + jnp.where(high, returned[...].astype(jnp.float32), 0.0)).astype(jnp.bfloat16)


def last_kernel(parts, later, grad_t, r1, r2, p1, p2, home, loss, other, grad_image, losses, grad_text, image_buf, loss_buf, text_buf, sems):
    width, rows = grad_text.shape
    half, step = rows // 2, width // parts
    low = later[len(MASKS)] == 0
    f32 = jnp.float32
    copies = []

    def send(source, target):
        copy = pltpu.make_async_copy(source, target, sems.at[len(copies)])
        copy.start()
        copies.append(copy)

    for k in range(parts):
        d = pl.ds(k * step, step)
        image_buf[d] = home[d] + other[d].astype(f32)
        send(image_buf.at[d], grad_image.at[d])
    loss_buf[...] = (loss[0:1] + unpacked_loss(other[width:])) / float(rows)
    send(loss_buf, losses)
    for k in range(parts):
        d = pl.ds(k * step, step)
        text_buf[d, :half] = grad_t[d, :half] + jnp.where(low, r1[d].astype(f32), 0.0) + p1[d].astype(f32)
        text_buf[d, half:] = grad_t[d, half:] + jnp.where(low, r2[d].astype(f32), 0.0) + p2[d].astype(f32)
        send(text_buf.at[d], grad_text.at[d])
    for copy in copies:
        copy.wait()


def call(kernel, out_shape, args, scratch=(), flops=0, out_space=pltpu.VMEM):
    spaces = [pltpu.SMEM if a.ndim == 1 else pltpu.VMEM for a in args]
    return pl.pallas_call(
        kernel,
        out_shape=out_shape,
        in_specs=[pl.BlockSpec(memory_space=s) for s in spaces],
        out_specs=jax.tree.map(lambda _: pl.BlockSpec(memory_space=out_space), out_shape),
        scratch_shapes=list(scratch),
        cost_estimate=pl.CostEstimate(flops=flops, bytes_accessed=0, transcendentals=0) if flops else None,
        compiler_params=pltpu.CompilerParams(vmem_limit_bytes=VMEM_BYTES),
    )(*args)


def shards(image, text, scale, bias):
    width, rows = image.shape
    half = rows // 2
    f32, bf16 = jnp.float32, jnp.bfloat16
    sds = jax.ShapeDtypeStruct
    place = lax.axis_index(AXES) % WINDOW
    tb = jnp.concatenate([scale, bias])
    later = jnp.stack([((place ^ m) >= place).astype(jnp.int32) for m in MASKS] + [(place >= SIDE).astype(jnp.int32)])
    unit = 2 * rows * rows * width

    high = place >= SIDE
    t1, t2 = call(halves_kernel, (sds((width, half), bf16),) * 2, (text,))
    sent, t1, t2 = lax.optimization_barrier((image, t1, t2))
    m1 = moved(t1, forward)
    m2 = moved(t2, forward)
    image_p = moved(sent, swap(PAIR))
    image_c = moved(sent, swap(CORE))
    x1 = moved(jnp.where(high, m1, t1), swap(SIDE))
    x2 = moved(jnp.where(high, m2, t2), swap(SIDE))
    image_pc = moved(image_p, swap(CORE))
    images = (image, image_c, image_p, image_pc)

    grad_t, grad_m1, grad_m2, g0, l0, kept = call(
        own_kernel,
        (
            sds((width, rows), f32),
            sds((width, half), f32),
            sds((width, half), f32),
            sds((4, rows, rows), bf16),
            sds((8, rows), f32),
            sds((2, width, rows), bf16),
        ),
        (tb, later, *images, text, m1, m2),
        scratch=(pltpu.VMEM((2, rows, width), bf16), pltpu.VMEM((2, 4, rows, rows), bf16)),
    )
    x1, _ = lax.optimization_barrier((x1, l0))
    scored = (sds((4, half, rows), bf16), sds((8, rows), f32))
    grad_x1, g1, l1 = call(partner_kernel, (sds((width, half), bf16), *scored), (tb, *images, x1))
    part = call(functools.partial(early_kernel, (1, 3)), sds((2, width, rows), f32), (later, kept, x1, g0, g1))
    g2, l2, away = call(away_kernel, (*scored, sds((2, width + EXTRA, rows), bf16)), (tb, *images, x2, part, l0, l1))
    came = moved(away, swap(CORE))
    grad_x2 = call(text_kernel, sds((width, half), bf16), (tb, *images, g2))
    _, held1 = lax.optimization_barrier((grad_x2, g1))
    part = call(functools.partial(early_kernel, (0, 2)), sds((2, width, rows), f32), (later, kept, x1, g0, held1))
    r1 = moved(grad_x1, swap(SIDE))
    r2 = moved(grad_x2, swap(SIDE))

    older = sds((width, half), bf16)
    older1 = call(older_kernel, older, (later, grad_m1, r1), flops=80 * unit)
    _, held = lax.optimization_barrier((older1, l2))
    joined = call(joined_kernel, sds((width + EXTRA, rows), bf16), (tb, x2, part, g2, l0, l1, held, came), flops=0 * unit)
    other = moved(joined, swap(PAIR))
    older1, grad_m2, _ = lax.optimization_barrier((older1, grad_m2, joined))
    past1 = moved(older1, back)
    past2 = moved(call(older_kernel, older, (later, grad_m2, r2), flops=20 * unit), back)
    _, late = lax.optimization_barrier((past1, l2))
    rest = (tb, x2, part, g2, l0, l1, late, came)
    home, home_loss = call(home_kernel, (sds((width, rows), f32), sds((8, rows), f32)), rest, flops=5 * unit)
    parts = 4
    grad_image, losses, grad_text = call(
        functools.partial(last_kernel, parts),
        (sds((width, rows), f32), sds((1, rows), f32), sds((width, rows), f32)),
        (later, grad_t, r1, r2, past1, past2, home, home_loss, other),
        scratch=(
            pltpu.VMEM((width, rows), f32),
            pltpu.VMEM((1, rows), f32),
            pltpu.VMEM((width, rows), f32),
            pltpu.SemaphoreType.DMA((2 * parts + 1,)),
        ),
        out_space=pl.ANY,
    )
    return grad_image, losses.reshape(rows), grad_text


def solution(mesh):
    spread = P(None, AXES)
    return jax.shard_map(
        shards,
        mesh=mesh,
        in_specs=(spread, spread, P(), P()),
        out_specs=(spread, P(AXES), spread),
        check_vma=False,
    )
```

time: 59.4 us -> 55.9 us (0.941)
  waiting for transfers between devices: 20.7 us -> 17.9 us
  local copies, waits for them, and re-layouts: 3.96 us -> 1.23 us
  Pallas kernels: 13.6 us -> 15.9 us
  other arithmetic: 1.08 us -> 0.15 us
  starting transfers between devices: 17.7 us -> 18.5 us
    ppermute x13, waiting for transfers between devices: 20.7 us -> 17.9 us  [moved(): return lax.ppermute(block, AXES, [(i, target(i, n)) for i in range(n)])]
    unnamed x14 -> x6, local copies, waits for them, and re-layouts: 3.86 us -> 1.13 us
    pallas_call x8 -> x12, Pallas kernels: 13.6 us -> 15.9 us  [call(): pl.pallas_call(kernel, out_shape=out_shape, in_specs=[pl.BlockSpec(memory...]
    ppermute x13, starting transfers between devices: 17.7 us -> 18.5 us  [moved(): return lax.ppermute(block, AXES, [(i, target(i, n)) for i in range(n)])]
    select_n x1, other arithmetic: 0.79 us -> 0.03 us  [shards(): x2 = moved(jnp.where(high, m2, t2), swap(SIDE))]
  transfers between devices with their start and end apart: 13 -> 13, of which waited for: 7 -> 7; matrix products, arithmetic and copies ran while one was open for 2% -> 0% of each run, Pallas kernels for 19% -> 25%
where the time goes in v3:
time: 55.9 us; the launch traced here: 55.7 us
  starting transfers between devices  18.5 us (33%)
  waiting for transfers between devices  17.9 us (32%)
  Pallas kernels  15.9 us (28%)
  between operations  2.07 us (4%)
  local copies, waits for them, and re-layouts  1.23 us (2%)
    ppermute x13, starting transfers between devices, moved(): return lax.ppermute(block, AXES, [(i, target(i, n)) for i in range(n)])  18.5 us
    ppermute x13, waiting for transfers between devices, moved(): return lax.ppermute(block, AXES, [(i, target(i, n)) for i in range(n)])  17.9 us
    pallas_call x12, Pallas kernels, call(): pl.pallas_call(kernel, out_shape=out_shape, in_specs=[pl.BlockSpec(memory...  15.9 us
    unnamed x6, local copies, waits for them, and re-layouts  1.13 us
  transfers between devices with their start and end apart: 13, of which 7 were waited for; matrix products, arithmetic and copies ran while one was open for 0% of the time, Pallas kernels for 25%

profile of v3, /device:TPU:0, one launch (start us, length us, event | category | flops | bytes accessed | tf_op | source)
XLA Modules:
  0.0 55.7 jit_solution(3310924931844636439)
XLA Ops:
  0.7 1.1 %copy-done.1 = bf16[1152,256]{1,0:T(8,128)(2,1)S(1)} copy-done((bf16[1152,256]{1,0:T(8,128)(2,1)S(1)}, bf16[1152,256]{1,0:T(8,128)(2,1)}, u32[]{:S(2)}) %copy-start.1) | copy-done | bytes 589848
  1.9 3.1 %collective-permute-start.3 = (bf16[1152,128]{1,0:T(8,128)(2,1)S(1)}, bf16[1152,128]{1,0:T(8,128)(2,1)S(1)}, u32[]{:S(2)}, u32[]{:S(2)}) collective-permute-start(bf16[1152,128]{1,0:T(8,128)(2,1)S(1)} %get-tuple-element.34), channel_id=1, source_target_pairs={{0,8},{1,9},{2,10},{3,11},{4,12},{5,13},{6,14},{7,15},{8,16},{9,17... | collective-permute-start | bytes 884744 | tf_op jit(solution)/shard_map/ppermute | solution.py:28
  5.0 1.5 %collective-permute-start.1 = (bf16[1152,256]{1,0:T(8,128)(2,1)}, bf16[1152,256]{1,0:T(8,128)(2,1)S(1)}, u32[]{:S(2)}, u32[]{:S(2)}) collective-permute-start(bf16[1152,256]{1,0:T(8,128)(2,1)} %i0.7), channel_id=1, source_target_pairs={{0,1},{1,0},{2,3},{3,2},{4,5},{5,4},{6,7},{7,6},{8,9},{9,8},{10,11... | collective-permute-start | bytes 1769480 | tf_op jit(solution)/shard_map/ppermute | solution.py:28
  6.4 1.6 %collective-permute-start.4 = (bf16[1152,128]{1,0:T(8,128)(2,1)S(1)}, bf16[1152,128]{1,0:T(8,128)(2,1)S(1)}, u32[]{:S(2)}, u32[]{:S(2)}) collective-permute-start(bf16[1152,128]{1,0:T(8,128)(2,1)S(1)} %get-tuple-element.35), channel_id=1, source_target_pairs={{0,8},{1,9},{2,10},{3,11},{4,12},{5,13},{6,14},{7,15},{8,16},{9,17... | collective-permute-start | bytes 884744 | tf_op jit(solution)/shard_map/ppermute | solution.py:28
  9.4 5.4 %collective-permute-done.3.m1 = bf16[1152,128]{1,0:T(8,128)(2,1)S(1)} collective-permute-done((bf16[1152,128]{1,0:T(8,128)(2,1)S(1)}, bf16[1152,128]{1,0:T(8,128)(2,1)S(1)}, u32[]{:S(2)}, u32[]{:S(2)}) %collective-permute-start.3) | collective-permute-done | bytes 294944 | tf_op jit(solution)/shard_map/ppermute | solution.py:28
  14.8 1.8 %collective-permute-start.5 = (bf16[1152,128]{1,0:T(8,128)(2,1)S(1)}, bf16[1152,128]{1,0:T(8,128)(2,1)S(1)}, u32[]{:S(2)}, u32[]{:S(2)}) collective-permute-start(bf16[1152,128]{1,0:T(8,128)(2,1)S(1)} %broadcast_select_fusion.1), channel_id=1, source_target_pairs={{0,4},{1,5},{2,6},{3,7},{4,0},{5,1},{6,2},{7,3},{8,12},{9,13},{10,... | collective-permute-start | bytes 884744 | tf_op jit(solution)/shard_map/ppermute | solution.py:28
  16.7 3.3 %collective-permute-done.1.i2 = bf16[1152,256]{1,0:T(8,128)(2,1)S(1)} collective-permute-done((bf16[1152,256]{1,0:T(8,128)(2,1)}, bf16[1152,256]{1,0:T(8,128)(2,1)S(1)}, u32[]{:S(2)}, u32[]{:S(2)}) %collective-permute-start.1) | collective-permute-done | bytes 589856 | tf_op jit(solution)/shard_map/ppermute | solution.py:28
  20.3 1.6 %collective-permute-start.7 = (bf16[1152,128]{1,0:T(8,128)(2,1)S(1)}, bf16[1152,128]{1,0:T(8,128)(2,1)S(1)}, u32[]{:S(2)}, u32[]{:S(2)}) collective-permute-start(bf16[1152,128]{1,0:T(8,128)(2,1)S(1)} %broadcast_select_fusion), channel_id=1, source_target_pairs={{0,4},{1,5},{2,6},{3,7},{4,0},{5,1},{6,2},{7,3},{8,12},{9,13},{10,... | collective-permute-start | bytes 884744 | tf_op jit(solution)/shard_map/ppermute | solution.py:28
  22.0 3.2 %shard_map.68 = (f32[1152,256]{1,0:T(8,128)S(1)}, f32[1152,128]{1,0:T(8,128)S(1)}, f32[1152,128]{1,0:T(8,128)S(1)}, bf16[4,256,256]{2,1,0:T(8,128)(2,1)S(1)}, f3...) custom-call(f32[2]{0:T(128)S(1)} %pad_maximum_fusion.tb, s32[5]{0:T(128)S(1)} %stack.26.later, ...), custom_call_target="tpu_custom_call" | custom-call | tf_op jit(solution)/shard_map/pallas_call | solution.py:206
  25.2 2.0 %shard_map.69 = (bf16[1152,128]{1,0:T(8,128)(2,1)S(1)}, bf16[4,128,256]{2,1,0:T(8,128)(2,1)S(1)}, f32[8,256]{1,0:T(8,128)S(1)}) custom-call(f32[2]{0:T(128)S(1)} %pad_maximum_fusion.tb, bf16[1152,256]{1,0:T(8,128)(2,1)S(1)} %copy-done, bf16[1152,256]{1,0:T(8,128)(2,1)S(1)} %collective-permute-done.i1, bf16[1152,256]{1,0:T(8,128)(2,1)S(1)} %collective-permute-done.1.i2, ...), custom_call_target="tpu_custom_call" | custom-call | tf_op jit(solution)/shard_map/pallas_call | solution.py:206
  27.2 1.5 %collective-permute-start.6 = (bf16[1152,128]{1,0:T(8,128)(2,1)S(1)}, bf16[1152,128]{1,0:T(8,128)(2,1)S(1)}, u32[]{:S(2)}, u32[]{:S(2)}) collective-permute-start(bf16[1152,128]{1,0:T(8,128)(2,1)S(1)} %get-tuple-element.39), channel_id=1, source_target_pairs={{0,4},{1,5},{2,6},{3,7},{4,0},{5,1},{6,2},{7,3},{8,12},{9,13},{10,... | collective-permute-start | bytes 884744 | tf_op jit(solution)/shard_map/ppermute | solution.py:28
  28.8 1.3 %shard_map.70.part = f32[2,1152,256]{2,1,0:T(8,128)S(1)} custom-call(s32[5]{0:T(128)S(1)} %stack.26.later, bf16[2,1152,256]{2,1,0:T(8,128)(2,1)S(1)} %get-tuple-element.40.kept, bf16[1152,128]{1,0:T(8,128)(2,1)S(1)} %collective-permute-done.5.text.k1, bf16[4,256,256]{2,1,0:T(8,128)(2,1)S(1)} %get-tuple-element.41.g, ...), custom_call_target="tpu_custom_call" | custom-call | tf_op jit(solution)/shard_map/pallas_call | solution.py:206
  30.1 1.7 %shard_map.71 = (bf16[4,128,256]{2,1,0:T(8,128)(2,1)S(1)}, f32[8,256]{1,0:T(8,128)S(1)}, bf16[2,1168,256]{2,1,0:T(8,128)(2,1)S(1)}) custom-call(f32[2]{0:T(128)S(1)} %pad_maximum_fusion.tb, bf16[1152,256]{1,0:T(8,128)(2,1)S(1)} %copy-done, bf16[1152,256]{1,0:T(8,128)(2,1)S(1)} %collective-permute-done.i1, bf16[1152,256]{1,0:T(8,128)(2,1)S(1)} %collective-permute-done.1.i2, ...), custom_call_target="tpu_custom_call" | custom-call | tf_op jit(solution)/shard_map/pallas_call | solution.py:206
  31.8 1.3 %shard_map.72 = bf16[1152,128]{1,0:T(8,128)(2,1)S(1)} custom-call(f32[2]{0:T(128)S(1)} %pad_maximum_fusion.tb, bf16[1152,256]{1,0:T(8,128)(2,1)S(1)} %copy-done, bf16[1152,256]{1,0:T(8,128)(2,1)S(1)} %collective-permute-done.i1, bf16[1152,256]{1,0:T(8,128)(2,1)S(1)} %collective-permute-done.1.i2, bf16[1152,256]{1,0:T(8,128)(2,1)S(1)} %collective-permute-done.2.i3, ...), custom_call_target="tpu_custom_call" | custom-call | tf_op jit(solution)/shard_map/pallas_call | solution.py:206
  33.1 1.0 %collective-permute-start.8 = (bf16[1152,128]{1,0:T(8,128)(2,1)S(1)}, bf16[1152,128]{1,0:T(8,128)(2,1)S(1)}, u32[]{:S(2)}, u32[]{:S(2)}) collective-permute-start(bf16[1152,128]{1,0:T(8,128)(2,1)S(1)} %shard_map.72), channel_id=1, source_target_pairs={{0,4},{1,5},{2,6},{3,7},{4,0},{5,1},{6,2},{7,3},{8,12},{9,13},{10,... | collective-permute-start | bytes 884744 | tf_op jit(solution)/shard_map/ppermute | solution.py:28
  34.1 1.3 %shard_map.74.part = f32[2,1152,256]{2,1,0:T(8,128)S(1)} custom-call(s32[5]{0:T(128)S(1)} %stack.26.later, bf16[2,1152,256]{2,1,0:T(8,128)(2,1)S(1)} %get-tuple-element.40.kept, bf16[1152,128]{1,0:T(8,128)(2,1)S(1)} %collective-permute-done.5.text.k1, bf16[4,256,256]{2,1,0:T(8,128)(2,1)S(1)} %get-tuple-element.41.g, ...), custom_call_target="tpu_custom_call" | custom-call | tf_op jit(solution)/shard_map/pallas_call | solution.py:206
  36.9 0.9 %shard_map.75 = bf16[1168,256]{1,0:T(8,128)(2,1)S(1)} custom-call(f32[2]{0:T(128)S(1)} %pad_maximum_fusion.tb, bf16[1152,128]{1,0:T(8,128)(2,1)S(1)} %collective-permute-done.7.text, f32[2,1152,256]{2,1,0:T(8,128)S(1)} %shard_map.74.part, bf16[4,128,256]{2,1,0:T(8,128)(2,1)S(1)} %get-tuple-element.44.grad, f32[8,256]{1,0:T(8,128)S(1)} %get-tuple-element.37.l0, ...), custom_call_target="tpu_custom_call" | custom-call | tf_op jit(solution)/shard_map/pallas_call | solution.py:206
  37.8 1.5 %collective-permute-start.12 = (bf16[1168,256]{1,0:T(8,128)(2,1)S(1)}, bf16[1168,256]{1,0:T(8,128)(2,1)S(1)}, u32[]{:S(2)}, u32[]{:S(2)}) collective-permute-start(bf16[1168,256]{1,0:T(8,128)(2,1)S(1)} %shard_map.75), channel_id=1, source_target_pairs={{0,1},{1,0},{2,3},{3,2},{4,5},{5,4},{6,7},{7,6},{8,9},{9,8},{10,11... | collective-permute-start | bytes 1794056 | tf_op jit(solution)/shard_map/ppermute | solution.py:28
  39.4 2.4 %collective-permute-start.10 = (bf16[1152,128]{1,0:T(8,128)(2,1)S(1)}, bf16[1152,128]{1,0:T(8,128)(2,1)S(1)}, u32[]{:S(2)}, u32[]{:S(2)}) collective-permute-start(bf16[1152,128]{1,0:T(8,128)(2,1)S(1)} %shard_map.73), channel_id=1, source_target_pairs={{0,24},{1,25},{2,26},{3,27},{4,28},{5,29},{6,30},{7,31},{8,0},{9,1... | collective-permute-start | bytes 884744 | tf_op jit(solution)/shard_map/ppermute | solution.py:28
  41.7 0.9 %collective-permute-done.8.returned.r2 = bf16[1152,128]{1,0:T(8,128)(2,1)S(1)} collective-permute-done((bf16[1152,128]{1,0:T(8,128)(2,1)S(1)}, bf16[1152,128]{1,0:T(8,128)(2,1)S(1)}, u32[]{:S(2)}, u32[]{:S(2)}) %collective-permute-start.8) | collective-permute-done | bytes 294944 | tf_op jit(solution)/shard_map/ppermute | solution.py:28
  43.2 2.4 %collective-permute-start.11 = (bf16[1152,128]{1,0:T(8,128)(2,1)S(1)}, bf16[1152,128]{1,0:T(8,128)(2,1)S(1)}, u32[]{:S(2)}, u32[]{:S(2)}) collective-permute-start(bf16[1152,128]{1,0:T(8,128)(2,1)S(1)} %shard_map.76), channel_id=1, source_target_pairs={{0,24},{1,25},{2,26},{3,27},{4,28},{5,29},{6,30},{7,31},{8,0},{9,1... | collective-permute-start | bytes 884744 | tf_op jit(solution)/shard_map/ppermute | solution.py:28
  45.7 3.4 %collective-permute-done.10.p1 = bf16[1152,128]{1,0:T(8,128)(2,1)S(1)} collective-permute-done((bf16[1152,128]{1,0:T(8,128)(2,1)S(1)}, bf16[1152,128]{1,0:T(8,128)(2,1)S(1)}, u32[]{:S(2)}, u32[]{:S(2)}) %collective-permute-start.10) | collective-permute-done | bytes 294944 | tf_op jit(solution)/shard_map/ppermute | solution.py:28
  49.9 3.8 %collective-permute-done.11.p2 = bf16[1152,128]{1,0:T(8,128)(2,1)S(1)} collective-permute-done((bf16[1152,128]{1,0:T(8,128)(2,1)S(1)}, bf16[1152,128]{1,0:T(8,128)(2,1)S(1)}, u32[]{:S(2)}, u32[]{:S(2)}) %collective-permute-start.11) | collective-permute-done | bytes 294944 | tf_op jit(solution)/shard_map/ppermute | solution.py:28
  53.7 2.0 %shard_map.78 = (f32[1152,256]{1,0:T(8,128)}, f32[1,256]{1,0:T(1,128)}, f32[1152,256]{1,0:T(8,128)}) custom-call(s32[5]{0:T(128)S(1)} %stack.26.later, f32[1152,256]{1,0:T(8,128)S(1)} %get-tuple-element.36.grad_t, bf16[1152,128]{1,0:T(8,128)(2,1)S(1)} %collective-permute-done.6.returned.r1, bf16[1152,128]{1,0:T(8,128)(2,1)S(1)} %collective-permute-done.8.returned.r2, ...), custom_call_target="tpu_custom_call" | custom-call | tf_op jit(solution)/shard_map/pallas_call | solution.py:206
  (25 shorter events, 3.7 us)
Async XLA Ops:
  0.6 21.4 %copy-start = (bf16[1152,256]{1,0:T(8,128)(2,1)S(1)}, bf16[1152,256]{1,0:T(8,128)(2,1)}, u32[]{:S(2)}) copy-start(bf16[1152,256]{1,0:T(8,128)(2,1)} %i0.7) | copy-start | bytes 1769476
  0.6 1.1 %copy-start.1 = (bf16[1152,256]{1,0:T(8,128)(2,1)S(1)}, bf16[1152,256]{1,0:T(8,128)(2,1)}, u32[]{:S(2)}) copy-start(bf16[1152,256]{1,0:T(8,128)(2,1)} %text.3) | copy-start | bytes 1769476
  1.8 20.2 %copy-start.2 = (bf16[1152,256]{1,0:T(8,128)(2,1)S(1)}, bf16[1152,256]{1,0:T(8,128)(2,1)}, u32[]{:S(2)}) copy-start(bf16[1152,256]{1,0:T(8,128)(2,1)} %text.3) | copy-start | bytes 1769476
  1.9 12.9 %collective-permute-start.3 = (bf16[1152,128]{1,0:T(8,128)(2,1)S(1)}, bf16[1152,128]{1,0:T(8,128)(2,1)S(1)}, u32[]{:S(2)}, u32[]{:S(2)}) collective-permute-start(bf16[1152,128]{1,0:T(8,128)(2,1)S(1)} %get-tuple-element.34), channel_id=1, source_target_pairs={{0,8},{1,9},{2,10},{3,11},{4,12},{5,13},{6,14},{7,15},{8,16},{9,17... | collective-permute-start | bytes 884744 | tf_op jit(solution)/shard_map/ppermute | solution.py:28
  5.0 15.0 %collective-permute-start.1 = (bf16[1152,256]{1,0:T(8,128)(2,1)}, bf16[1152,256]{1,0:T(8,128)(2,1)S(1)}, u32[]{:S(2)}, u32[]{:S(2)}) collective-permute-start(bf16[1152,256]{1,0:T(8,128)(2,1)} %i0.7), channel_id=1, source_target_pairs={{0,1},{1,0},{2,3},{3,2},{4,5},{5,4},{6,7},{7,6},{8,9},{9,8},{10,11... | collective-permute-start | bytes 1769480 | tf_op jit(solution)/shard_map/ppermute | solution.py:28
  6.4 15.6 %collective-permute-start = (bf16[1152,256]{1,0:T(8,128)(2,1)}, bf16[1152,256]{1,0:T(8,128)(2,1)S(1)}, u32[]{:S(2)}, u32[]{:S(2)}) collective-permute-start(bf16[1152,256]{1,0:T(8,128)(2,1)} %i0.7), channel_id=1, source_target_pairs={{0,2},{1,3},{2,0},{3,1},{4,6},{5,7},{6,4},{7,5},{8,10},{9,11},{10,... | collective-permute-start | bytes 1769480 | tf_op jit(solution)/shard_map/ppermute | solution.py:28
  6.4 13.9 %collective-permute-start.4 = (bf16[1152,128]{1,0:T(8,128)(2,1)S(1)}, bf16[1152,128]{1,0:T(8,128)(2,1)S(1)}, u32[]{:S(2)}, u32[]{:S(2)}) collective-permute-start(bf16[1152,128]{1,0:T(8,128)(2,1)S(1)} %get-tuple-element.35), channel_id=1, source_target_pairs={{0,8},{1,9},{2,10},{3,11},{4,12},{5,13},{6,14},{7,15},{8,16},{9,17... | collective-permute-start | bytes 884744 | tf_op jit(solution)/shard_map/ppermute | solution.py:28
  14.8 10.4 %collective-permute-start.5 = (bf16[1152,128]{1,0:T(8,128)(2,1)S(1)}, bf16[1152,128]{1,0:T(8,128)(2,1)S(1)}, u32[]{:S(2)}, u32[]{:S(2)}) collective-permute-start(bf16[1152,128]{1,0:T(8,128)(2,1)S(1)} %broadcast_select_fusion.1), channel_id=1, source_target_pairs={{0,4},{1,5},{2,6},{3,7},{4,0},{5,1},{6,2},{7,3},{8,12},{9,13},{10,... | collective-permute-start | bytes 884744 | tf_op jit(solution)/shard_map/ppermute | solution.py:28
  20.0 2.1 %collective-permute-start.2 = (bf16[1152,256]{1,0:T(8,128)(2,1)S(1)}, bf16[1152,256]{1,0:T(8,128)(2,1)S(1)}, u32[]{:S(2)}, u32[]{:S(2)}) collective-permute-start(bf16[1152,256]{1,0:T(8,128)(2,1)S(1)} %collective-permute-done.1.i2), channel_id=1, source_target_pairs={{0,2},{1,3},{2,0},{3,1},{4,6},{5,7},{6,4},{7,5},{8,10},{9,11},{10,... | collective-permute-start | bytes 1769480 | tf_op jit(solution)/shard_map/ppermute | solution.py:28
  20.3 9.7 %collective-permute-start.7 = (bf16[1152,128]{1,0:T(8,128)(2,1)S(1)}, bf16[1152,128]{1,0:T(8,128)(2,1)S(1)}, u32[]{:S(2)}, u32[]{:S(2)}) collective-permute-start(bf16[1152,128]{1,0:T(8,128)(2,1)S(1)} %broadcast_select_fusion), channel_id=1, source_target_pairs={{0,4},{1,5},{2,6},{3,7},{4,0},{5,1},{6,2},{7,3},{8,12},{9,13},{10,... | collective-permute-start | bytes 884744 | tf_op jit(solution)/shard_map/ppermute | solution.py:28
  27.2 9.1 %collective-permute-start.6 = (bf16[1152,128]{1,0:T(8,128)(2,1)S(1)}, bf16[1152,128]{1,0:T(8,128)(2,1)S(1)}, u32[]{:S(2)}, u32[]{:S(2)}) collective-permute-start(bf16[1152,128]{1,0:T(8,128)(2,1)S(1)} %get-tuple-element.39), channel_id=1, source_target_pairs={{0,4},{1,5},{2,6},{3,7},{4,0},{5,1},{6,2},{7,3},{8,12},{9,13},{10,... | collective-permute-start | bytes 884744 | tf_op jit(solution)/shard_map/ppermute | solution.py:28
  31.7 5.2 %collective-permute-start.9 = (bf16[2,1168,256]{2,1,0:T(8,128)(2,1)S(1)}, bf16[2,1168,256]{2,1,0:T(8,128)(2,1)S(1)}, u32[]{:S(2)}, u32[]{:S(2)}) collective-permute-start(bf16[2,1168,256]{2,1,0:T(8,128)(2,1)S(1)} %get-tuple-element.50), channel_id=1, source_target_pairs={{0,2},{1,3},{2,0},{3,1},{4,6},{5,7},{6,4},{7,5},{8,10},{9,11},{10,... | collective-permute-start | bytes 3588104 | tf_op jit(solution)/shard_map/ppermute | solution.py:28
  33.1 9.5 %collective-permute-start.8 = (bf16[1152,128]{1,0:T(8,128)(2,1)S(1)}, bf16[1152,128]{1,0:T(8,128)(2,1)S(1)}, u32[]{:S(2)}, u32[]{:S(2)}) collective-permute-start(bf16[1152,128]{1,0:T(8,128)(2,1)S(1)} %shard_map.72), channel_id=1, source_target_pairs={{0,4},{1,5},{2,6},{3,7},{4,0},{5,1},{6,2},{7,3},{8,12},{9,13},{10,... | collective-permute-start | bytes 884744 | tf_op jit(solution)/shard_map/ppermute | solution.py:28
  37.8 15.9 %collective-permute-start.12 = (bf16[1168,256]{1,0:T(8,128)(2,1)S(1)}, bf16[1168,256]{1,0:T(8,128)(2,1)S(1)}, u32[]{:S(2)}, u32[]{:S(2)}) collective-permute-start(bf16[1168,256]{1,0:T(8,128)(2,1)S(1)} %shard_map.75), channel_id=1, source_target_pairs={{0,1},{1,0},{2,3},{3,2},{4,5},{5,4},{6,7},{7,6},{8,9},{9,8},{10,11... | collective-permute-start | bytes 1794056 | tf_op jit(solution)/shard_map/ppermute | solution.py:28
  39.4 9.7 %collective-permute-start.10 = (bf16[1152,128]{1,0:T(8,128)(2,1)S(1)}, bf16[1152,128]{1,0:T(8,128)(2,1)S(1)}, u32[]{:S(2)}, u32[]{:S(2)}) collective-permute-start(bf16[1152,128]{1,0:T(8,128)(2,1)S(1)} %shard_map.73), channel_id=1, source_target_pairs={{0,24},{1,25},{2,26},{3,27},{4,28},{5,29},{6,30},{7,31},{8,0},{9,1... | collective-permute-start | bytes 884744 | tf_op jit(solution)/shard_map/ppermute | solution.py:28
  43.2 10.4 %collective-permute-start.11 = (bf16[1152,128]{1,0:T(8,128)(2,1)S(1)}, bf16[1152,128]{1,0:T(8,128)(2,1)S(1)}, u32[]{:S(2)}, u32[]{:S(2)}) collective-permute-start(bf16[1152,128]{1,0:T(8,128)(2,1)S(1)} %shard_map.76), channel_id=1, source_target_pairs={{0,24},{1,25},{2,26},{3,27},{4,28},{5,29},{6,30},{7,31},{8,0},{9,1... | collective-permute-start | bytes 884744 | tf_op jit(solution)/shard_map/ppermute | solution.py:28

commit v4 on v3

--- a/solution.py
+++ b/solution.py
@@ -73,7 +73,10 @@
         out[d : d + TILE] = (tb[0] * total).astype(jnp.bfloat16)
 
 
-def partner_kernel(tb, i0, i1, i2, i3, text, grad_x, grad, loss):
+def partner_kernel(tb, i0, i1, i2, i3, upper, lower, grad_x, grad, loss, text):
+    cut = upper.shape[0]
+    text[:cut] = upper[...]
+    text[cut:] = lower[...]
     scores(tb, (i0, i1, i2, i3), text[...].T, grad, loss)
     text_side(tb, (i0, i1, i2, i3), grad, grad_x)
 
@@ -82,15 +85,18 @@
     text_side(tb, (i0, i1, i2, i3), grad, grad_x)
 
 
-def own_kernel(tb, later, i0, i1, i2, i3, text, m1, m2, grad_t, grad_m1, grad_m2, grad, loss, kept, turned, masked):
+def own_kernel(tb, later, i0, i1, i2, i3, text, m1a, m1b, m2, grad_m1, grad_m2, grad, loss, kept, turned, masked):
     temper = tb[0]
     rows = text.shape[1]
     half = rows // 2
     kept[0] = text[...]
-    kept[1, :, :half] = m1[...]
+    cut = m1a.shape[0]
+    kept[1, :cut, :half] = m1a[...]
+    kept[1, cut:, :half] = m1b[...]
     kept[1, :, half:] = m2[...]
     turned[0] = text[...].T
-    turned[1, :half] = m1[...].T
+    turned[1, :half, :cut] = m1a[...].T
+    turned[1, :half, cut:] = m1b[...].T
     turned[1, half:] = m2[...].T
     images = (i0, i1, i2, i3)
     for r, image in enumerate(images):
@@ -103,24 +109,31 @@
         g = s.astype(jnp.bfloat16)
         grad[r] = g
         loss[r : r + 1] = soft
-        masked[0, r] = jnp.where(same == 1, g, jnp.zeros_like(g))
-        masked[1, r] = jnp.where(same == 1, jnp.zeros_like(g), g)
+        masked[r] = jnp.where(same == 1, jnp.zeros_like(g), g)
     for d in range(0, text.shape[0], TILE):
-        total = dot(i0[d : d + TILE], masked[0, 0], NT)
-        for r in (1, 2, 3):
-            total = total + dot(images[r][d : d + TILE], masked[0, r], NT)
-        grad_t[d : d + TILE] = temper * total
-        total = dot(i1[d : d + TILE], masked[1, 1], NT)
+        total = dot(i1[d : d + TILE], masked[1], NT)
         for r in (2, 3):
-            total = total + dot(images[r][d : d + TILE], masked[1, r], NT)
+            total = total + dot(images[r][d : d + TILE], masked[r], NT)
         total = temper * total
         grad_m1[d : d + TILE] = total[:, :half]
         grad_m2[d : d + TILE] = total[:, half:]
 
 
-def halves_kernel(text, first, second):
-    half = first.shape[1]
-    first[...] = text[:, :half]
+def own_text_kernel(tb, later, i0, i1, i2, i3, grad, grad_t, masked):
+    images = (i0, i1, i2, i3)
+    for r in (1, 2, 3):
+        masked[r] = jnp.where(later[r] == 1, grad[r], jnp.zeros(grad.shape[1:], grad.dtype))
+    for d in range(0, grad_t.shape[0], TILE):
+        total = dot(i0[d : d + TILE], grad[0], NT)
+        for r in (1, 2, 3):
+            total = total + dot(images[r][d : d + TILE], masked[r], NT)
+        grad_t[d : d + TILE] = tb[0] * total
+
+
+def halves_kernel(text, upper, lower, second):
+    half, cut = second.shape[1], upper.shape[0]
+    upper[...] = text[:cut, :half]
+    lower[...] = text[cut:, :half]
     second[...] = text[:, half:]
 
 
@@ -155,16 +168,17 @@
 def joined_kernel(tb, text, part, grad, l0, l1, l2, came, out):
     width = text.shape[0]
     for d in range(0, width, TILE):
-        total = tb[0] * (part[1, d : d + TILE] + dot(text[d : d + TILE], grad[2], NN))
+        total = tb[0] * (part[2, d : d + TILE] + dot(text[d : d + TILE], grad[2], NN))
         out[d : d + TILE] = (total + came[1, d : d + TILE].astype(jnp.float32)).astype(jnp.bfloat16)
     loss = l0[2:3] + l1[2:3] + l2[2:3] + unpacked_loss(came[1, width:])
     out[width:] = packed_loss(loss, (EXTRA, out.shape[1]))
 
 
-def home_kernel(tb, text, part, grad, l0, l1, l2, came, out, loss):
-    width = text.shape[0]
+def home_kernel(tb, later, kept, x1, x2, g, g1, g2, l0, l1, l2, came, out, loss):
+    width = x2.shape[0]
     for d in range(0, width, TILE):
-        total = tb[0] * (part[0, d : d + TILE] + dot(text[d : d + TILE], grad[0], NN))
+        total = dot(kept[1 - later[0], d : d + TILE], g[0], NN) + dot(x1[d : d + TILE], g1[0], NN)
+        total = tb[0] * (total + dot(x2[d : d + TILE], g2[0], NN))
         out[d : d + TILE] = total + came[0, d : d + TILE].astype(jnp.float32)
     loss[0:1] = l0[0:1] + l1[0:1] + l2[0:1] + unpacked_loss(came[0, width:])
 
@@ -225,39 +239,40 @@
     unit = 2 * rows * rows * width
 
     high = place >= SIDE
-    t1, t2 = call(halves_kernel, (sds((width, half), bf16),) * 2, (text,))
-    sent, t1, t2 = lax.optimization_barrier((image, t1, t2))
-    m1 = moved(t1, forward)
+    cut = width // 256 * 128
+    upper, lower = sds((cut, half), bf16), sds((width - cut, half), bf16)
+    t1a, t1b, t2 = call(halves_kernel, (upper, lower, sds((width, half), bf16)), (text,))
+    sent, t1a, t1b, t2 = lax.optimization_barrier((image, t1a, t1b, t2))
+    m1a = moved(t1a, forward)
+    m1b = moved(t1b, forward)
     m2 = moved(t2, forward)
     image_p = moved(sent, swap(PAIR))
     image_c = moved(sent, swap(CORE))
-    x1 = moved(jnp.where(high, m1, t1), swap(SIDE))
+    x1a = moved(jnp.where(high, m1a, t1a), swap(SIDE))
+    x1b = moved(jnp.where(high, m1b, t1b), swap(SIDE))
     x2 = moved(jnp.where(high, m2, t2), swap(SIDE))
     image_pc = moved(image_p, swap(CORE))
     images = (image, image_c, image_p, image_pc)
 
-    grad_t, grad_m1, grad_m2, g0, l0, kept = call(
+    grad_m1, grad_m2, g0, l0, kept = call(
         own_kernel,
         (
-            sds((width, rows), f32),
             sds((width, half), f32),
             sds((width, half), f32),
             sds((4, rows, rows), bf16),
             sds((8, rows), f32),
             sds((2, width, rows), bf16),
         ),
-        (tb, later, *images, text, m1, m2),
-        scratch=(pltpu.VMEM((2, rows, width), bf16), pltpu.VMEM((2, 4, rows, rows), bf16)),
+        (tb, later, *images, text, m1a, m1b, m2),
+        scratch=(pltpu.VMEM((2, rows, width), bf16), pltpu.VMEM((4, rows, rows), bf16)),
     )
-    x1, _ = lax.optimization_barrier((x1, l0))
+    x1a, x1b, _ = lax.optimization_barrier((x1a, x1b, l0))
     scored = (sds((4, half, rows), bf16), sds((8, rows), f32))
-    grad_x1, g1, l1 = call(partner_kernel, (sds((width, half), bf16), *scored), (tb, *images, x1))
-    part = call(functools.partial(early_kernel, (1, 3)), sds((2, width, rows), f32), (later, kept, x1, g0, g1))
+    grad_x1, g1, l1, x1 = call(partner_kernel, (sds((width, half), bf16), *scored, sds((width, half), bf16)), (tb, *images, x1a, x1b))
+    part = call(functools.partial(early_kernel, (1, 3, 2)), sds((3, width, rows), f32), (later, kept, x1, g0, g1))
     g2, l2, away = call(away_kernel, (*scored, sds((2, width + EXTRA, rows), bf16)), (tb, *images, x2, part, l0, l1))
     came = moved(away, swap(CORE))
     grad_x2 = call(text_kernel, sds((width, half), bf16), (tb, *images, g2))
-    _, held1 = lax.optimization_barrier((grad_x2, g1))
-    part = call(functools.partial(early_kernel, (0, 2)), sds((2, width, rows), f32), (later, kept, x1, g0, held1))
     r1 = moved(grad_x1, swap(SIDE))
     r2 = moved(grad_x2, swap(SIDE))
 
@@ -268,9 +283,17 @@
     other = moved(joined, swap(PAIR))
     older1, grad_m2, _ = lax.optimization_barrier((older1, grad_m2, joined))
     past1 = moved(older1, back)
-    past2 = moved(call(older_kernel, older, (later, grad_m2, r2), flops=20 * unit), back)
+    older2 = call(older_kernel, older, (later, grad_m2, r2), flops=20 * unit)
+    past2 = moved(older2, back)
+    _, late0 = lax.optimization_barrier((older2, g0))
+    grad_t = call(
+        own_text_kernel,
+        sds((width, rows), f32),
+        (tb, later, *images, late0),
+        scratch=(pltpu.VMEM((4, rows, rows), bf16),),
+    )
     _, late = lax.optimization_barrier((past1, l2))
-    rest = (tb, x2, part, g2, l0, l1, late, came)
+    rest = (tb, later, kept, x1, x2, g0, g1, g2, l0, l1, late, came)
     home, home_loss = call(home_kernel, (sds((width, rows), f32), sds((8, rows), f32)), rest, flops=5 * unit)
     parts = 4
     grad_image, losses, grad_text = call(

time: 55.9 us -> 55.3 us (0.989)
  waiting for transfers between devices: 17.9 us -> 14.7 us
  starting transfers between devices: 18.5 us -> 20.9 us
    ppermute x13 -> x15, waiting for transfers between devices: 17.9 us -> 14.7 us  [moved(): return lax.ppermute(block, AXES, [(i, target(i, n)) for i in range(n)])]
    ppermute x13 -> x15, starting transfers between devices: 18.5 us -> 20.9 us  [moved(): return lax.ppermute(block, AXES, [(i, target(i, n)) for i in range(n)])]
  transfers between devices with their start and end apart: 13 -> 15, of which waited for: 7 -> 8; matrix products, arithmetic and copies ran while one was open for 0% -> 0% of each run, Pallas kernels for 25% -> 25%
where the time goes in v4:
time: 55.3 us; the launch traced here: 55.1 us
  starting transfers between devices  20.9 us (38%)
  Pallas kernels  16.1 us (29%)
  waiting for transfers between devices  14.7 us (27%)
  between operations  2.1 us (4%)
  local copies, waits for them, and re-layouts  1.23 us (2%)
    ppermute x15, starting transfers between devices, moved(): return lax.ppermute(block, AXES, [(i, target(i, n)) for i in range(n)])  20.9 us
    pallas_call x12, Pallas kernels, call(): pl.pallas_call(kernel, out_shape=out_shape, in_specs=[pl.BlockSpec(memory...  16.1 us
    ppermute x15, waiting for transfers between devices, moved(): return lax.ppermute(block, AXES, [(i, target(i, n)) for i in range(n)])  14.7 us
    unnamed x6, local copies, waits for them, and re-layouts  1.13 us
  transfers between devices with their start and end apart: 15, of which 8 were waited for; matrix products, arithmetic and copies ran while one was open for 0% of the time, Pallas kernels for 25%

profile of v4, /device:TPU:0, one launch (start us, length us, event | category | flops | bytes accessed | tf_op | source)
XLA Modules:
  0.0 55.1 jit_solution(2957970431736175621)
XLA Ops:
  1.9 3.1 %collective-permute-start.3 = (bf16[512,128]{1,0:T(8,128)(2,1)S(1)}, bf16[512,128]{1,0:T(8,128)(2,1)S(1)}, u32[]{:S(2)}, u32[]{:S(2)}) collective-permute-start(bf16[512,128]{1,0:T(8,128)(2,1)S(1)} %get-tuple-element.38), channel_id=1, source_target_pairs={{0,8},{1,9},{2,10},{3,11},{4,12},{5,13},{6,14},{7,15},{8,16},{9,17... | collective-permute-start | bytes 393224 | tf_op jit(solution)/shard_map/ppermute | solution.py:28
  5.0 1.5 %collective-permute-start.1 = (bf16[1152,256]{1,0:T(8,128)(2,1)}, bf16[1152,256]{1,0:T(8,128)(2,1)S(1)}, u32[]{:S(2)}, u32[]{:S(2)}) collective-permute-start(bf16[1152,256]{1,0:T(8,128)(2,1)} %i0.9), channel_id=1, source_target_pairs={{0,1},{1,0},{2,3},{3,2},{4,5},{5,4},{6,7},{7,6},{8,9},{9,8},{10,11... | collective-permute-start | bytes 1769480 | tf_op jit(solution)/shard_map/ppermute | solution.py:28
  6.4 1.6 %collective-permute-start.4 = (bf16[640,128]{1,0:T(8,128)(2,1)S(1)}, bf16[640,128]{1,0:T(8,128)(2,1)S(1)}, u32[]{:S(2)}, u32[]{:S(2)}) collective-permute-start(bf16[640,128]{1,0:T(8,128)(2,1)S(1)} %get-tuple-element.39), channel_id=1, source_target_pairs={{0,8},{1,9},{2,10},{3,11},{4,12},{5,13},{6,14},{7,15},{8,16},{9,17... | collective-permute-start | bytes 491528 | tf_op jit(solution)/shard_map/ppermute | solution.py:28
  8.0 1.6 %collective-permute-start.5 = (bf16[1152,128]{1,0:T(8,128)(2,1)S(1)}, bf16[1152,128]{1,0:T(8,128)(2,1)S(1)}, u32[]{:S(2)}, u32[]{:S(2)}) collective-permute-start(bf16[1152,128]{1,0:T(8,128)(2,1)S(1)} %get-tuple-element.40), channel_id=1, source_target_pairs={{0,8},{1,9},{2,10},{3,11},{4,12},{5,13},{6,14},{7,15},{8,16},{9,17... | collective-permute-start | bytes 884744 | tf_op jit(solution)/shard_map/ppermute | solution.py:28
  11.0 1.6 %collective-permute-start.6 = (bf16[512,128]{1,0:T(8,128)(2,1)S(1)}, bf16[512,128]{1,0:T(8,128)(2,1)S(1)}, u32[]{:S(2)}, u32[]{:S(2)}) collective-permute-start(bf16[512,128]{1,0:T(8,128)(2,1)S(1)} %broadcast_select_fusion.2), channel_id=1, source_target_pairs={{0,4},{1,5},{2,6},{3,7},{4,0},{5,1},{6,2},{7,3},{8,12},{9,13},{10,... | collective-permute-start | bytes 393224 | tf_op jit(solution)/shard_map/ppermute | solution.py:28
  12.6 2.6 %collective-permute-done.4.m1b = bf16[640,128]{1,0:T(8,128)(2,1)S(1)} collective-permute-done((bf16[640,128]{1,0:T(8,128)(2,1)S(1)}, bf16[640,128]{1,0:T(8,128)(2,1)S(1)}, u32[]{:S(2)}, u32[]{:S(2)}) %collective-permute-start.4) | collective-permute-done | bytes 163872 | tf_op jit(solution)/shard_map/ppermute | solution.py:28
  15.3 1.6 %collective-permute-start.7 = (bf16[640,128]{1,0:T(8,128)(2,1)S(1)}, bf16[640,128]{1,0:T(8,128)(2,1)S(1)}, u32[]{:S(2)}, u32[]{:S(2)}) collective-permute-start(bf16[640,128]{1,0:T(8,128)(2,1)S(1)} %broadcast_select_fusion.1), channel_id=1, source_target_pairs={{0,4},{1,5},{2,6},{3,7},{4,0},{5,1},{6,2},{7,3},{8,12},{9,13},{10,... | collective-permute-start | bytes 491528 | tf_op jit(solution)/shard_map/ppermute | solution.py:28
  16.8 3.1 %collective-permute-done.1.i2 = bf16[1152,256]{1,0:T(8,128)(2,1)S(1)} collective-permute-done((bf16[1152,256]{1,0:T(8,128)(2,1)}, bf16[1152,256]{1,0:T(8,128)(2,1)S(1)}, u32[]{:S(2)}, u32[]{:S(2)}) %collective-permute-start.1) | collective-permute-done | bytes 589856 | tf_op jit(solution)/shard_map/ppermute | solution.py:28
  20.0 1.2 %collective-permute-done.5.m2 = bf16[1152,128]{1,0:T(8,128)(2,1)S(1)} collective-permute-done((bf16[1152,128]{1,0:T(8,128)(2,1)S(1)}, bf16[1152,128]{1,0:T(8,128)(2,1)S(1)}, u32[]{:S(2)}, u32[]{:S(2)}) %collective-permute-start.5) | collective-permute-done | bytes 294944 | tf_op jit(solution)/shard_map/ppermute | solution.py:28
  21.2 1.6 %collective-permute-start.9 = (bf16[1152,128]{1,0:T(8,128)(2,1)S(1)}, bf16[1152,128]{1,0:T(8,128)(2,1)S(1)}, u32[]{:S(2)}, u32[]{:S(2)}) collective-permute-start(bf16[1152,128]{1,0:T(8,128)(2,1)S(1)} %broadcast_select_fusion), channel_id=1, source_target_pairs={{0,4},{1,5},{2,6},{3,7},{4,0},{5,1},{6,2},{7,3},{8,12},{9,13},{10,... | collective-permute-start | bytes 884744 | tf_op jit(solution)/shard_map/ppermute | solution.py:28
  22.9 2.7 %shard_map.68 = (f32[1152,128]{1,0:T(8,128)S(1)}, f32[1152,128]{1,0:T(8,128)S(1)}, bf16[4,256,256]{2,1,0:T(8,128)(2,1)S(1)}, f32[8,256]{1,0:T(8,128)S(1)}, bf16[2,1152,256]{2,1,0:T(8,128)(2,1)S(1)}) custom-call(f32[2]{0:T(128)S(1)} %pad_maximum_fusion.tb, s32[5]{0:T(128)S(1)} %stack.26.later, bf16[1152,256]{1,0:T(8,128)(2,1)S(1)} %copy-done, ...), custom_call_target="tpu_custom_call" | custom-call | tf_op jit(solution)/shard_map/pallas_call | solution.py:220
  25.6 2.0 %shard_map.69 = (bf16[1152,128]{1,0:T(8,128)(2,1)S(1)}, bf16[4,128,256]{2,1,0:T(8,128)(2,1)S(1)}, f32[8,256]{1,0:T(8,128)S(1)}, bf16[1152,128]{1,0:T(8,128)(2,1)S(1)}) custom-call(f32[2]{0:T(128)S(1)} %pad_maximum_fusion.tb, bf16[1152,256]{1,0:T(8,128)(2,1)S(1)} %copy-done, bf16[1152,256]{1,0:T(8,128)(2,1)S(1)} %collective-permute-done.i1, ...), custom_call_target="tpu_custom_call" | custom-call | tf_op jit(solution)/shard_map/pallas_call | solution.py:220
  28.3 1.6 %shard_map.71.part = f32[3,1152,256]{2,1,0:T(8,128)S(1)} custom-call(s32[5]{0:T(128)S(1)} %stack.26.later, bf16[2,1152,256]{2,1,0:T(8,128)(2,1)S(1)} %get-tuple-element.47.kept, bf16[1152,128]{1,0:T(8,128)(2,1)S(1)} %get-tuple-element.48.k1.x1, bf16[4,256,256]{2,1,0:T(8,128)(2,1)S(1)} %get-tuple-element.57.g.grad, bf16[4,128,256]{2,1,0:T(8,128)(2,1)S(1)} %get-tuple-element.50.g1), custom_call_target="tpu_custom_call" | custom-call | tf_op jit(solution)/shard_map/pallas_call | solution.py:220
  30.0 1.7 %shard_map.72 = (bf16[4,128,256]{2,1,0:T(8,128)(2,1)S(1)}, f32[8,256]{1,0:T(8,128)S(1)}, bf16[2,1168,256]{2,1,0:T(8,128)(2,1)S(1)}) custom-call(f32[2]{0:T(128)S(1)} %pad_maximum_fusion.tb, bf16[1152,256]{1,0:T(8,128)(2,1)S(1)} %copy-done, bf16[1152,256]{1,0:T(8,128)(2,1)S(1)} %collective-permute-done.i1, bf16[1152,256]{1,0:T(8,128)(2,1)S(1)} %collective-permute-done.1.i2, ...), custom_call_target="tpu_custom_call" | custom-call | tf_op jit(solution)/shard_map/pallas_call | solution.py:220
  31.8 1.3 %shard_map.74 = bf16[1152,128]{1,0:T(8,128)(2,1)S(1)} custom-call(f32[2]{0:T(128)S(1)} %pad_maximum_fusion.tb, bf16[1152,256]{1,0:T(8,128)(2,1)S(1)} %copy-done, bf16[1152,256]{1,0:T(8,128)(2,1)S(1)} %collective-permute-done.i1, bf16[1152,256]{1,0:T(8,128)(2,1)S(1)} %collective-permute-done.1.i2, bf16[1152,256]{1,0:T(8,128)(2,1)S(1)} %collective-permute-done.2.i3, ...), custom_call_target="tpu_custom_call" | custom-call | tf_op jit(solution)/shard_map/pallas_call | solution.py:220
  33.1 1.8 %collective-permute-start.11 = (bf16[1152,128]{1,0:T(8,128)(2,1)S(1)}, bf16[1152,128]{1,0:T(8,128)(2,1)S(1)}, u32[]{:S(2)}, u32[]{:S(2)}) collective-permute-start(bf16[1152,128]{1,0:T(8,128)(2,1)S(1)} %shard_map.74), channel_id=1, source_target_pairs={{0,4},{1,5},{2,6},{3,7},{4,0},{5,1},{6,2},{7,3},{8,12},{9,13},{10,... | collective-permute-start | bytes 884744 | tf_op jit(solution)/shard_map/ppermute | solution.py:28
  34.9 1.3 %collective-permute-done.8.returned.r1 = bf16[1152,128]{1,0:T(8,128)(2,1)S(1)} collective-permute-done((bf16[1152,128]{1,0:T(8,128)(2,1)S(1)}, bf16[1152,128]{1,0:T(8,128)(2,1)S(1)}, u32[]{:S(2)}, u32[]{:S(2)}) %collective-permute-start.8) | collective-permute-done | bytes 294944 | tf_op jit(solution)/shard_map/ppermute | solution.py:28
  38.9 2.4 %collective-permute-start.12 = (bf16[1152,128]{1,0:T(8,128)(2,1)S(1)}, bf16[1152,128]{1,0:T(8,128)(2,1)S(1)}, u32[]{:S(2)}, u32[]{:S(2)}) collective-permute-start(bf16[1152,128]{1,0:T(8,128)(2,1)S(1)} %shard_map.70), channel_id=1, source_target_pairs={{0,24},{1,25},{2,26},{3,27},{4,28},{5,29},{6,30},{7,31},{8,0},{9,1... | collective-permute-start | bytes 884744 | tf_op jit(solution)/shard_map/ppermute | solution.py:28
  41.3 1.3 %collective-permute-done.11.returned.r2 = bf16[1152,128]{1,0:T(8,128)(2,1)S(1)} collective-permute-done((bf16[1152,128]{1,0:T(8,128)(2,1)S(1)}, bf16[1152,128]{1,0:T(8,128)(2,1)S(1)}, u32[]{:S(2)}, u32[]{:S(2)}) %collective-permute-start.11) | collective-permute-done | bytes 294944 | tf_op jit(solution)/shard_map/ppermute | solution.py:28
  43.2 2.3 %collective-permute-start.13 = (bf16[1152,128]{1,0:T(8,128)(2,1)S(1)}, bf16[1152,128]{1,0:T(8,128)(2,1)S(1)}, u32[]{:S(2)}, u32[]{:S(2)}) collective-permute-start(bf16[1152,128]{1,0:T(8,128)(2,1)S(1)} %shard_map.75), channel_id=1, source_target_pairs={{0,24},{1,25},{2,26},{3,27},{4,28},{5,29},{6,30},{7,31},{8,0},{9,1... | collective-permute-start | bytes 884744 | tf_op jit(solution)/shard_map/ppermute | solution.py:28
  45.5 1.4 %shard_map.76.grad_t = f32[1152,256]{1,0:T(8,128)S(1)} custom-call(f32[2]{0:T(128)S(1)} %pad_maximum_fusion.tb, s32[5]{0:T(128)S(1)} %stack.26.later, bf16[1152,256]{1,0:T(8,128)(2,1)S(1)} %copy-done, bf16[1152,256]{1,0:T(8,128)(2,1)S(1)} %collective-permute-done.i1, bf16[1152,256]{1,0:T(8,128)(2,1)S(1)} %collective-permute-done.1.i2, ...), custom_call_target="tpu_custom_call" | custom-call | tf_op jit(solution)/shard_map/pallas_call | solution.py:220
  48.1 1.2 %shard_map.77 = (f32[1152,256]{1,0:T(8,128)S(1)}, f32[8,256]{1,0:T(8,128)S(1)}) custom-call(f32[2]{0:T(128)S(1)} %pad_maximum_fusion.tb, s32[5]{0:T(128)S(1)} %stack.26.later, bf16[2,1152,256]{2,1,0:T(8,128)(2,1)S(1)} %get-tuple-element.47.kept, bf16[1152,128]{1,0:T(8,128)(2,1)S(1)} %get-tuple-element.48.k1.x1, ...), custom_call_target="tpu_custom_call" | custom-call | flops 754974720 | tf_op jit(solution)/shard_map/pallas_call | solution.py:220
  49.2 3.8 %collective-permute-done.13.p2 = bf16[1152,128]{1,0:T(8,128)(2,1)S(1)} collective-permute-done((bf16[1152,128]{1,0:T(8,128)(2,1)S(1)}, bf16[1152,128]{1,0:T(8,128)(2,1)S(1)}, u32[]{:S(2)}, u32[]{:S(2)}) %collective-permute-start.13) | collective-permute-done | bytes 294944 | tf_op jit(solution)/shard_map/ppermute | solution.py:28
  53.1 2.0 %shard_map.78 = (f32[1152,256]{1,0:T(8,128)}, f32[1,256]{1,0:T(1,128)}, f32[1152,256]{1,0:T(8,128)}) custom-call(s32[5]{0:T(128)S(1)} %stack.26.later, f32[1152,256]{1,0:T(8,128)S(1)} %shard_map.76.grad_t, bf16[1152,128]{1,0:T(8,128)(2,1)S(1)} %collective-permute-done.8.returned.r1, bf16[1152,128]{1,0:T(8,128)(2,1)S(1)} %collective-permute-done.11.returned.r2, ...), custom_call_target="tpu_custom_call" | custom-call | tf_op jit(solution)/shard_map/pallas_call | solution.py:220
  (30 shorter events, 6.8 us)
Async XLA Ops:
  0.6 22.3 %copy-start = (bf16[1152,256]{1,0:T(8,128)(2,1)S(1)}, bf16[1152,256]{1,0:T(8,128)(2,1)}, u32[]{:S(2)}) copy-start(bf16[1152,256]{1,0:T(8,128)(2,1)} %i0.9) | copy-start | bytes 1769476
  0.6 1.1 %copy-start.1 = (bf16[1152,256]{1,0:T(8,128)(2,1)S(1)}, bf16[1152,256]{1,0:T(8,128)(2,1)}, u32[]{:S(2)}) copy-start(bf16[1152,256]{1,0:T(8,128)(2,1)} %text.3) | copy-start | bytes 1769476
  1.8 21.1 %copy-start.2 = (bf16[1152,256]{1,0:T(8,128)(2,1)S(1)}, bf16[1152,256]{1,0:T(8,128)(2,1)}, u32[]{:S(2)}) copy-start(bf16[1152,256]{1,0:T(8,128)(2,1)} %text.3) | copy-start | bytes 1769476
  1.9 9.1 %collective-permute-start.3 = (bf16[512,128]{1,0:T(8,128)(2,1)S(1)}, bf16[512,128]{1,0:T(8,128)(2,1)S(1)}, u32[]{:S(2)}, u32[]{:S(2)}) collective-permute-start(bf16[512,128]{1,0:T(8,128)(2,1)S(1)} %get-tuple-element.38), channel_id=1, source_target_pairs={{0,8},{1,9},{2,10},{3,11},{4,12},{5,13},{6,14},{7,15},{8,16},{9,17... | collective-permute-start | bytes 393224 | tf_op jit(solution)/shard_map/ppermute | solution.py:28
  5.0 15.0 %collective-permute-start.1 = (bf16[1152,256]{1,0:T(8,128)(2,1)}, bf16[1152,256]{1,0:T(8,128)(2,1)S(1)}, u32[]{:S(2)}, u32[]{:S(2)}) collective-permute-start(bf16[1152,256]{1,0:T(8,128)(2,1)} %i0.9), channel_id=1, source_target_pairs={{0,1},{1,0},{2,3},{3,2},{4,5},{5,4},{6,7},{7,6},{8,9},{9,8},{10,11... | collective-permute-start | bytes 1769480 | tf_op jit(solution)/shard_map/ppermute | solution.py:28
  6.4 16.4 %collective-permute-start = (bf16[1152,256]{1,0:T(8,128)(2,1)}, bf16[1152,256]{1,0:T(8,128)(2,1)S(1)}, u32[]{:S(2)}, u32[]{:S(2)}) collective-permute-start(bf16[1152,256]{1,0:T(8,128)(2,1)} %i0.9), channel_id=1, source_target_pairs={{0,2},{1,3},{2,0},{3,1},{4,6},{5,7},{6,4},{7,5},{8,10},{9,11},{10,... | collective-permute-start | bytes 1769480 | tf_op jit(solution)/shard_map/ppermute | solution.py:28
  6.4 8.8 %collective-permute-start.4 = (bf16[640,128]{1,0:T(8,128)(2,1)S(1)}, bf16[640,128]{1,0:T(8,128)(2,1)S(1)}, u32[]{:S(2)}, u32[]{:S(2)}) collective-permute-start(bf16[640,128]{1,0:T(8,128)(2,1)S(1)} %get-tuple-element.39), channel_id=1, source_target_pairs={{0,8},{1,9},{2,10},{3,11},{4,12},{5,13},{6,14},{7,15},{8,16},{9,17... | collective-permute-start | bytes 491528 | tf_op jit(solution)/shard_map/ppermute | solution.py:28
  8.0 13.2 %collective-permute-start.5 = (bf16[1152,128]{1,0:T(8,128)(2,1)S(1)}, bf16[1152,128]{1,0:T(8,128)(2,1)S(1)}, u32[]{:S(2)}, u32[]{:S(2)}) collective-permute-start(bf16[1152,128]{1,0:T(8,128)(2,1)S(1)} %get-tuple-element.40), channel_id=1, source_target_pairs={{0,8},{1,9},{2,10},{3,11},{4,12},{5,13},{6,14},{7,15},{8,16},{9,17... | collective-permute-start | bytes 884744 | tf_op jit(solution)/shard_map/ppermute | solution.py:28
  11.0 14.6 %collective-permute-start.6 = (bf16[512,128]{1,0:T(8,128)(2,1)S(1)}, bf16[512,128]{1,0:T(8,128)(2,1)S(1)}, u32[]{:S(2)}, u32[]{:S(2)}) collective-permute-start(bf16[512,128]{1,0:T(8,128)(2,1)S(1)} %broadcast_select_fusion.2), channel_id=1, source_target_pairs={{0,4},{1,5},{2,6},{3,7},{4,0},{5,1},{6,2},{7,3},{8,12},{9,13},{10,... | collective-permute-start | bytes 393224 | tf_op jit(solution)/shard_map/ppermute | solution.py:28
  15.3 10.3 %collective-permute-start.7 = (bf16[640,128]{1,0:T(8,128)(2,1)S(1)}, bf16[640,128]{1,0:T(8,128)(2,1)S(1)}, u32[]{:S(2)}, u32[]{:S(2)}) collective-permute-start(bf16[640,128]{1,0:T(8,128)(2,1)S(1)} %broadcast_select_fusion.1), channel_id=1, source_target_pairs={{0,4},{1,5},{2,6},{3,7},{4,0},{5,1},{6,2},{7,3},{8,12},{9,13},{10,... | collective-permute-start | bytes 491528 | tf_op jit(solution)/shard_map/ppermute | solution.py:28
  20.0 2.9 %collective-permute-start.2 = (bf16[1152,256]{1,0:T(8,128)(2,1)S(1)}, bf16[1152,256]{1,0:T(8,128)(2,1)S(1)}, u32[]{:S(2)}, u32[]{:S(2)}) collective-permute-start(bf16[1152,256]{1,0:T(8,128)(2,1)S(1)} %collective-permute-done.1.i2), channel_id=1, source_target_pairs={{0,2},{1,3},{2,0},{3,1},{4,6},{5,7},{6,4},{7,5},{8,10},{9,11},{10,... | collective-permute-start | bytes 1769480 | tf_op jit(solution)/shard_map/ppermute | solution.py:28
  21.2 8.8 %collective-permute-start.9 = (bf16[1152,128]{1,0:T(8,128)(2,1)S(1)}, bf16[1152,128]{1,0:T(8,128)(2,1)S(1)}, u32[]{:S(2)}, u32[]{:S(2)}) collective-permute-start(bf16[1152,128]{1,0:T(8,128)(2,1)S(1)} %broadcast_select_fusion), channel_id=1, source_target_pairs={{0,4},{1,5},{2,6},{3,7},{4,0},{5,1},{6,2},{7,3},{8,12},{9,13},{10,... | collective-permute-start | bytes 884744 | tf_op jit(solution)/shard_map/ppermute | solution.py:28
  27.6 8.6 %collective-permute-start.8 = (bf16[1152,128]{1,0:T(8,128)(2,1)S(1)}, bf16[1152,128]{1,0:T(8,128)(2,1)S(1)}, u32[]{:S(2)}, u32[]{:S(2)}) collective-permute-start(bf16[1152,128]{1,0:T(8,128)(2,1)S(1)} %get-tuple-element.45), channel_id=1, source_target_pairs={{0,4},{1,5},{2,6},{3,7},{4,0},{5,1},{6,2},{7,3},{8,12},{9,13},{10,... | collective-permute-start | bytes 884744 | tf_op jit(solution)/shard_map/ppermute | solution.py:28
  31.7 5.2 %collective-permute-start.10 = (bf16[2,1168,256]{2,1,0:T(8,128)(2,1)S(1)}, bf16[2,1168,256]{2,1,0:T(8,128)(2,1)S(1)}, u32[]{:S(2)}, u32[]{:S(2)}) collective-permute-start(bf16[2,1168,256]{2,1,0:T(8,128)(2,1)S(1)} %get-tuple-element.55), channel_id=1, source_target_pairs={{0,2},{1,3},{2,0},{3,1},{4,6},{5,7},{6,4},{7,5},{8,10},{9,11},{10,... | collective-permute-start | bytes 3588104 | tf_op jit(solution)/shard_map/ppermute | solution.py:28
  33.1 9.5 %collective-permute-start.11 = (bf16[1152,128]{1,0:T(8,128)(2,1)S(1)}, bf16[1152,128]{1,0:T(8,128)(2,1)S(1)}, u32[]{:S(2)}, u32[]{:S(2)}) collective-permute-start(bf16[1152,128]{1,0:T(8,128)(2,1)S(1)} %shard_map.74), channel_id=1, source_target_pairs={{0,4},{1,5},{2,6},{3,7},{4,0},{5,1},{6,2},{7,3},{8,12},{9,13},{10,... | collective-permute-start | bytes 884744 | tf_op jit(solution)/shard_map/ppermute | solution.py:28
  37.8 15.3 %collective-permute-start.14 = (bf16[1168,256]{1,0:T(8,128)(2,1)S(1)}, bf16[1168,256]{1,0:T(8,128)(2,1)S(1)}, u32[]{:S(2)}, u32[]{:S(2)}) collective-permute-start(bf16[1168,256]{1,0:T(8,128)(2,1)S(1)} %shard_map.73), channel_id=1, source_target_pairs={{0,1},{1,0},{2,3},{3,2},{4,5},{5,4},{6,7},{7,6},{8,9},{9,8},{10,11... | collective-permute-start | bytes 1794056 | tf_op jit(solution)/shard_map/ppermute | solution.py:28
  38.9 9.2 %collective-permute-start.12 = (bf16[1152,128]{1,0:T(8,128)(2,1)S(1)}, bf16[1152,128]{1,0:T(8,128)(2,1)S(1)}, u32[]{:S(2)}, u32[]{:S(2)}) collective-permute-start(bf16[1152,128]{1,0:T(8,128)(2,1)S(1)} %shard_map.70), channel_id=1, source_target_pairs={{0,24},{1,25},{2,26},{3,27},{4,28},{5,29},{6,30},{7,31},{8,0},{9,1... | collective-permute-start | bytes 884744 | tf_op jit(solution)/shard_map/ppermute | solution.py:28
  43.2 9.9 %collective-permute-start.13 = (bf16[1152,128]{1,0:T(8,128)(2,1)S(1)}, bf16[1152,128]{1,0:T(8,128)(2,1)S(1)}, u32[]{:S(2)}, u32[]{:S(2)}) collective-permute-start(bf16[1152,128]{1,0:T(8,128)(2,1)S(1)} %shard_map.75), channel_id=1, source_target_pairs={{0,24},{1,25},{2,26},{3,27},{4,28},{5,29},{6,30},{7,31},{8,0},{9,1... | collective-permute-start | bytes 884744 | tf_op jit(solution)/shard_map/ppermute | solution.py:28

commit v5 on v4

--- a/solution.py
+++ b/solution.py
@@ -119,15 +119,19 @@
         grad_m2[d : d + TILE] = total[:, half:]
 
 
-def own_text_kernel(tb, later, i0, i1, i2, i3, grad, grad_t, masked):
+def own_text_kernel(tb, later, i0, i1, i2, i3, grad, r1, r2, first, second, masked):
     images = (i0, i1, i2, i3)
+    half = r1.shape[1]
+    low = later[len(MASKS)] == 0
     for r in (1, 2, 3):
         masked[r] = jnp.where(later[r] == 1, grad[r], jnp.zeros(grad.shape[1:], grad.dtype))
-    for d in range(0, grad_t.shape[0], TILE):
+    for d in range(0, r1.shape[0], TILE):
         total = dot(i0[d : d + TILE], grad[0], NT)
         for r in (1, 2, 3):
             total = total + dot(images[r][d : d + TILE], masked[r], NT)
-        grad_t[d : d + TILE] = tb[0] * total
+        total = tb[0] * total
+        first[d : d + TILE] = total[:, :half] + jnp.where(low, r1[d : d + TILE].astype(jnp.float32), 0.0)
+        second[d : d + TILE] = total[:, half:] + jnp.where(low, r2[d : d + TILE].astype(jnp.float32), 0.0)
 
 
 def halves_kernel(text, upper, lower, second):
@@ -174,13 +178,14 @@
     out[width:] = packed_loss(loss, (EXTRA, out.shape[1]))
 
 
-def home_kernel(tb, later, kept, x1, x2, g, g1, g2, l0, l1, l2, came, out, loss):
+def home_kernel(tb, later, kept, x1, x2, g, g1, g2, l0, l1, l2, came, first, past, out, loss, text):
     width = x2.shape[0]
     for d in range(0, width, TILE):
         total = dot(kept[1 - later[0], d : d + TILE], g[0], NN) + dot(x1[d : d + TILE], g1[0], NN)
         total = tb[0] * (total + dot(x2[d : d + TILE], g2[0], NN))
         out[d : d + TILE] = total + came[0, d : d + TILE].astype(jnp.float32)
     loss[0:1] = l0[0:1] + l1[0:1] + l2[0:1] + unpacked_loss(came[0, width:])
+    text[...] = first[...] + past[...].astype(jnp.float32)
 
 
 def older_kernel(later, grad_m, returned, out):
@@ -188,10 +193,9 @@
     out[...] = (grad_m[...] + jnp.where(high, returned[...].astype(jnp.float32), 0.0)).astype(jnp.bfloat16)
 
 
-def last_kernel(parts, later, grad_t, r1, r2, p1, p2, home, loss, other, grad_image, losses, grad_text, image_buf, loss_buf, text_buf, sems):
+def last_kernel(parts, first, second, past, home, loss, other, grad_image, losses, grad_text, image_buf, loss_buf, text_buf, sems):
     width, rows = grad_text.shape
     half, step = rows // 2, width // parts
-    low = later[len(MASKS)] == 0
     f32 = jnp.float32
     copies = []
 
@@ -200,6 +204,7 @@
         copy.start()
         copies.append(copy)
 
+    send(first, grad_text.at[:, pl.ds(0, half)])
     for k in range(parts):
         d = pl.ds(k * step, step)
         image_buf[d] = home[d] + other[d].astype(f32)
@@ -208,9 +213,8 @@
     send(loss_buf, losses)
     for k in range(parts):
         d = pl.ds(k * step, step)
-        text_buf[d, :half] = grad_t[d, :half] + jnp.where(low, r1[d].astype(f32), 0.0) + p1[d].astype(f32)
-        text_buf[d, half:] = grad_t[d, half:] + jnp.where(low, r2[d].astype(f32), 0.0) + p2[d].astype(f32)
-        send(text_buf.at[d], grad_text.at[d])
+        text_buf[d] = second[d] + past[d].astype(f32)
+        send(text_buf.at[d], grad_text.at[d, pl.ds(half, half)])
     for copy in copies:
         copy.wait()
 
@@ -286,25 +290,25 @@
     older2 = call(older_kernel, older, (later, grad_m2, r2), flops=20 * unit)
     past2 = moved(older2, back)
     _, late0 = lax.optimization_barrier((older2, g0))
-    grad_t = call(
+    first, second = call(
         own_text_kernel,
-        sds((width, rows), f32),
-        (tb, later, *images, late0),
+        (sds((width, half), f32),) * 2,
+        (tb, later, *images, late0, r1, r2),
         scratch=(pltpu.VMEM((4, rows, rows), bf16),),
     )
     _, late = lax.optimization_barrier((past1, l2))
-    rest = (tb, later, kept, x1, x2, g0, g1, g2, l0, l1, late, came)
-    home, home_loss = call(home_kernel, (sds((width, rows), f32), sds((8, rows), f32)), rest, flops=5 * unit)
+    rest = (tb, later, kept, x1, x2, g0, g1, g2, l0, l1, late, came, first, past1)
+    home, home_loss, first = call(home_kernel, (sds((width, rows), f32), sds((8, rows), f32), sds((width, half), f32)), rest, flops=5 * unit)
     parts = 4
     grad_image, losses, grad_text = call(
         functools.partial(last_kernel, parts),
         (sds((width, rows), f32), sds((1, rows), f32), sds((width, rows), f32)),
-        (later, grad_t, r1, r2, past1, past2, home, home_loss, other),
+        (first, second, past2, home, home_loss, other),
         scratch=(
             pltpu.VMEM((width, rows), f32),
             pltpu.VMEM((1, rows), f32),
-            pltpu.VMEM((width, rows), f32),
-            pltpu.SemaphoreType.DMA((2 * parts + 1,)),
+            pltpu.VMEM((width, half), f32),
+            pltpu.SemaphoreType.DMA((2 * parts + 2,)),
         ),
         out_space=pl.ANY,
     )

time: 55.3 us -> 54.7 us (0.989)
  transfers between devices with their start and end apart: 15 -> 15, of which waited for: 8 -> 8; matrix products, arithmetic and copies ran while one was open for 0% -> 0% of each run, Pallas kernels for 25% -> 26%
where the time goes in v5:
time: 54.7 us; the launch traced here: 54.6 us
  starting transfers between devices  20.9 us (38%)
  Pallas kernels  15.6 us (29%)
  waiting for transfers between devices  14.7 us (27%)
  between operations  2.1 us (4%)
  local copies, waits for them, and re-layouts  1.23 us (2%)
    ppermute x15, starting transfers between devices, moved(): return lax.ppermute(block, AXES, [(i, target(i, n)) for i in range(n)])  20.9 us
    pallas_call x12, Pallas kernels, call(): pl.pallas_call(kernel, out_shape=out_shape, in_specs=[pl.BlockSpec(memory...  15.6 us
    ppermute x15, waiting for transfers between devices, moved(): return lax.ppermute(block, AXES, [(i, target(i, n)) for i in range(n)])  14.7 us
    unnamed x6, local copies, waits for them, and re-layouts  1.13 us
  transfers between devices with their start and end apart: 15, of which 8 were waited for; matrix products, arithmetic and copies ran while one was open for 0% of the time, Pallas kernels for 26%

profile of v5, /device:TPU:0, one launch (start us, length us, event | category | flops | bytes accessed | tf_op | source)
XLA Modules:
  0.0 54.6 jit_solution(15717680065706111892)
XLA Ops:
  1.9 3.1 %collective-permute-start.3 = (bf16[512,128]{1,0:T(8,128)(2,1)S(1)}, bf16[512,128]{1,0:T(8,128)(2,1)S(1)}, u32[]{:S(2)}, u32[]{:S(2)}) collective-permute-start(bf16[512,128]{1,0:T(8,128)(2,1)S(1)} %get-tuple-element.41), channel_id=1, source_target_pairs={{0,8},{1,9},{2,10},{3,11},{4,12},{5,13},{6,14},{7,15},{8,16},{9,17... | collective-permute-start | bytes 393224 | tf_op jit(solution)/shard_map/ppermute | solution.py:28
  5.0 1.5 %collective-permute-start.1 = (bf16[1152,256]{1,0:T(8,128)(2,1)}, bf16[1152,256]{1,0:T(8,128)(2,1)S(1)}, u32[]{:S(2)}, u32[]{:S(2)}) collective-permute-start(bf16[1152,256]{1,0:T(8,128)(2,1)} %i0.9), channel_id=1, source_target_pairs={{0,1},{1,0},{2,3},{3,2},{4,5},{5,4},{6,7},{7,6},{8,9},{9,8},{10,11... | collective-permute-start | bytes 1769480 | tf_op jit(solution)/shard_map/ppermute | solution.py:28
  6.4 1.6 %collective-permute-start.4 = (bf16[640,128]{1,0:T(8,128)(2,1)S(1)}, bf16[640,128]{1,0:T(8,128)(2,1)S(1)}, u32[]{:S(2)}, u32[]{:S(2)}) collective-permute-start(bf16[640,128]{1,0:T(8,128)(2,1)S(1)} %get-tuple-element.42), channel_id=1, source_target_pairs={{0,8},{1,9},{2,10},{3,11},{4,12},{5,13},{6,14},{7,15},{8,16},{9,17... | collective-permute-start | bytes 491528 | tf_op jit(solution)/shard_map/ppermute | solution.py:28
  8.0 1.6 %collective-permute-start.5 = (bf16[1152,128]{1,0:T(8,128)(2,1)S(1)}, bf16[1152,128]{1,0:T(8,128)(2,1)S(1)}, u32[]{:S(2)}, u32[]{:S(2)}) collective-permute-start(bf16[1152,128]{1,0:T(8,128)(2,1)S(1)} %get-tuple-element.43), channel_id=1, source_target_pairs={{0,8},{1,9},{2,10},{3,11},{4,12},{5,13},{6,14},{7,15},{8,16},{9,17... | collective-permute-start | bytes 884744 | tf_op jit(solution)/shard_map/ppermute | solution.py:28
  11.0 1.6 %collective-permute-start.6 = (bf16[512,128]{1,0:T(8,128)(2,1)S(1)}, bf16[512,128]{1,0:T(8,128)(2,1)S(1)}, u32[]{:S(2)}, u32[]{:S(2)}) collective-permute-start(bf16[512,128]{1,0:T(8,128)(2,1)S(1)} %broadcast_select_fusion.2), channel_id=1, source_target_pairs={{0,4},{1,5},{2,6},{3,7},{4,0},{5,1},{6,2},{7,3},{8,12},{9,13},{10,... | collective-permute-start | bytes 393224 | tf_op jit(solution)/shard_map/ppermute | solution.py:28
  12.6 2.6 %collective-permute-done.4.m1b = bf16[640,128]{1,0:T(8,128)(2,1)S(1)} collective-permute-done((bf16[640,128]{1,0:T(8,128)(2,1)S(1)}, bf16[640,128]{1,0:T(8,128)(2,1)S(1)}, u32[]{:S(2)}, u32[]{:S(2)}) %collective-permute-start.4) | collective-permute-done | bytes 163872 | tf_op jit(solution)/shard_map/ppermute | solution.py:28
  15.3 1.6 %collective-permute-start.7 = (bf16[640,128]{1,0:T(8,128)(2,1)S(1)}, bf16[640,128]{1,0:T(8,128)(2,1)S(1)}, u32[]{:S(2)}, u32[]{:S(2)}) collective-permute-start(bf16[640,128]{1,0:T(8,128)(2,1)S(1)} %broadcast_select_fusion.1), channel_id=1, source_target_pairs={{0,4},{1,5},{2,6},{3,7},{4,0},{5,1},{6,2},{7,3},{8,12},{9,13},{10,... | collective-permute-start | bytes 491528 | tf_op jit(solution)/shard_map/ppermute | solution.py:28
  16.8 3.1 %collective-permute-done.1.i2 = bf16[1152,256]{1,0:T(8,128)(2,1)S(1)} collective-permute-done((bf16[1152,256]{1,0:T(8,128)(2,1)}, bf16[1152,256]{1,0:T(8,128)(2,1)S(1)}, u32[]{:S(2)}, u32[]{:S(2)}) %collective-permute-start.1) | collective-permute-done | bytes 589856 | tf_op jit(solution)/shard_map/ppermute | solution.py:28
  20.0 1.2 %collective-permute-done.5.m2 = bf16[1152,128]{1,0:T(8,128)(2,1)S(1)} collective-permute-done((bf16[1152,128]{1,0:T(8,128)(2,1)S(1)}, bf16[1152,128]{1,0:T(8,128)(2,1)S(1)}, u32[]{:S(2)}, u32[]{:S(2)}) %collective-permute-start.5) | collective-permute-done | bytes 294944 | tf_op jit(solution)/shard_map/ppermute | solution.py:28
  21.2 1.6 %collective-permute-start.8 = (bf16[1152,128]{1,0:T(8,128)(2,1)S(1)}, bf16[1152,128]{1,0:T(8,128)(2,1)S(1)}, u32[]{:S(2)}, u32[]{:S(2)}) collective-permute-start(bf16[1152,128]{1,0:T(8,128)(2,1)S(1)} %broadcast_select_fusion), channel_id=1, source_target_pairs={{0,4},{1,5},{2,6},{3,7},{4,0},{5,1},{6,2},{7,3},{8,12},{9,13},{10,... | collective-permute-start | bytes 884744 | tf_op jit(solution)/shard_map/ppermute | solution.py:28
  22.9 2.7 %shard_map.68 = (f32[1152,128]{1,0:T(8,128)S(1)}, f32[1152,128]{1,0:T(8,128)S(1)}, bf16[4,256,256]{2,1,0:T(8,128)(2,1)S(1)}, f32[8,256]{1,0:T(8,128)S(1)}, bf16[2,1152,256]{2,1,0:T(8,128)(2,1)S(1)}) custom-call(f32[2]{0:T(128)S(1)} %pad_maximum_fusion.tb, s32[5]{0:T(128)S(1)} %stack.26.later, bf16[1152,256]{1,0:T(8,128)(2,1)S(1)} %copy-done, ...), custom_call_target="tpu_custom_call" | custom-call | tf_op jit(solution)/shard_map/pallas_call | solution.py:224
  25.6 2.0 %shard_map.69 = (bf16[1152,128]{1,0:T(8,128)(2,1)S(1)}, bf16[4,128,256]{2,1,0:T(8,128)(2,1)S(1)}, f32[8,256]{1,0:T(8,128)S(1)}, bf16[1152,128]{1,0:T(8,128)(2,1)S(1)}) custom-call(f32[2]{0:T(128)S(1)} %pad_maximum_fusion.tb, bf16[1152,256]{1,0:T(8,128)(2,1)S(1)} %copy-done, bf16[1152,256]{1,0:T(8,128)(2,1)S(1)} %collective-permute-done.i1, ...), custom_call_target="tpu_custom_call" | custom-call | tf_op jit(solution)/shard_map/pallas_call | solution.py:224
  28.3 1.6 %shard_map.70.part = f32[3,1152,256]{2,1,0:T(8,128)S(1)} custom-call(s32[5]{0:T(128)S(1)} %stack.26.later, bf16[2,1152,256]{2,1,0:T(8,128)(2,1)S(1)} %get-tuple-element.44.kept, bf16[1152,128]{1,0:T(8,128)(2,1)S(1)} %get-tuple-element.48.k1.x1, bf16[4,256,256]{2,1,0:T(8,128)(2,1)S(1)} %get-tuple-element.62.g.grad, bf16[4,128,256]{2,1,0:T(8,128)(2,1)S(1)} %get-tuple-element.50.g1), custom_call_target="tpu_custom_call" | custom-call | tf_op jit(solution)/shard_map/pallas_call | solution.py:224
  30.0 1.7 %shard_map.71 = (bf16[4,128,256]{2,1,0:T(8,128)(2,1)S(1)}, f32[8,256]{1,0:T(8,128)S(1)}, bf16[2,1168,256]{2,1,0:T(8,128)(2,1)S(1)}) custom-call(f32[2]{0:T(128)S(1)} %pad_maximum_fusion.tb, bf16[1152,256]{1,0:T(8,128)(2,1)S(1)} %copy-done, bf16[1152,256]{1,0:T(8,128)(2,1)S(1)} %collective-permute-done.i1, bf16[1152,256]{1,0:T(8,128)(2,1)S(1)} %collective-permute-done.1.i2, ...), custom_call_target="tpu_custom_call" | custom-call | tf_op jit(solution)/shard_map/pallas_call | solution.py:224
  31.8 1.3 %shard_map.74 = bf16[1152,128]{1,0:T(8,128)(2,1)S(1)} custom-call(f32[2]{0:T(128)S(1)} %pad_maximum_fusion.tb, bf16[1152,256]{1,0:T(8,128)(2,1)S(1)} %copy-done, bf16[1152,256]{1,0:T(8,128)(2,1)S(1)} %collective-permute-done.i1, bf16[1152,256]{1,0:T(8,128)(2,1)S(1)} %collective-permute-done.1.i2, bf16[1152,256]{1,0:T(8,128)(2,1)S(1)} %collective-permute-done.2.i3, ...), custom_call_target="tpu_custom_call" | custom-call | tf_op jit(solution)/shard_map/pallas_call | solution.py:224
  33.1 1.8 %collective-permute-start.12 = (bf16[1152,128]{1,0:T(8,128)(2,1)S(1)}, bf16[1152,128]{1,0:T(8,128)(2,1)S(1)}, u32[]{:S(2)}, u32[]{:S(2)}) collective-permute-start(bf16[1152,128]{1,0:T(8,128)(2,1)S(1)} %shard_map.74), channel_id=1, source_target_pairs={{0,4},{1,5},{2,6},{3,7},{4,0},{5,1},{6,2},{7,3},{8,12},{9,13},{10,... | collective-permute-start | bytes 884744 | tf_op jit(solution)/shard_map/ppermute | solution.py:28
  34.9 1.3 %collective-permute-done.9.returned.r1 = bf16[1152,128]{1,0:T(8,128)(2,1)S(1)} collective-permute-done((bf16[1152,128]{1,0:T(8,128)(2,1)S(1)}, bf16[1152,128]{1,0:T(8,128)(2,1)S(1)}, u32[]{:S(2)}, u32[]{:S(2)}) %collective-permute-start.9) | collective-permute-done | bytes 294944 | tf_op jit(solution)/shard_map/ppermute | solution.py:28
  38.9 2.4 %collective-permute-start.11 = (bf16[1152,128]{1,0:T(8,128)(2,1)S(1)}, bf16[1152,128]{1,0:T(8,128)(2,1)S(1)}, u32[]{:S(2)}, u32[]{:S(2)}) collective-permute-start(bf16[1152,128]{1,0:T(8,128)(2,1)S(1)} %shard_map.72), channel_id=1, source_target_pairs={{0,24},{1,25},{2,26},{3,27},{4,28},{5,29},{6,30},{7,31},{8,0},{9,1... | collective-permute-start | bytes 884744 | tf_op jit(solution)/shard_map/ppermute | solution.py:28
  41.3 1.3 %collective-permute-done.12.returned.r2 = bf16[1152,128]{1,0:T(8,128)(2,1)S(1)} collective-permute-done((bf16[1152,128]{1,0:T(8,128)(2,1)S(1)}, bf16[1152,128]{1,0:T(8,128)(2,1)S(1)}, u32[]{:S(2)}, u32[]{:S(2)}) %collective-permute-start.12) | collective-permute-done | bytes 294944 | tf_op jit(solution)/shard_map/ppermute | solution.py:28
  43.2 2.3 %collective-permute-start.13 = (bf16[1152,128]{1,0:T(8,128)(2,1)S(1)}, bf16[1152,128]{1,0:T(8,128)(2,1)S(1)}, u32[]{:S(2)}, u32[]{:S(2)}) collective-permute-start(bf16[1152,128]{1,0:T(8,128)(2,1)S(1)} %shard_map.75), channel_id=1, source_target_pairs={{0,24},{1,25},{2,26},{3,27},{4,28},{5,29},{6,30},{7,31},{8,0},{9,1... | collective-permute-start | bytes 884744 | tf_op jit(solution)/shard_map/ppermute | solution.py:28
  45.5 1.4 %shard_map.76 = (f32[1152,128]{1,0:T(8,128)S(1)}, f32[1152,128]{1,0:T(8,128)S(1)}) custom-call(f32[2]{0:T(128)S(1)} %pad_maximum_fusion.tb, s32[5]{0:T(128)S(1)} %stack.26.later, bf16[1152,256]{1,0:T(8,128)(2,1)S(1)} %copy-done, bf16[1152,256]{1,0:T(8,128)(2,1)S(1)} %collective-permute-done.i1, bf16[1152,256]{1,0:T(8,128)(2,1)S(1)} %collective-permute-done.1.i2, ...), custom_call_target="tpu_custom_call" | custom-call | tf_op jit(solution)/shard_map/pallas_call | solution.py:224
  48.1 1.2 %shard_map.77 = (f32[1152,256]{1,0:T(8,128)S(1)}, f32[8,256]{1,0:T(8,128)S(1)}, f32[1152,128]{1,0:T(8,128)S(1)}) custom-call(f32[2]{0:T(128)S(1)} %pad_maximum_fusion.tb, s32[5]{0:T(128)S(1)} %stack.26.later, bf16[2,1152,256]{2,1,0:T(8,128)(2,1)S(1)} %get-tuple-element.44.kept, bf16[1152,128]{1,0:T(8,128)(2,1)S(1)} %get-tuple-element.48.k1.x1, ...), custom_call_target="tpu_custom_call" | custom-call | flops 754974720 | tf_op jit(solution)/shard_map/pallas_call | solution.py:224
  49.3 3.8 %collective-permute-done.13.past = bf16[1152,128]{1,0:T(8,128)(2,1)S(1)} collective-permute-done((bf16[1152,128]{1,0:T(8,128)(2,1)S(1)}, bf16[1152,128]{1,0:T(8,128)(2,1)S(1)}, u32[]{:S(2)}, u32[]{:S(2)}) %collective-permute-start.13) | collective-permute-done | bytes 294944 | tf_op jit(solution)/shard_map/ppermute | solution.py:28
  53.1 1.5 %shard_map.78 = (f32[1152,256]{1,0:T(8,128)}, f32[1,256]{1,0:T(1,128)}, f32[1152,256]{1,0:T(8,128)}) custom-call(f32[1152,128]{1,0:T(8,128)S(1)} %get-tuple-element.64.first, f32[1152,128]{1,0:T(8,128)S(1)} %get-tuple-element.65.second, bf16[1152,128]{1,0:T(8,128)(2,1)S(1)} %collective-permute-done.13.past, f32[1152,256]{1,0:T(8,128)S(1)} %get-tuple-element.66.home, ...), custom_call_target="tpu_custom_call" | custom-call | tf_op jit(solution)/shard_map/pallas_call | solution.py:224
  (30 shorter events, 6.8 us)
Async XLA Ops:
  0.6 22.3 %copy-start = (bf16[1152,256]{1,0:T(8,128)(2,1)S(1)}, bf16[1152,256]{1,0:T(8,128)(2,1)}, u32[]{:S(2)}) copy-start(bf16[1152,256]{1,0:T(8,128)(2,1)} %i0.9) | copy-start | bytes 1769476
  0.6 1.1 %copy-start.1 = (bf16[1152,256]{1,0:T(8,128)(2,1)S(1)}, bf16[1152,256]{1,0:T(8,128)(2,1)}, u32[]{:S(2)}) copy-start(bf16[1152,256]{1,0:T(8,128)(2,1)} %text.3) | copy-start | bytes 1769476
  1.8 21.1 %copy-start.2 = (bf16[1152,256]{1,0:T(8,128)(2,1)S(1)}, bf16[1152,256]{1,0:T(8,128)(2,1)}, u32[]{:S(2)}) copy-start(bf16[1152,256]{1,0:T(8,128)(2,1)} %text.3) | copy-start | bytes 1769476
  1.9 9.2 %collective-permute-start.3 = (bf16[512,128]{1,0:T(8,128)(2,1)S(1)}, bf16[512,128]{1,0:T(8,128)(2,1)S(1)}, u32[]{:S(2)}, u32[]{:S(2)}) collective-permute-start(bf16[512,128]{1,0:T(8,128)(2,1)S(1)} %get-tuple-element.41), channel_id=1, source_target_pairs={{0,8},{1,9},{2,10},{3,11},{4,12},{5,13},{6,14},{7,15},{8,16},{9,17... | collective-permute-start | bytes 393224 | tf_op jit(solution)/shard_map/ppermute | solution.py:28
  5.0 15.0 %collective-permute-start.1 = (bf16[1152,256]{1,0:T(8,128)(2,1)}, bf16[1152,256]{1,0:T(8,128)(2,1)S(1)}, u32[]{:S(2)}, u32[]{:S(2)}) collective-permute-start(bf16[1152,256]{1,0:T(8,128)(2,1)} %i0.9), channel_id=1, source_target_pairs={{0,1},{1,0},{2,3},{3,2},{4,5},{5,4},{6,7},{7,6},{8,9},{9,8},{10,11... | collective-permute-start | bytes 1769480 | tf_op jit(solution)/shard_map/ppermute | solution.py:28
  6.4 16.4 %collective-permute-start = (bf16[1152,256]{1,0:T(8,128)(2,1)}, bf16[1152,256]{1,0:T(8,128)(2,1)S(1)}, u32[]{:S(2)}, u32[]{:S(2)}) collective-permute-start(bf16[1152,256]{1,0:T(8,128)(2,1)} %i0.9), channel_id=1, source_target_pairs={{0,2},{1,3},{2,0},{3,1},{4,6},{5,7},{6,4},{7,5},{8,10},{9,11},{10,... | collective-permute-start | bytes 1769480 | tf_op jit(solution)/shard_map/ppermute | solution.py:28
  6.4 8.8 %collective-permute-start.4 = (bf16[640,128]{1,0:T(8,128)(2,1)S(1)}, bf16[640,128]{1,0:T(8,128)(2,1)S(1)}, u32[]{:S(2)}, u32[]{:S(2)}) collective-permute-start(bf16[640,128]{1,0:T(8,128)(2,1)S(1)} %get-tuple-element.42), channel_id=1, source_target_pairs={{0,8},{1,9},{2,10},{3,11},{4,12},{5,13},{6,14},{7,15},{8,16},{9,17... | collective-permute-start | bytes 491528 | tf_op jit(solution)/shard_map/ppermute | solution.py:28
  8.0 13.2 %collective-permute-start.5 = (bf16[1152,128]{1,0:T(8,128)(2,1)S(1)}, bf16[1152,128]{1,0:T(8,128)(2,1)S(1)}, u32[]{:S(2)}, u32[]{:S(2)}) collective-permute-start(bf16[1152,128]{1,0:T(8,128)(2,1)S(1)} %get-tuple-element.43), channel_id=1, source_target_pairs={{0,8},{1,9},{2,10},{3,11},{4,12},{5,13},{6,14},{7,15},{8,16},{9,17... | collective-permute-start | bytes 884744 | tf_op jit(solution)/shard_map/ppermute | solution.py:28
  11.0 14.6 %collective-permute-start.6 = (bf16[512,128]{1,0:T(8,128)(2,1)S(1)}, bf16[512,128]{1,0:T(8,128)(2,1)S(1)}, u32[]{:S(2)}, u32[]{:S(2)}) collective-permute-start(bf16[512,128]{1,0:T(8,128)(2,1)S(1)} %broadcast_select_fusion.2), channel_id=1, source_target_pairs={{0,4},{1,5},{2,6},{3,7},{4,0},{5,1},{6,2},{7,3},{8,12},{9,13},{10,... | collective-permute-start | bytes 393224 | tf_op jit(solution)/shard_map/ppermute | solution.py:28
  15.3 10.3 %collective-permute-start.7 = (bf16[640,128]{1,0:T(8,128)(2,1)S(1)}, bf16[640,128]{1,0:T(8,128)(2,1)S(1)}, u32[]{:S(2)}, u32[]{:S(2)}) collective-permute-start(bf16[640,128]{1,0:T(8,128)(2,1)S(1)} %broadcast_select_fusion.1), channel_id=1, source_target_pairs={{0,4},{1,5},{2,6},{3,7},{4,0},{5,1},{6,2},{7,3},{8,12},{9,13},{10,... | collective-permute-start | bytes 491528 | tf_op jit(solution)/shard_map/ppermute | solution.py:28
  20.0 2.9 %collective-permute-start.2 = (bf16[1152,256]{1,0:T(8,128)(2,1)S(1)}, bf16[1152,256]{1,0:T(8,128)(2,1)S(1)}, u32[]{:S(2)}, u32[]{:S(2)}) collective-permute-start(bf16[1152,256]{1,0:T(8,128)(2,1)S(1)} %collective-permute-done.1.i2), channel_id=1, source_target_pairs={{0,2},{1,3},{2,0},{3,1},{4,6},{5,7},{6,4},{7,5},{8,10},{9,11},{10,... | collective-permute-start | bytes 1769480 | tf_op jit(solution)/shard_map/ppermute | solution.py:28
  21.2 8.8 %collective-permute-start.8 = (bf16[1152,128]{1,0:T(8,128)(2,1)S(1)}, bf16[1152,128]{1,0:T(8,128)(2,1)S(1)}, u32[]{:S(2)}, u32[]{:S(2)}) collective-permute-start(bf16[1152,128]{1,0:T(8,128)(2,1)S(1)} %broadcast_select_fusion), channel_id=1, source_target_pairs={{0,4},{1,5},{2,6},{3,7},{4,0},{5,1},{6,2},{7,3},{8,12},{9,13},{10,... | collective-permute-start | bytes 884744 | tf_op jit(solution)/shard_map/ppermute | solution.py:28
  27.6 8.6 %collective-permute-start.9 = (bf16[1152,128]{1,0:T(8,128)(2,1)S(1)}, bf16[1152,128]{1,0:T(8,128)(2,1)S(1)}, u32[]{:S(2)}, u32[]{:S(2)}) collective-permute-start(bf16[1152,128]{1,0:T(8,128)(2,1)S(1)} %get-tuple-element.54), channel_id=1, source_target_pairs={{0,4},{1,5},{2,6},{3,7},{4,0},{5,1},{6,2},{7,3},{8,12},{9,13},{10,... | collective-permute-start | bytes 884744 | tf_op jit(solution)/shard_map/ppermute | solution.py:28
  31.7 5.2 %collective-permute-start.10 = (bf16[2,1168,256]{2,1,0:T(8,128)(2,1)S(1)}, bf16[2,1168,256]{2,1,0:T(8,128)(2,1)S(1)}, u32[]{:S(2)}, u32[]{:S(2)}) collective-permute-start(bf16[2,1168,256]{2,1,0:T(8,128)(2,1)S(1)} %get-tuple-element.58), channel_id=1, source_target_pairs={{0,2},{1,3},{2,0},{3,1},{4,6},{5,7},{6,4},{7,5},{8,10},{9,11},{10,... | collective-permute-start | bytes 3588104 | tf_op jit(solution)/shard_map/ppermute | solution.py:28
  33.1 9.5 %collective-permute-start.12 = (bf16[1152,128]{1,0:T(8,128)(2,1)S(1)}, bf16[1152,128]{1,0:T(8,128)(2,1)S(1)}, u32[]{:S(2)}, u32[]{:S(2)}) collective-permute-start(bf16[1152,128]{1,0:T(8,128)(2,1)S(1)} %shard_map.74), channel_id=1, source_target_pairs={{0,4},{1,5},{2,6},{3,7},{4,0},{5,1},{6,2},{7,3},{8,12},{9,13},{10,... | collective-permute-start | bytes 884744 | tf_op jit(solution)/shard_map/ppermute | solution.py:28
  37.7 15.3 %collective-permute-start.14 = (bf16[1168,256]{1,0:T(8,128)(2,1)S(1)}, bf16[1168,256]{1,0:T(8,128)(2,1)S(1)}, u32[]{:S(2)}, u32[]{:S(2)}) collective-permute-start(bf16[1168,256]{1,0:T(8,128)(2,1)S(1)} %shard_map.73), channel_id=1, source_target_pairs={{0,1},{1,0},{2,3},{3,2},{4,5},{5,4},{6,7},{7,6},{8,9},{9,8},{10,11... | collective-permute-start | bytes 1794056 | tf_op jit(solution)/shard_map/ppermute | solution.py:28
  38.9 9.2 %collective-permute-start.11 = (bf16[1152,128]{1,0:T(8,128)(2,1)S(1)}, bf16[1152,128]{1,0:T(8,128)(2,1)S(1)}, u32[]{:S(2)}, u32[]{:S(2)}) collective-permute-start(bf16[1152,128]{1,0:T(8,128)(2,1)S(1)} %shard_map.72), channel_id=1, source_target_pairs={{0,24},{1,25},{2,26},{3,27},{4,28},{5,29},{6,30},{7,31},{8,0},{9,1... | collective-permute-start | bytes 884744 | tf_op jit(solution)/shard_map/ppermute | solution.py:28
  43.2 9.9 %collective-permute-start.13 = (bf16[1152,128]{1,0:T(8,128)(2,1)S(1)}, bf16[1152,128]{1,0:T(8,128)(2,1)S(1)}, u32[]{:S(2)}, u32[]{:S(2)}) collective-permute-start(bf16[1152,128]{1,0:T(8,128)(2,1)S(1)} %shard_map.75), channel_id=1, source_target_pairs={{0,24},{1,25},{2,26},{3,27},{4,28},{5,29},{6,30},{7,31},{8,0},{9,1... | collective-permute-start | bytes 884744 | tf_op jit(solution)/shard_map/ppermute | solution.py:28

commit v6 on v5

--- a/solution.py
+++ b/solution.py
@@ -169,11 +169,14 @@
         out[slot, width:] = packed_loss(l0[r : r + 1] + l1[r : r + 1] + loss[r : r + 1], (EXTRA, out.shape[2]))
 
 
-def joined_kernel(tb, text, part, grad, l0, l1, l2, came, out):
-    width = text.shape[0]
-    for d in range(0, width, TILE):
-        total = tb[0] * (part[2, d : d + TILE] + dot(text[d : d + TILE], grad[2], NN))
-        out[d : d + TILE] = (total + came[1, d : d + TILE].astype(jnp.float32)).astype(jnp.bfloat16)
+def pair_kernel(tb, text, part, grad, out):
+    for d in range(0, text.shape[0], TILE):
+        out[d : d + TILE] = tb[0] * (part[2, d : d + TILE] + dot(text[d : d + TILE], grad[2], NN))
+
+
+def joined_kernel(pair, l0, l1, l2, came, out):
+    width = pair.shape[0]
+    out[:width] = (pair[...] + came[1, :width].astype(jnp.float32)).astype(jnp.bfloat16)
     loss = l0[2:3] + l1[2:3] + l2[2:3] + unpacked_loss(came[1, width:])
     out[width:] = packed_loss(loss, (EXTRA, out.shape[1]))
 
@@ -281,9 +284,12 @@
     r2 = moved(grad_x2, swap(SIDE))
 
     older = sds((width, half), bf16)
+    _, after = lax.optimization_barrier((grad_x2, g2))
+    pair = call(pair_kernel, sds((width, rows), f32), (tb, x2, part, after))
+    grad_m1, pair = lax.optimization_barrier((grad_m1, pair))
     older1 = call(older_kernel, older, (later, grad_m1, r1), flops=80 * unit)
     _, held = lax.optimization_barrier((older1, l2))
-    joined = call(joined_kernel, sds((width + EXTRA, rows), bf16), (tb, x2, part, g2, l0, l1, held, came), flops=0 * unit)
+    joined = call(joined_kernel, sds((width + EXTRA, rows), bf16), (pair, l0, l1, held, came), flops=0 * unit)
     other = moved(joined, swap(PAIR))
     older1, grad_m2, _ = lax.optimization_barrier((older1, grad_m2, joined))
     past1 = moved(older1, back)

time: 54.7 us -> 54.2 us (level)
  waiting for transfers between devices: 14.7 us -> 14 us
    ppermute x15, waiting for transfers between devices: 14.7 us -> 14 us  [moved(): return lax.ppermute(block, AXES, [(i, target(i, n)) for i in range(n)])]
    pallas_call x12 -> x13, Pallas kernels: 15.6 us -> 15.7 us  [call(): pl.pallas_call(kernel, out_shape=out_shape, in_specs=[pl.BlockSpec(memory...]
  transfers between devices with their start and end apart: 15 -> 15, of which waited for: 8 -> 7; matrix products, arithmetic and copies ran while one was open for 0% -> 0% of each run, Pallas kernels for 26% -> 26%
where the time goes in v6:
time: 54.2 us; the launch traced here: 54 us
  starting transfers between devices  20.9 us (39%)
  Pallas kernels  15.7 us (29%)
  waiting for transfers between devices  14 us (26%)
  between operations  2.09 us (4%)
  local copies, waits for them, and re-layouts  1.23 us (2%)
    ppermute x15, starting transfers between devices, moved(): return lax.ppermute(block, AXES, [(i, target(i, n)) for i in range(n)])  20.9 us
    pallas_call x13, Pallas kernels, call(): pl.pallas_call(kernel, out_shape=out_shape, in_specs=[pl.BlockSpec(memory...  15.7 us
    ppermute x15, waiting for transfers between devices, moved(): return lax.ppermute(block, AXES, [(i, target(i, n)) for i in range(n)])  14 us
    unnamed x6, local copies, waits for them, and re-layouts  1.13 us
  transfers between devices with their start and end apart: 15, of which 7 were waited for; matrix products, arithmetic and copies ran while one was open for 0% of the time, Pallas kernels for 26%

profile of v6, /device:TPU:0, one launch (start us, length us, event | category | flops | bytes accessed | tf_op | source)
XLA Modules:
  0.0 54.0 jit_solution(7799680476827375022)
XLA Ops:
  1.9 3.1 %collective-permute-start.3 = (bf16[512,128]{1,0:T(8,128)(2,1)S(1)}, bf16[512,128]{1,0:T(8,128)(2,1)S(1)}, u32[]{:S(2)}, u32[]{:S(2)}) collective-permute-start(bf16[512,128]{1,0:T(8,128)(2,1)S(1)} %get-tuple-element.44), channel_id=1, source_target_pairs={{0,8},{1,9},{2,10},{3,11},{4,12},{5,13},{6,14},{7,15},{8,16},{9,17... | collective-permute-start | bytes 393224 | tf_op jit(solution)/shard_map/ppermute | solution.py:28
  5.0 1.5 %collective-permute-start.1 = (bf16[1152,256]{1,0:T(8,128)(2,1)}, bf16[1152,256]{1,0:T(8,128)(2,1)S(1)}, u32[]{:S(2)}, u32[]{:S(2)}) collective-permute-start(bf16[1152,256]{1,0:T(8,128)(2,1)} %i0.9), channel_id=1, source_target_pairs={{0,1},{1,0},{2,3},{3,2},{4,5},{5,4},{6,7},{7,6},{8,9},{9,8},{10,11... | collective-permute-start | bytes 1769480 | tf_op jit(solution)/shard_map/ppermute | solution.py:28
  6.4 1.6 %collective-permute-start.4 = (bf16[640,128]{1,0:T(8,128)(2,1)S(1)}, bf16[640,128]{1,0:T(8,128)(2,1)S(1)}, u32[]{:S(2)}, u32[]{:S(2)}) collective-permute-start(bf16[640,128]{1,0:T(8,128)(2,1)S(1)} %get-tuple-element.45), channel_id=1, source_target_pairs={{0,8},{1,9},{2,10},{3,11},{4,12},{5,13},{6,14},{7,15},{8,16},{9,17... | collective-permute-start | bytes 491528 | tf_op jit(solution)/shard_map/ppermute | solution.py:28
  8.0 1.6 %collective-permute-start.5 = (bf16[1152,128]{1,0:T(8,128)(2,1)S(1)}, bf16[1152,128]{1,0:T(8,128)(2,1)S(1)}, u32[]{:S(2)}, u32[]{:S(2)}) collective-permute-start(bf16[1152,128]{1,0:T(8,128)(2,1)S(1)} %get-tuple-element.46), channel_id=1, source_target_pairs={{0,8},{1,9},{2,10},{3,11},{4,12},{5,13},{6,14},{7,15},{8,16},{9,17... | collective-permute-start | bytes 884744 | tf_op jit(solution)/shard_map/ppermute | solution.py:28
  11.0 1.6 %collective-permute-start.6 = (bf16[512,128]{1,0:T(8,128)(2,1)S(1)}, bf16[512,128]{1,0:T(8,128)(2,1)S(1)}, u32[]{:S(2)}, u32[]{:S(2)}) collective-permute-start(bf16[512,128]{1,0:T(8,128)(2,1)S(1)} %broadcast_select_fusion.2), channel_id=1, source_target_pairs={{0,4},{1,5},{2,6},{3,7},{4,0},{5,1},{6,2},{7,3},{8,12},{9,13},{10,... | collective-permute-start | bytes 393224 | tf_op jit(solution)/shard_map/ppermute | solution.py:28
  12.6 2.6 %collective-permute-done.4.m1b = bf16[640,128]{1,0:T(8,128)(2,1)S(1)} collective-permute-done((bf16[640,128]{1,0:T(8,128)(2,1)S(1)}, bf16[640,128]{1,0:T(8,128)(2,1)S(1)}, u32[]{:S(2)}, u32[]{:S(2)}) %collective-permute-start.4) | collective-permute-done | bytes 163872 | tf_op jit(solution)/shard_map/ppermute | solution.py:28
  15.3 1.6 %collective-permute-start.7 = (bf16[640,128]{1,0:T(8,128)(2,1)S(1)}, bf16[640,128]{1,0:T(8,128)(2,1)S(1)}, u32[]{:S(2)}, u32[]{:S(2)}) collective-permute-start(bf16[640,128]{1,0:T(8,128)(2,1)S(1)} %broadcast_select_fusion.1), channel_id=1, source_target_pairs={{0,4},{1,5},{2,6},{3,7},{4,0},{5,1},{6,2},{7,3},{8,12},{9,13},{10,... | collective-permute-start | bytes 491528 | tf_op jit(solution)/shard_map/ppermute | solution.py:28
  16.8 3.1 %collective-permute-done.1.i2 = bf16[1152,256]{1,0:T(8,128)(2,1)S(1)} collective-permute-done((bf16[1152,256]{1,0:T(8,128)(2,1)}, bf16[1152,256]{1,0:T(8,128)(2,1)S(1)}, u32[]{:S(2)}, u32[]{:S(2)}) %collective-permute-start.1) | collective-permute-done | bytes 589856 | tf_op jit(solution)/shard_map/ppermute | solution.py:28
  20.0 1.2 %collective-permute-done.5.m2 = bf16[1152,128]{1,0:T(8,128)(2,1)S(1)} collective-permute-done((bf16[1152,128]{1,0:T(8,128)(2,1)S(1)}, bf16[1152,128]{1,0:T(8,128)(2,1)S(1)}, u32[]{:S(2)}, u32[]{:S(2)}) %collective-permute-start.5) | collective-permute-done | bytes 294944 | tf_op jit(solution)/shard_map/ppermute | solution.py:28
  21.2 1.6 %collective-permute-start.8 = (bf16[1152,128]{1,0:T(8,128)(2,1)S(1)}, bf16[1152,128]{1,0:T(8,128)(2,1)S(1)}, u32[]{:S(2)}, u32[]{:S(2)}) collective-permute-start(bf16[1152,128]{1,0:T(8,128)(2,1)S(1)} %broadcast_select_fusion), channel_id=1, source_target_pairs={{0,4},{1,5},{2,6},{3,7},{4,0},{5,1},{6,2},{7,3},{8,12},{9,13},{10,... | collective-permute-start | bytes 884744 | tf_op jit(solution)/shard_map/ppermute | solution.py:28
  22.9 2.7 %shard_map.68 = (f32[1152,128]{1,0:T(8,128)S(1)}, f32[1152,128]{1,0:T(8,128)S(1)}, bf16[4,256,256]{2,1,0:T(8,128)(2,1)S(1)}, f32[8,256]{1,0:T(8,128)S(1)}, bf16[2,1152,256]{2,1,0:T(8,128)(2,1)S(1)}) custom-call(f32[2]{0:T(128)S(1)} %pad_maximum_fusion.tb, s32[5]{0:T(128)S(1)} %stack.26.later, bf16[1152,256]{1,0:T(8,128)(2,1)S(1)} %copy-done, ...), custom_call_target="tpu_custom_call" | custom-call | tf_op jit(solution)/shard_map/pallas_call | solution.py:227
  25.6 2.0 %shard_map.69 = (bf16[1152,128]{1,0:T(8,128)(2,1)S(1)}, bf16[4,128,256]{2,1,0:T(8,128)(2,1)S(1)}, f32[8,256]{1,0:T(8,128)S(1)}, bf16[1152,128]{1,0:T(8,128)(2,1)S(1)}) custom-call(f32[2]{0:T(128)S(1)} %pad_maximum_fusion.tb, bf16[1152,256]{1,0:T(8,128)(2,1)S(1)} %copy-done, bf16[1152,256]{1,0:T(8,128)(2,1)S(1)} %collective-permute-done.i1, ...), custom_call_target="tpu_custom_call" | custom-call | tf_op jit(solution)/shard_map/pallas_call | solution.py:227
  28.3 1.6 %shard_map.70.part = f32[3,1152,256]{2,1,0:T(8,128)S(1)} custom-call(s32[5]{0:T(128)S(1)} %stack.26.later, bf16[2,1152,256]{2,1,0:T(8,128)(2,1)S(1)} %get-tuple-element.47.kept, bf16[1152,128]{1,0:T(8,128)(2,1)S(1)} %get-tuple-element.51.k1.x1, bf16[4,256,256]{2,1,0:T(8,128)(2,1)S(1)} %get-tuple-element.68.g.grad, bf16[4,128,256]{2,1,0:T(8,128)(2,1)S(1)} %get-tuple-element.53.g1), custom_call_target="tpu_custom_call" | custom-call | tf_op jit(solution)/shard_map/pallas_call | solution.py:227
  30.0 1.7 %shard_map.71 = (bf16[4,128,256]{2,1,0:T(8,128)(2,1)S(1)}, f32[8,256]{1,0:T(8,128)S(1)}, bf16[2,1168,256]{2,1,0:T(8,128)(2,1)S(1)}) custom-call(f32[2]{0:T(128)S(1)} %pad_maximum_fusion.tb, bf16[1152,256]{1,0:T(8,128)(2,1)S(1)} %copy-done, bf16[1152,256]{1,0:T(8,128)(2,1)S(1)} %collective-permute-done.i1, bf16[1152,256]{1,0:T(8,128)(2,1)S(1)} %collective-permute-done.1.i2, ...), custom_call_target="tpu_custom_call" | custom-call | tf_op jit(solution)/shard_map/pallas_call | solution.py:227
  31.7 1.3 %shard_map.72 = bf16[1152,128]{1,0:T(8,128)(2,1)S(1)} custom-call(f32[2]{0:T(128)S(1)} %pad_maximum_fusion.tb, bf16[1152,256]{1,0:T(8,128)(2,1)S(1)} %copy-done, bf16[1152,256]{1,0:T(8,128)(2,1)S(1)} %collective-permute-done.i1, bf16[1152,256]{1,0:T(8,128)(2,1)S(1)} %collective-permute-done.1.i2, bf16[1152,256]{1,0:T(8,128)(2,1)S(1)} %collective-permute-done.2.i3, ...), custom_call_target="tpu_custom_call" | custom-call | tf_op jit(solution)/shard_map/pallas_call | solution.py:227
  33.1 1.8 %collective-permute-start.12 = (bf16[1152,128]{1,0:T(8,128)(2,1)S(1)}, bf16[1152,128]{1,0:T(8,128)(2,1)S(1)}, u32[]{:S(2)}, u32[]{:S(2)}) collective-permute-start(bf16[1152,128]{1,0:T(8,128)(2,1)S(1)} %shard_map.72), channel_id=1, source_target_pairs={{0,4},{1,5},{2,6},{3,7},{4,0},{5,1},{6,2},{7,3},{8,12},{9,13},{10,... | collective-permute-start | bytes 884744 | tf_op jit(solution)/shard_map/ppermute | solution.py:28
  37.0 1.1 %collective-permute-start.14 = (bf16[1168,256]{1,0:T(8,128)(2,1)S(1)}, bf16[1168,256]{1,0:T(8,128)(2,1)S(1)}, u32[]{:S(2)}, u32[]{:S(2)}) collective-permute-start(bf16[1168,256]{1,0:T(8,128)(2,1)S(1)} %shard_map.75), channel_id=1, source_target_pairs={{0,1},{1,0},{2,3},{3,2},{4,5},{5,4},{6,7},{7,6},{8,9},{9,8},{10,11... | collective-permute-start | bytes 1794056 | tf_op jit(solution)/shard_map/ppermute | solution.py:28
  38.2 2.4 %collective-permute-start.11 = (bf16[1152,128]{1,0:T(8,128)(2,1)S(1)}, bf16[1152,128]{1,0:T(8,128)(2,1)S(1)}, u32[]{:S(2)}, u32[]{:S(2)}) collective-permute-start(bf16[1152,128]{1,0:T(8,128)(2,1)S(1)} %shard_map.74), channel_id=1, source_target_pairs={{0,24},{1,25},{2,26},{3,27},{4,28},{5,29},{6,30},{7,31},{8,0},{9,1... | collective-permute-start | bytes 884744 | tf_op jit(solution)/shard_map/ppermute | solution.py:28
  40.6 2.0 %collective-permute-done.12.returned.r2 = bf16[1152,128]{1,0:T(8,128)(2,1)S(1)} collective-permute-done((bf16[1152,128]{1,0:T(8,128)(2,1)S(1)}, bf16[1152,128]{1,0:T(8,128)(2,1)S(1)}, u32[]{:S(2)}, u32[]{:S(2)}) %collective-permute-start.12) | collective-permute-done | bytes 294944 | tf_op jit(solution)/shard_map/ppermute | solution.py:28
  43.2 2.3 %collective-permute-start.13 = (bf16[1152,128]{1,0:T(8,128)(2,1)S(1)}, bf16[1152,128]{1,0:T(8,128)(2,1)S(1)}, u32[]{:S(2)}, u32[]{:S(2)}) collective-permute-start(bf16[1152,128]{1,0:T(8,128)(2,1)S(1)} %shard_map.76), channel_id=1, source_target_pairs={{0,24},{1,25},{2,26},{3,27},{4,28},{5,29},{6,30},{7,31},{8,0},{9,1... | collective-permute-start | bytes 884744 | tf_op jit(solution)/shard_map/ppermute | solution.py:28
  45.5 1.4 %shard_map.77 = (f32[1152,128]{1,0:T(8,128)S(1)}, f32[1152,128]{1,0:T(8,128)S(1)}) custom-call(f32[2]{0:T(128)S(1)} %pad_maximum_fusion.tb, s32[5]{0:T(128)S(1)} %stack.26.later, bf16[1152,256]{1,0:T(8,128)(2,1)S(1)} %copy-done, bf16[1152,256]{1,0:T(8,128)(2,1)S(1)} %collective-permute-done.i1, bf16[1152,256]{1,0:T(8,128)(2,1)S(1)} %collective-permute-done.1.i2, ...), custom_call_target="tpu_custom_call" | custom-call | tf_op jit(solution)/shard_map/pallas_call | solution.py:227
  46.9 1.2 %shard_map.78 = (f32[1152,256]{1,0:T(8,128)S(1)}, f32[8,256]{1,0:T(8,128)S(1)}, f32[1152,128]{1,0:T(8,128)S(1)}) custom-call(f32[2]{0:T(128)S(1)} %pad_maximum_fusion.tb, s32[5]{0:T(128)S(1)} %stack.26.later, bf16[2,1152,256]{2,1,0:T(8,128)(2,1)S(1)} %get-tuple-element.47.kept, bf16[1152,128]{1,0:T(8,128)(2,1)S(1)} %get-tuple-element.51.k1.x1, ...), custom_call_target="tpu_custom_call" | custom-call | flops 754974720 | tf_op jit(solution)/shard_map/pallas_call | solution.py:227
  48.1 4.4 %collective-permute-done.13.past = bf16[1152,128]{1,0:T(8,128)(2,1)S(1)} collective-permute-done((bf16[1152,128]{1,0:T(8,128)(2,1)S(1)}, bf16[1152,128]{1,0:T(8,128)(2,1)S(1)}, u32[]{:S(2)}, u32[]{:S(2)}) %collective-permute-start.13) | collective-permute-done | bytes 294944 | tf_op jit(solution)/shard_map/ppermute | solution.py:28
  52.5 1.5 %shard_map.79 = (f32[1152,256]{1,0:T(8,128)}, f32[1,256]{1,0:T(1,128)}, f32[1152,256]{1,0:T(8,128)}) custom-call(f32[1152,128]{1,0:T(8,128)S(1)} %get-tuple-element.70.first, f32[1152,128]{1,0:T(8,128)S(1)} %get-tuple-element.71.second, bf16[1152,128]{1,0:T(8,128)(2,1)S(1)} %collective-permute-done.13.past, f32[1152,256]{1,0:T(8,128)S(1)} %get-tuple-element.72.home, ...), custom_call_target="tpu_custom_call" | custom-call | tf_op jit(solution)/shard_map/pallas_call | solution.py:227
  (31 shorter events, 5.1 us)
Async XLA Ops:
  0.6 22.3 %copy-start = (bf16[1152,256]{1,0:T(8,128)(2,1)S(1)}, bf16[1152,256]{1,0:T(8,128)(2,1)}, u32[]{:S(2)}) copy-start(bf16[1152,256]{1,0:T(8,128)(2,1)} %i0.9) | copy-start | bytes 1769476
  0.6 1.1 %copy-start.1 = (bf16[1152,256]{1,0:T(8,128)(2,1)S(1)}, bf16[1152,256]{1,0:T(8,128)(2,1)}, u32[]{:S(2)}) copy-start(bf16[1152,256]{1,0:T(8,128)(2,1)} %text.3) | copy-start | bytes 1769476
  1.8 21.1 %copy-start.2 = (bf16[1152,256]{1,0:T(8,128)(2,1)S(1)}, bf16[1152,256]{1,0:T(8,128)(2,1)}, u32[]{:S(2)}) copy-start(bf16[1152,256]{1,0:T(8,128)(2,1)} %text.3) | copy-start | bytes 1769476
  1.9 9.1 %collective-permute-start.3 = (bf16[512,128]{1,0:T(8,128)(2,1)S(1)}, bf16[512,128]{1,0:T(8,128)(2,1)S(1)}, u32[]{:S(2)}, u32[]{:S(2)}) collective-permute-start(bf16[512,128]{1,0:T(8,128)(2,1)S(1)} %get-tuple-element.44), channel_id=1, source_target_pairs={{0,8},{1,9},{2,10},{3,11},{4,12},{5,13},{6,14},{7,15},{8,16},{9,17... | collective-permute-start | bytes 393224 | tf_op jit(solution)/shard_map/ppermute | solution.py:28
  5.0 15.0 %collective-permute-start.1 = (bf16[1152,256]{1,0:T(8,128)(2,1)}, bf16[1152,256]{1,0:T(8,128)(2,1)S(1)}, u32[]{:S(2)}, u32[]{:S(2)}) collective-permute-start(bf16[1152,256]{1,0:T(8,128)(2,1)} %i0.9), channel_id=1, source_target_pairs={{0,1},{1,0},{2,3},{3,2},{4,5},{5,4},{6,7},{7,6},{8,9},{9,8},{10,11... | collective-permute-start | bytes 1769480 | tf_op jit(solution)/shard_map/ppermute | solution.py:28
  6.4 16.4 %collective-permute-start = (bf16[1152,256]{1,0:T(8,128)(2,1)}, bf16[1152,256]{1,0:T(8,128)(2,1)S(1)}, u32[]{:S(2)}, u32[]{:S(2)}) collective-permute-start(bf16[1152,256]{1,0:T(8,128)(2,1)} %i0.9), channel_id=1, source_target_pairs={{0,2},{1,3},{2,0},{3,1},{4,6},{5,7},{6,4},{7,5},{8,10},{9,11},{10,... | collective-permute-start | bytes 1769480 | tf_op jit(solution)/shard_map/ppermute | solution.py:28
  6.4 8.8 %collective-permute-start.4 = (bf16[640,128]{1,0:T(8,128)(2,1)S(1)}, bf16[640,128]{1,0:T(8,128)(2,1)S(1)}, u32[]{:S(2)}, u32[]{:S(2)}) collective-permute-start(bf16[640,128]{1,0:T(8,128)(2,1)S(1)} %get-tuple-element.45), channel_id=1, source_target_pairs={{0,8},{1,9},{2,10},{3,11},{4,12},{5,13},{6,14},{7,15},{8,16},{9,17... | collective-permute-start | bytes 491528 | tf_op jit(solution)/shard_map/ppermute | solution.py:28
  8.0 13.2 %collective-permute-start.5 = (bf16[1152,128]{1,0:T(8,128)(2,1)S(1)}, bf16[1152,128]{1,0:T(8,128)(2,1)S(1)}, u32[]{:S(2)}, u32[]{:S(2)}) collective-permute-start(bf16[1152,128]{1,0:T(8,128)(2,1)S(1)} %get-tuple-element.46), channel_id=1, source_target_pairs={{0,8},{1,9},{2,10},{3,11},{4,12},{5,13},{6,14},{7,15},{8,16},{9,17... | collective-permute-start | bytes 884744 | tf_op jit(solution)/shard_map/ppermute | solution.py:28
  11.0 14.6 %collective-permute-start.6 = (bf16[512,128]{1,0:T(8,128)(2,1)S(1)}, bf16[512,128]{1,0:T(8,128)(2,1)S(1)}, u32[]{:S(2)}, u32[]{:S(2)}) collective-permute-start(bf16[512,128]{1,0:T(8,128)(2,1)S(1)} %broadcast_select_fusion.2), channel_id=1, source_target_pairs={{0,4},{1,5},{2,6},{3,7},{4,0},{5,1},{6,2},{7,3},{8,12},{9,13},{10,... | collective-permute-start | bytes 393224 | tf_op jit(solution)/shard_map/ppermute | solution.py:28
  15.3 10.3 %collective-permute-start.7 = (bf16[640,128]{1,0:T(8,128)(2,1)S(1)}, bf16[640,128]{1,0:T(8,128)(2,1)S(1)}, u32[]{:S(2)}, u32[]{:S(2)}) collective-permute-start(bf16[640,128]{1,0:T(8,128)(2,1)S(1)} %broadcast_select_fusion.1), channel_id=1, source_target_pairs={{0,4},{1,5},{2,6},{3,7},{4,0},{5,1},{6,2},{7,3},{8,12},{9,13},{10,... | collective-permute-start | bytes 491528 | tf_op jit(solution)/shard_map/ppermute | solution.py:28
  20.0 2.9 %collective-permute-start.2 = (bf16[1152,256]{1,0:T(8,128)(2,1)S(1)}, bf16[1152,256]{1,0:T(8,128)(2,1)S(1)}, u32[]{:S(2)}, u32[]{:S(2)}) collective-permute-start(bf16[1152,256]{1,0:T(8,128)(2,1)S(1)} %collective-permute-done.1.i2), channel_id=1, source_target_pairs={{0,2},{1,3},{2,0},{3,1},{4,6},{5,7},{6,4},{7,5},{8,10},{9,11},{10,... | collective-permute-start | bytes 1769480 | tf_op jit(solution)/shard_map/ppermute | solution.py:28
  21.2 8.8 %collective-permute-start.8 = (bf16[1152,128]{1,0:T(8,128)(2,1)S(1)}, bf16[1152,128]{1,0:T(8,128)(2,1)S(1)}, u32[]{:S(2)}, u32[]{:S(2)}) collective-permute-start(bf16[1152,128]{1,0:T(8,128)(2,1)S(1)} %broadcast_select_fusion), channel_id=1, source_target_pairs={{0,4},{1,5},{2,6},{3,7},{4,0},{5,1},{6,2},{7,3},{8,12},{9,13},{10,... | collective-permute-start | bytes 884744 | tf_op jit(solution)/shard_map/ppermute | solution.py:28
  27.6 8.6 %collective-permute-start.9 = (bf16[1152,128]{1,0:T(8,128)(2,1)S(1)}, bf16[1152,128]{1,0:T(8,128)(2,1)S(1)}, u32[]{:S(2)}, u32[]{:S(2)}) collective-permute-start(bf16[1152,128]{1,0:T(8,128)(2,1)S(1)} %get-tuple-element.59), channel_id=1, source_target_pairs={{0,4},{1,5},{2,6},{3,7},{4,0},{5,1},{6,2},{7,3},{8,12},{9,13},{10,... | collective-permute-start | bytes 884744 | tf_op jit(solution)/shard_map/ppermute | solution.py:28
  31.7 5.2 %collective-permute-start.10 = (bf16[2,1168,256]{2,1,0:T(8,128)(2,1)S(1)}, bf16[2,1168,256]{2,1,0:T(8,128)(2,1)S(1)}, u32[]{:S(2)}, u32[]{:S(2)}) collective-permute-start(bf16[2,1168,256]{2,1,0:T(8,128)(2,1)S(1)} %get-tuple-element.64), channel_id=1, source_target_pairs={{0,2},{1,3},{2,0},{3,1},{4,6},{5,7},{6,4},{7,5},{8,10},{9,11},{10,... | collective-permute-start | bytes 3588104 | tf_op jit(solution)/shard_map/ppermute | solution.py:28
  33.1 9.5 %collective-permute-start.12 = (bf16[1152,128]{1,0:T(8,128)(2,1)S(1)}, bf16[1152,128]{1,0:T(8,128)(2,1)S(1)}, u32[]{:S(2)}, u32[]{:S(2)}) collective-permute-start(bf16[1152,128]{1,0:T(8,128)(2,1)S(1)} %shard_map.72), channel_id=1, source_target_pairs={{0,4},{1,5},{2,6},{3,7},{4,0},{5,1},{6,2},{7,3},{8,12},{9,13},{10,... | collective-permute-start | bytes 884744 | tf_op jit(solution)/shard_map/ppermute | solution.py:28
  37.0 15.5 %collective-permute-start.14 = (bf16[1168,256]{1,0:T(8,128)(2,1)S(1)}, bf16[1168,256]{1,0:T(8,128)(2,1)S(1)}, u32[]{:S(2)}, u32[]{:S(2)}) collective-permute-start(bf16[1168,256]{1,0:T(8,128)(2,1)S(1)} %shard_map.75), channel_id=1, source_target_pairs={{0,1},{1,0},{2,3},{3,2},{4,5},{5,4},{6,7},{7,6},{8,9},{9,8},{10,11... | collective-permute-start | bytes 1794056 | tf_op jit(solution)/shard_map/ppermute | solution.py:28
  38.2 8.7 %collective-permute-start.11 = (bf16[1152,128]{1,0:T(8,128)(2,1)S(1)}, bf16[1152,128]{1,0:T(8,128)(2,1)S(1)}, u32[]{:S(2)}, u32[]{:S(2)}) collective-permute-start(bf16[1152,128]{1,0:T(8,128)(2,1)S(1)} %shard_map.74), channel_id=1, source_target_pairs={{0,24},{1,25},{2,26},{3,27},{4,28},{5,29},{6,30},{7,31},{8,0},{9,1... | collective-permute-start | bytes 884744 | tf_op jit(solution)/shard_map/ppermute | solution.py:28
  43.2 9.3 %collective-permute-start.13 = (bf16[1152,128]{1,0:T(8,128)(2,1)S(1)}, bf16[1152,128]{1,0:T(8,128)(2,1)S(1)}, u32[]{:S(2)}, u32[]{:S(2)}) collective-permute-start(bf16[1152,128]{1,0:T(8,128)(2,1)S(1)} %shard_map.76), channel_id=1, source_target_pairs={{0,24},{1,25},{2,26},{3,27},{4,28},{5,29},{6,30},{7,31},{8,0},{9,1... | collective-permute-start | bytes 884744 | tf_op jit(solution)/shard_map/ppermute | solution.py:28

commit v7 on v6

--- a/solution.py
+++ b/solution.py
@@ -293,7 +293,7 @@
     other = moved(joined, swap(PAIR))
     older1, grad_m2, _ = lax.optimization_barrier((older1, grad_m2, joined))
     past1 = moved(older1, back)
-    older2 = call(older_kernel, older, (later, grad_m2, r2), flops=20 * unit)
+    older2 = (grad_m2 + jnp.where(high, r2.astype(f32), 0.0)).astype(bf16)
     past2 = moved(older2, back)
     _, late0 = lax.optimization_barrier((older2, g0))
     first, second = call(

time: 54.2 us -> 54.2 us (level)
  Pallas kernels: 15.7 us -> 15 us
    pallas_call x13 -> x12, Pallas kernels: 15.7 us -> 15 us  [call(): pl.pallas_call(kernel, out_shape=out_shape, in_specs=[pl.BlockSpec(memory...]
  transfers between devices with their start and end apart: 15 -> 15, of which waited for: 7 -> 8; matrix products, arithmetic and copies ran while one was open for 0% -> 1% of each run, Pallas kernels for 26% -> 25%
where the time goes in v7:
time: 54.2 us; the launch traced here: 54 us
  starting transfers between devices  20.9 us (39%)
  Pallas kernels  15 us (28%)
  waiting for transfers between devices  14.5 us (27%)
  between operations  2.09 us (4%)
  local copies, waits for them, and re-layouts  1.23 us (2%)
    ppermute x15, starting transfers between devices, moved(): return lax.ppermute(block, AXES, [(i, target(i, n)) for i in range(n)])  20.9 us
    pallas_call x12, Pallas kernels, call(): pl.pallas_call(kernel, out_shape=out_shape, in_specs=[pl.BlockSpec(memory...  15 us
    ppermute x15, waiting for transfers between devices, moved(): return lax.ppermute(block, AXES, [(i, target(i, n)) for i in range(n)])  14.5 us
    unnamed x6, local copies, waits for them, and re-layouts  1.13 us
  transfers between devices with their start and end apart: 15, of which 8 were waited for; matrix products, arithmetic and copies ran while one was open for 1% of the time, Pallas kernels for 25%

profile of v7, /device:TPU:0, one launch (start us, length us, event | category | flops | bytes accessed | tf_op | source)
XLA Modules:
  0.0 54.0 jit_solution(11698365569999697869)
XLA Ops:
  1.9 3.1 %collective-permute-start.3 = (bf16[512,128]{1,0:T(8,128)(2,1)S(1)}, bf16[512,128]{1,0:T(8,128)(2,1)S(1)}, u32[]{:S(2)}, u32[]{:S(2)}) collective-permute-start(bf16[512,128]{1,0:T(8,128)(2,1)S(1)} %get-tuple-element.44), channel_id=1, source_target_pairs={{0,8},{1,9},{2,10},{3,11},{4,12},{5,13},{6,14},{7,15},{8,16},{9,17... | collective-permute-start | bytes 393224 | tf_op jit(solution)/shard_map/ppermute | solution.py:28
  5.0 1.5 %collective-permute-start.1 = (bf16[1152,256]{1,0:T(8,128)(2,1)}, bf16[1152,256]{1,0:T(8,128)(2,1)S(1)}, u32[]{:S(2)}, u32[]{:S(2)}) collective-permute-start(bf16[1152,256]{1,0:T(8,128)(2,1)} %i0.9), channel_id=1, source_target_pairs={{0,1},{1,0},{2,3},{3,2},{4,5},{5,4},{6,7},{7,6},{8,9},{9,8},{10,11... | collective-permute-start | bytes 1769480 | tf_op jit(solution)/shard_map/ppermute | solution.py:28
  6.4 1.6 %collective-permute-start.4 = (bf16[640,128]{1,0:T(8,128)(2,1)S(1)}, bf16[640,128]{1,0:T(8,128)(2,1)S(1)}, u32[]{:S(2)}, u32[]{:S(2)}) collective-permute-start(bf16[640,128]{1,0:T(8,128)(2,1)S(1)} %get-tuple-element.45), channel_id=1, source_target_pairs={{0,8},{1,9},{2,10},{3,11},{4,12},{5,13},{6,14},{7,15},{8,16},{9,17... | collective-permute-start | bytes 491528 | tf_op jit(solution)/shard_map/ppermute | solution.py:28
  8.0 1.6 %collective-permute-start.5 = (bf16[1152,128]{1,0:T(8,128)(2,1)S(1)}, bf16[1152,128]{1,0:T(8,128)(2,1)S(1)}, u32[]{:S(2)}, u32[]{:S(2)}) collective-permute-start(bf16[1152,128]{1,0:T(8,128)(2,1)S(1)} %get-tuple-element.46), channel_id=1, source_target_pairs={{0,8},{1,9},{2,10},{3,11},{4,12},{5,13},{6,14},{7,15},{8,16},{9,17... | collective-permute-start | bytes 884744 | tf_op jit(solution)/shard_map/ppermute | solution.py:28
  11.0 1.6 %collective-permute-start.6 = (bf16[512,128]{1,0:T(8,128)(2,1)S(1)}, bf16[512,128]{1,0:T(8,128)(2,1)S(1)}, u32[]{:S(2)}, u32[]{:S(2)}) collective-permute-start(bf16[512,128]{1,0:T(8,128)(2,1)S(1)} %broadcast_select_fusion.2), channel_id=1, source_target_pairs={{0,4},{1,5},{2,6},{3,7},{4,0},{5,1},{6,2},{7,3},{8,12},{9,13},{10,... | collective-permute-start | bytes 393224 | tf_op jit(solution)/shard_map/ppermute | solution.py:28
  12.6 2.6 %collective-permute-done.4.m1b = bf16[640,128]{1,0:T(8,128)(2,1)S(1)} collective-permute-done((bf16[640,128]{1,0:T(8,128)(2,1)S(1)}, bf16[640,128]{1,0:T(8,128)(2,1)S(1)}, u32[]{:S(2)}, u32[]{:S(2)}) %collective-permute-start.4) | collective-permute-done | bytes 163872 | tf_op jit(solution)/shard_map/ppermute | solution.py:28
  15.3 1.6 %collective-permute-start.7 = (bf16[640,128]{1,0:T(8,128)(2,1)S(1)}, bf16[640,128]{1,0:T(8,128)(2,1)S(1)}, u32[]{:S(2)}, u32[]{:S(2)}) collective-permute-start(bf16[640,128]{1,0:T(8,128)(2,1)S(1)} %broadcast_select_fusion.1), channel_id=1, source_target_pairs={{0,4},{1,5},{2,6},{3,7},{4,0},{5,1},{6,2},{7,3},{8,12},{9,13},{10,... | collective-permute-start | bytes 491528 | tf_op jit(solution)/shard_map/ppermute | solution.py:28
  16.8 3.1 %collective-permute-done.1.i2 = bf16[1152,256]{1,0:T(8,128)(2,1)S(1)} collective-permute-done((bf16[1152,256]{1,0:T(8,128)(2,1)}, bf16[1152,256]{1,0:T(8,128)(2,1)S(1)}, u32[]{:S(2)}, u32[]{:S(2)}) %collective-permute-start.1) | collective-permute-done | bytes 589856 | tf_op jit(solution)/shard_map/ppermute | solution.py:28
  20.0 1.2 %collective-permute-done.5.m2 = bf16[1152,128]{1,0:T(8,128)(2,1)S(1)} collective-permute-done((bf16[1152,128]{1,0:T(8,128)(2,1)S(1)}, bf16[1152,128]{1,0:T(8,128)(2,1)S(1)}, u32[]{:S(2)}, u32[]{:S(2)}) %collective-permute-start.5) | collective-permute-done | bytes 294944 | tf_op jit(solution)/shard_map/ppermute | solution.py:28
  21.2 1.6 %collective-permute-start.8 = (bf16[1152,128]{1,0:T(8,128)(2,1)S(1)}, bf16[1152,128]{1,0:T(8,128)(2,1)S(1)}, u32[]{:S(2)}, u32[]{:S(2)}) collective-permute-start(bf16[1152,128]{1,0:T(8,128)(2,1)S(1)} %broadcast_select_fusion), channel_id=1, source_target_pairs={{0,4},{1,5},{2,6},{3,7},{4,0},{5,1},{6,2},{7,3},{8,12},{9,13},{10,... | collective-permute-start | bytes 884744 | tf_op jit(solution)/shard_map/ppermute | solution.py:28
  22.9 2.7 %shard_map.68 = (f32[1152,128]{1,0:T(8,128)S(1)}, f32[1152,128]{1,0:T(8,128)S(1)}, bf16[4,256,256]{2,1,0:T(8,128)(2,1)S(1)}, f32[8,256]{1,0:T(8,128)S(1)}, bf16[2,1152,256]{2,1,0:T(8,128)(2,1)S(1)}) custom-call(f32[2]{0:T(128)S(1)} %pad_maximum_fusion.tb, s32[5]{0:T(128)S(1)} %stack.26.later, bf16[1152,256]{1,0:T(8,128)(2,1)S(1)} %copy-done, ...), custom_call_target="tpu_custom_call" | custom-call | tf_op jit(solution)/shard_map/pallas_call | solution.py:227
  25.6 2.0 %shard_map.69 = (bf16[1152,128]{1,0:T(8,128)(2,1)S(1)}, bf16[4,128,256]{2,1,0:T(8,128)(2,1)S(1)}, f32[8,256]{1,0:T(8,128)S(1)}, bf16[1152,128]{1,0:T(8,128)(2,1)S(1)}) custom-call(f32[2]{0:T(128)S(1)} %pad_maximum_fusion.tb, bf16[1152,256]{1,0:T(8,128)(2,1)S(1)} %copy-done, bf16[1152,256]{1,0:T(8,128)(2,1)S(1)} %collective-permute-done.i1, ...), custom_call_target="tpu_custom_call" | custom-call | tf_op jit(solution)/shard_map/pallas_call | solution.py:227
  28.3 1.6 %shard_map.70.part = f32[3,1152,256]{2,1,0:T(8,128)S(1)} custom-call(s32[5]{0:T(128)S(1)} %stack.26.later, bf16[2,1152,256]{2,1,0:T(8,128)(2,1)S(1)} %get-tuple-element.47.kept, bf16[1152,128]{1,0:T(8,128)(2,1)S(1)} %get-tuple-element.51.k1.x1, bf16[4,256,256]{2,1,0:T(8,128)(2,1)S(1)} %get-tuple-element.68.g.grad, bf16[4,128,256]{2,1,0:T(8,128)(2,1)S(1)} %get-tuple-element.53.g1), custom_call_target="tpu_custom_call" | custom-call | tf_op jit(solution)/shard_map/pallas_call | solution.py:227
  30.0 1.7 %shard_map.71 = (bf16[4,128,256]{2,1,0:T(8,128)(2,1)S(1)}, f32[8,256]{1,0:T(8,128)S(1)}, bf16[2,1168,256]{2,1,0:T(8,128)(2,1)S(1)}) custom-call(f32[2]{0:T(128)S(1)} %pad_maximum_fusion.tb, bf16[1152,256]{1,0:T(8,128)(2,1)S(1)} %copy-done, bf16[1152,256]{1,0:T(8,128)(2,1)S(1)} %collective-permute-done.i1, bf16[1152,256]{1,0:T(8,128)(2,1)S(1)} %collective-permute-done.1.i2, ...), custom_call_target="tpu_custom_call" | custom-call | tf_op jit(solution)/shard_map/pallas_call | solution.py:227
  31.7 1.3 %shard_map.72 = bf16[1152,128]{1,0:T(8,128)(2,1)S(1)} custom-call(f32[2]{0:T(128)S(1)} %pad_maximum_fusion.tb, bf16[1152,256]{1,0:T(8,128)(2,1)S(1)} %copy-done, bf16[1152,256]{1,0:T(8,128)(2,1)S(1)} %collective-permute-done.i1, bf16[1152,256]{1,0:T(8,128)(2,1)S(1)} %collective-permute-done.1.i2, bf16[1152,256]{1,0:T(8,128)(2,1)S(1)} %collective-permute-done.2.i3, ...), custom_call_target="tpu_custom_call" | custom-call | tf_op jit(solution)/shard_map/pallas_call | solution.py:227
  33.1 1.8 %collective-permute-start.12 = (bf16[1152,128]{1,0:T(8,128)(2,1)S(1)}, bf16[1152,128]{1,0:T(8,128)(2,1)S(1)}, u32[]{:S(2)}, u32[]{:S(2)}) collective-permute-start(bf16[1152,128]{1,0:T(8,128)(2,1)S(1)} %shard_map.72), channel_id=1, source_target_pairs={{0,4},{1,5},{2,6},{3,7},{4,0},{5,1},{6,2},{7,3},{8,12},{9,13},{10,... | collective-permute-start | bytes 884744 | tf_op jit(solution)/shard_map/ppermute | solution.py:28
  37.0 1.1 %collective-permute-start.14 = (bf16[1168,256]{1,0:T(8,128)(2,1)S(1)}, bf16[1168,256]{1,0:T(8,128)(2,1)S(1)}, u32[]{:S(2)}, u32[]{:S(2)}) collective-permute-start(bf16[1168,256]{1,0:T(8,128)(2,1)S(1)} %shard_map.75), channel_id=1, source_target_pairs={{0,1},{1,0},{2,3},{3,2},{4,5},{5,4},{6,7},{7,6},{8,9},{9,8},{10,11... | collective-permute-start | bytes 1794056 | tf_op jit(solution)/shard_map/ppermute | solution.py:28
  38.2 2.4 %collective-permute-start.11 = (bf16[1152,128]{1,0:T(8,128)(2,1)S(1)}, bf16[1152,128]{1,0:T(8,128)(2,1)S(1)}, u32[]{:S(2)}, u32[]{:S(2)}) collective-permute-start(bf16[1152,128]{1,0:T(8,128)(2,1)S(1)} %shard_map.74), channel_id=1, source_target_pairs={{0,24},{1,25},{2,26},{3,27},{4,28},{5,29},{6,30},{7,31},{8,0},{9,1... | collective-permute-start | bytes 884744 | tf_op jit(solution)/shard_map/ppermute | solution.py:28
  40.6 2.0 %collective-permute-done.12.r2 = bf16[1152,128]{1,0:T(8,128)(2,1)S(1)} collective-permute-done((bf16[1152,128]{1,0:T(8,128)(2,1)S(1)}, bf16[1152,128]{1,0:T(8,128)(2,1)S(1)}, u32[]{:S(2)}, u32[]{:S(2)}) %collective-permute-start.12) | collective-permute-done | bytes 294944 | tf_op jit(solution)/shard_map/ppermute | solution.py:28
  42.7 2.3 %collective-permute-start.13 = (bf16[1152,128]{1,0:T(8,128)(2,1)S(1)}, bf16[1152,128]{1,0:T(8,128)(2,1)S(1)}, u32[]{:S(2)}, u32[]{:S(2)}) collective-permute-start(bf16[1152,128]{1,0:T(8,128)(2,1)S(1)} %add_convert_fusion), channel_id=1, source_target_pairs={{0,24},{1,25},{2,26},{3,27},{4,28},{5,29},{6,30},{7,31},{8,0},{9,1... | collective-permute-start | bytes 884744 | tf_op jit(solution)/shard_map/ppermute | solution.py:28
  45.0 1.4 %shard_map.76 = (f32[1152,128]{1,0:T(8,128)S(1)}, f32[1152,128]{1,0:T(8,128)S(1)}) custom-call(f32[2]{0:T(128)S(1)} %pad_maximum_fusion.tb, s32[5]{0:T(128)S(1)} %stack.26.later, bf16[1152,256]{1,0:T(8,128)(2,1)S(1)} %copy-done, bf16[1152,256]{1,0:T(8,128)(2,1)S(1)} %collective-permute-done.i1, bf16[1152,256]{1,0:T(8,128)(2,1)S(1)} %collective-permute-done.1.i2, ...), custom_call_target="tpu_custom_call" | custom-call | tf_op jit(solution)/shard_map/pallas_call | solution.py:227
  47.3 1.2 %shard_map.77 = (f32[1152,256]{1,0:T(8,128)S(1)}, f32[8,256]{1,0:T(8,128)S(1)}, f32[1152,128]{1,0:T(8,128)S(1)}) custom-call(f32[2]{0:T(128)S(1)} %pad_maximum_fusion.tb, s32[5]{0:T(128)S(1)} %stack.26.later, bf16[2,1152,256]{2,1,0:T(8,128)(2,1)S(1)} %get-tuple-element.47.kept, bf16[1152,128]{1,0:T(8,128)(2,1)S(1)} %get-tuple-element.51.k1.x1, ...), custom_call_target="tpu_custom_call" | custom-call | flops 754974720 | tf_op jit(solution)/shard_map/pallas_call | solution.py:227
  48.5 4.0 %collective-permute-done.13.past = bf16[1152,128]{1,0:T(8,128)(2,1)S(1)} collective-permute-done((bf16[1152,128]{1,0:T(8,128)(2,1)S(1)}, bf16[1152,128]{1,0:T(8,128)(2,1)S(1)}, u32[]{:S(2)}, u32[]{:S(2)}) %collective-permute-start.13) | collective-permute-done | bytes 294944 | tf_op jit(solution)/shard_map/ppermute | solution.py:28
  52.5 1.5 %shard_map.78 = (f32[1152,256]{1,0:T(8,128)}, f32[1,256]{1,0:T(1,128)}, f32[1152,256]{1,0:T(8,128)}) custom-call(f32[1152,128]{1,0:T(8,128)S(1)} %get-tuple-element.70.first, f32[1152,128]{1,0:T(8,128)S(1)} %get-tuple-element.71.second, bf16[1152,128]{1,0:T(8,128)(2,1)S(1)} %collective-permute-done.13.past, f32[1152,256]{1,0:T(8,128)S(1)} %get-tuple-element.72.home, ...), custom_call_target="tpu_custom_call" | custom-call | tf_op jit(solution)/shard_map/pallas_call | solution.py:227
  (31 shorter events, 5.5 us)
Async XLA Ops:
  0.6 22.3 %copy-start = (bf16[1152,256]{1,0:T(8,128)(2,1)S(1)}, bf16[1152,256]{1,0:T(8,128)(2,1)}, u32[]{:S(2)}) copy-start(bf16[1152,256]{1,0:T(8,128)(2,1)} %i0.9) | copy-start | bytes 1769476
  0.6 1.1 %copy-start.1 = (bf16[1152,256]{1,0:T(8,128)(2,1)S(1)}, bf16[1152,256]{1,0:T(8,128)(2,1)}, u32[]{:S(2)}) copy-start(bf16[1152,256]{1,0:T(8,128)(2,1)} %text.3) | copy-start | bytes 1769476
  1.8 21.1 %copy-start.2 = (bf16[1152,256]{1,0:T(8,128)(2,1)S(1)}, bf16[1152,256]{1,0:T(8,128)(2,1)}, u32[]{:S(2)}) copy-start(bf16[1152,256]{1,0:T(8,128)(2,1)} %text.3) | copy-start | bytes 1769476
  1.9 9.1 %collective-permute-start.3 = (bf16[512,128]{1,0:T(8,128)(2,1)S(1)}, bf16[512,128]{1,0:T(8,128)(2,1)S(1)}, u32[]{:S(2)}, u32[]{:S(2)}) collective-permute-start(bf16[512,128]{1,0:T(8,128)(2,1)S(1)} %get-tuple-element.44), channel_id=1, source_target_pairs={{0,8},{1,9},{2,10},{3,11},{4,12},{5,13},{6,14},{7,15},{8,16},{9,17... | collective-permute-start | bytes 393224 | tf_op jit(solution)/shard_map/ppermute | solution.py:28
  5.0 15.0 %collective-permute-start.1 = (bf16[1152,256]{1,0:T(8,128)(2,1)}, bf16[1152,256]{1,0:T(8,128)(2,1)S(1)}, u32[]{:S(2)}, u32[]{:S(2)}) collective-permute-start(bf16[1152,256]{1,0:T(8,128)(2,1)} %i0.9), channel_id=1, source_target_pairs={{0,1},{1,0},{2,3},{3,2},{4,5},{5,4},{6,7},{7,6},{8,9},{9,8},{10,11... | collective-permute-start | bytes 1769480 | tf_op jit(solution)/shard_map/ppermute | solution.py:28
  6.4 16.4 %collective-permute-start = (bf16[1152,256]{1,0:T(8,128)(2,1)}, bf16[1152,256]{1,0:T(8,128)(2,1)S(1)}, u32[]{:S(2)}, u32[]{:S(2)}) collective-permute-start(bf16[1152,256]{1,0:T(8,128)(2,1)} %i0.9), channel_id=1, source_target_pairs={{0,2},{1,3},{2,0},{3,1},{4,6},{5,7},{6,4},{7,5},{8,10},{9,11},{10,... | collective-permute-start | bytes 1769480 | tf_op jit(solution)/shard_map/ppermute | solution.py:28
  6.4 8.8 %collective-permute-start.4 = (bf16[640,128]{1,0:T(8,128)(2,1)S(1)}, bf16[640,128]{1,0:T(8,128)(2,1)S(1)}, u32[]{:S(2)}, u32[]{:S(2)}) collective-permute-start(bf16[640,128]{1,0:T(8,128)(2,1)S(1)} %get-tuple-element.45), channel_id=1, source_target_pairs={{0,8},{1,9},{2,10},{3,11},{4,12},{5,13},{6,14},{7,15},{8,16},{9,17... | collective-permute-start | bytes 491528 | tf_op jit(solution)/shard_map/ppermute | solution.py:28
  8.0 13.2 %collective-permute-start.5 = (bf16[1152,128]{1,0:T(8,128)(2,1)S(1)}, bf16[1152,128]{1,0:T(8,128)(2,1)S(1)}, u32[]{:S(2)}, u32[]{:S(2)}) collective-permute-start(bf16[1152,128]{1,0:T(8,128)(2,1)S(1)} %get-tuple-element.46), channel_id=1, source_target_pairs={{0,8},{1,9},{2,10},{3,11},{4,12},{5,13},{6,14},{7,15},{8,16},{9,17... | collective-permute-start | bytes 884744 | tf_op jit(solution)/shard_map/ppermute | solution.py:28
  11.0 14.6 %collective-permute-start.6 = (bf16[512,128]{1,0:T(8,128)(2,1)S(1)}, bf16[512,128]{1,0:T(8,128)(2,1)S(1)}, u32[]{:S(2)}, u32[]{:S(2)}) collective-permute-start(bf16[512,128]{1,0:T(8,128)(2,1)S(1)} %broadcast_select_fusion.2), channel_id=1, source_target_pairs={{0,4},{1,5},{2,6},{3,7},{4,0},{5,1},{6,2},{7,3},{8,12},{9,13},{10,... | collective-permute-start | bytes 393224 | tf_op jit(solution)/shard_map/ppermute | solution.py:28
  15.3 10.3 %collective-permute-start.7 = (bf16[640,128]{1,0:T(8,128)(2,1)S(1)}, bf16[640,128]{1,0:T(8,128)(2,1)S(1)}, u32[]{:S(2)}, u32[]{:S(2)}) collective-permute-start(bf16[640,128]{1,0:T(8,128)(2,1)S(1)} %broadcast_select_fusion.1), channel_id=1, source_target_pairs={{0,4},{1,5},{2,6},{3,7},{4,0},{5,1},{6,2},{7,3},{8,12},{9,13},{10,... | collective-permute-start | bytes 491528 | tf_op jit(solution)/shard_map/ppermute | solution.py:28
  20.0 2.9 %collective-permute-start.2 = (bf16[1152,256]{1,0:T(8,128)(2,1)S(1)}, bf16[1152,256]{1,0:T(8,128)(2,1)S(1)}, u32[]{:S(2)}, u32[]{:S(2)}) collective-permute-start(bf16[1152,256]{1,0:T(8,128)(2,1)S(1)} %collective-permute-done.1.i2), channel_id=1, source_target_pairs={{0,2},{1,3},{2,0},{3,1},{4,6},{5,7},{6,4},{7,5},{8,10},{9,11},{10,... | collective-permute-start | bytes 1769480 | tf_op jit(solution)/shard_map/ppermute | solution.py:28
  21.2 8.8 %collective-permute-start.8 = (bf16[1152,128]{1,0:T(8,128)(2,1)S(1)}, bf16[1152,128]{1,0:T(8,128)(2,1)S(1)}, u32[]{:S(2)}, u32[]{:S(2)}) collective-permute-start(bf16[1152,128]{1,0:T(8,128)(2,1)S(1)} %broadcast_select_fusion), channel_id=1, source_target_pairs={{0,4},{1,5},{2,6},{3,7},{4,0},{5,1},{6,2},{7,3},{8,12},{9,13},{10,... | collective-permute-start | bytes 884744 | tf_op jit(solution)/shard_map/ppermute | solution.py:28
  27.6 8.6 %collective-permute-start.9 = (bf16[1152,128]{1,0:T(8,128)(2,1)S(1)}, bf16[1152,128]{1,0:T(8,128)(2,1)S(1)}, u32[]{:S(2)}, u32[]{:S(2)}) collective-permute-start(bf16[1152,128]{1,0:T(8,128)(2,1)S(1)} %get-tuple-element.59), channel_id=1, source_target_pairs={{0,4},{1,5},{2,6},{3,7},{4,0},{5,1},{6,2},{7,3},{8,12},{9,13},{10,... | collective-permute-start | bytes 884744 | tf_op jit(solution)/shard_map/ppermute | solution.py:28
  31.7 5.2 %collective-permute-start.10 = (bf16[2,1168,256]{2,1,0:T(8,128)(2,1)S(1)}, bf16[2,1168,256]{2,1,0:T(8,128)(2,1)S(1)}, u32[]{:S(2)}, u32[]{:S(2)}) collective-permute-start(bf16[2,1168,256]{2,1,0:T(8,128)(2,1)S(1)} %get-tuple-element.64), channel_id=1, source_target_pairs={{0,2},{1,3},{2,0},{3,1},{4,6},{5,7},{6,4},{7,5},{8,10},{9,11},{10,... | collective-permute-start | bytes 3588104 | tf_op jit(solution)/shard_map/ppermute | solution.py:28
  33.1 9.5 %collective-permute-start.12 = (bf16[1152,128]{1,0:T(8,128)(2,1)S(1)}, bf16[1152,128]{1,0:T(8,128)(2,1)S(1)}, u32[]{:S(2)}, u32[]{:S(2)}) collective-permute-start(bf16[1152,128]{1,0:T(8,128)(2,1)S(1)} %shard_map.72), channel_id=1, source_target_pairs={{0,4},{1,5},{2,6},{3,7},{4,0},{5,1},{6,2},{7,3},{8,12},{9,13},{10,... | collective-permute-start | bytes 884744 | tf_op jit(solution)/shard_map/ppermute | solution.py:28
  37.0 15.5 %collective-permute-start.14 = (bf16[1168,256]{1,0:T(8,128)(2,1)S(1)}, bf16[1168,256]{1,0:T(8,128)(2,1)S(1)}, u32[]{:S(2)}, u32[]{:S(2)}) collective-permute-start(bf16[1168,256]{1,0:T(8,128)(2,1)S(1)} %shard_map.75), channel_id=1, source_target_pairs={{0,1},{1,0},{2,3},{3,2},{4,5},{5,4},{6,7},{7,6},{8,9},{9,8},{10,11... | collective-permute-start | bytes 1794056 | tf_op jit(solution)/shard_map/ppermute | solution.py:28
  38.2 9.1 %collective-permute-start.11 = (bf16[1152,128]{1,0:T(8,128)(2,1)S(1)}, bf16[1152,128]{1,0:T(8,128)(2,1)S(1)}, u32[]{:S(2)}, u32[]{:S(2)}) collective-permute-start(bf16[1152,128]{1,0:T(8,128)(2,1)S(1)} %shard_map.74), channel_id=1, source_target_pairs={{0,24},{1,25},{2,26},{3,27},{4,28},{5,29},{6,30},{7,31},{8,0},{9,1... | collective-permute-start | bytes 884744 | tf_op jit(solution)/shard_map/ppermute | solution.py:28
  42.7 9.8 %collective-permute-start.13 = (bf16[1152,128]{1,0:T(8,128)(2,1)S(1)}, bf16[1152,128]{1,0:T(8,128)(2,1)S(1)}, u32[]{:S(2)}, u32[]{:S(2)}) collective-permute-start(bf16[1152,128]{1,0:T(8,128)(2,1)S(1)} %add_convert_fusion), channel_id=1, source_target_pairs={{0,24},{1,25},{2,26},{3,27},{4,28},{5,29},{6,30},{7,31},{8,0},{9,1... | collective-permute-start | bytes 884744 | tf_op jit(solution)/shard_map/ppermute | solution.py:28
